TPU v7x, 32 devices: a whole 2x2x4 slice. The times are simulated.
32 devices in a mesh: groups: 2 (over y), tile: 4 (over z), inst: 4 (over x, core).
Axes of the slice: x: 2, y: 2, z: 4, core: 2. Of those that a mesh axis runs over, the one named last changes fastest.
Arguments:
- features: bfloat16 [512, 256, 256], P(('groups', 'tile')), parts along dimension 0, may hold values from -6 to 6
- kernels: bfloat16 [2048, 256], P(('groups', 'tile', 'inst')), parts along dimension 0, may hold values from -0.375 to 0.375
- home: int32 [2048, 1], P(('groups', 'tile', 'inst')), parts along dimension 0, may hold values from 0 to 3; in each aligned block of 64 rows (0 to 63, 64 to 127, ...) at most 40 rows name the same one
- boxes: int32 [2048, 4], P(('groups', 'tile', 'inst')), parts along dimension 0, may hold values from 0 to 7, as said below
- gain: float32 [256], replicated, may hold values from 0.1 to 1.9
- w_in: bfloat16 [256, 2048], P(None, 'inst'), may hold values from -0.375 to 0.375
- w_out: bfloat16 [2048, 256], P('inst'), may hold values from -0.125 to 0.125
Outputs:
- updated: bfloat16 [2048, 256], P(('groups', 'tile', 'inst')), parts along dimension 0
There are 2 independent parts, one for each index of `groups`. A program takes and returns all parts, laid end to end along the dimension named above; an argument that names none is the same for every part. Nothing has to cross between parts.
Inputs may be any that keep to these rules, and one draw needn't show every extreme that they name: `home`: each device's 64 rows name any one strip at most 40 times, and in some of these aligned blocks one strip is named exactly 40 times. `boxes`: each row holds first row <= last row of tiles, both below 2, then first column <= last column, both below 8.
All inputs are finite; a program needn't handle non-finite values.
Results may differ from a plain program's by a relative error of at most 0.0058.
Values may be sent and summed in bfloat16 or wider, within the bound.
No kernel may reach another device: no remote copies, remote signals or barrier semaphores. Data moves between devices by JAX's collectives and lax.ppermute only.
A program may use at most 64 MiB of HBM per device.

v0:
```python
import jax
import jax.numpy as jnp
from jax import lax
from jax.sharding import PartitionSpec as P

TS = 32
SR = 2
WC = 8


def strip_ranks(home_col, strips):
    member = (home_col[:, None] == jnp.arange(strips, dtype=jnp.int32)[None, :]).astype(jnp.int32)
    before = jnp.cumsum(member, axis=0) - member
    return jnp.sum(before * member, axis=1)


def tile_pool(kernel_rows, box_rows, strip_feats):
    feat_width = kernel_rows.shape[1]
    pooled = jnp.zeros((kernel_rows.shape[0], feat_width), jnp.float32)
    covered = jnp.zeros((kernel_rows.shape[0],), jnp.float32)
    for tile_row in range(SR):
        for tile_col in range(WC):
            block = strip_feats[
                tile_row * TS : (tile_row + 1) * TS, tile_col * TS : (tile_col + 1) * TS
            ]
            block = block.reshape(TS * TS, feat_width)
            logits = lax.dot_general(
                kernel_rows, block, (((1,), (1,)), ((), ())), preferred_element_type=jnp.float32
            )
            inside = (
                (box_rows[:, 0] <= tile_row)
                & (tile_row <= box_rows[:, 1])
                & (box_rows[:, 2] <= tile_col)
                & (tile_col <= box_rows[:, 3])
            )
            masked = jnp.where(
                inside[:, None], jax.nn.sigmoid(logits), jnp.zeros_like(logits)
            ).astype(jnp.bfloat16)
            pooled = pooled + jnp.dot(masked, block, preferred_element_type=jnp.float32)
            covered = covered + jnp.sum(masked.astype(jnp.float32), axis=1)
    return (pooled, covered)


def local(features, kernels, home, boxes, gain, w_in, w_out):
    strips = lax.axis_size("tile")
    kernel_count = kernels.shape[0]
    feat_width = kernels.shape[1]
    capacity = min(kernel_count, max(2, 5 * kernel_count // (2 * strips)))
    home_col = home[:, 0]
    slots = home_col * capacity + strip_ranks(home_col, strips)
    all_rows, all_boxes, all_home = (
        lax.all_gather(kernels, "tile", axis=0, tiled=True),
        lax.all_gather(boxes.astype(jnp.bfloat16), "tile", axis=0, tiled=True),
        lax.all_gather(home.astype(jnp.bfloat16), "tile", axis=0, tiled=True),
    )
    src_home = all_home[:, 0].astype(jnp.int32).reshape(strips, kernel_count)
    src_ranks = jax.vmap(lambda column: strip_ranks(column, strips))(src_home)
    mine = lax.axis_index("tile")
    select = (
        (src_home == mine)[:, None, :]
        & (src_ranks[:, None, :] == jnp.arange(capacity, dtype=jnp.int32)[None, :, None])
    ).astype(jnp.bfloat16)
    got_rows = jnp.einsum(
        "bsj,bjc->bsc",
        select,
        all_rows.reshape(strips, kernel_count, feat_width),
        preferred_element_type=jnp.float32,
    )
    got_rows = got_rows.astype(jnp.bfloat16).reshape(strips * capacity, feat_width)
    box_sum = jnp.einsum(
        "bsj,bjc->bsc",
        select,
        all_boxes.reshape(strips, kernel_count, 4),
        preferred_element_type=jnp.float32,
    )
    filled = jnp.sum(select.astype(jnp.float32), axis=2)[:, :, None]
    blank = jnp.array([1.0, 0.0, 1.0, 0.0], jnp.float32)
    got_boxes = (
        (box_sum + (1.0 - filled) * blank[None, None, :])
        .astype(jnp.int32)
        .reshape(strips * capacity, 4)
    )
    pooled, covered = tile_pool(got_rows, got_boxes, features)
    back_pooled, back_covered = (
        lax.all_to_all(
            pooled.reshape(strips, capacity, feat_width),
            "tile",
            split_axis=0,
            concat_axis=0,
            tiled=True,
        ),
        lax.all_to_all(
            covered.reshape(strips, capacity), "tile", split_axis=0, concat_axis=0, tiled=True
        ),
    )
    own_pooled = back_pooled.reshape(strips * capacity, feat_width)[slots]
    own_covered = back_covered.reshape(strips * capacity)[slots]
    merged = kernels.astype(jnp.float32) + own_pooled / own_covered[:, None]
    centred = merged - jnp.mean(merged, axis=1, keepdims=True)
    spread = jnp.mean(centred * centred, axis=1, keepdims=True)
    normed = (centred * lax.rsqrt(spread + 1e-05) * gain[None, :]).astype(jnp.bfloat16)
    all_normed = lax.all_gather(normed, "inst", axis=0, tiled=True)
    hidden = jax.nn.relu(jnp.dot(all_normed, w_in, preferred_element_type=jnp.float32)).astype(
        jnp.bfloat16
    )
    delta = lax.psum_scatter(
        jnp.dot(hidden, w_out, preferred_element_type=jnp.float32),
        "inst",
        scatter_dimension=0,
        tiled=True,
    )
    return (merged + delta).astype(jnp.bfloat16)


def solution(mesh):
    return jax.shard_map(
        local,
        mesh=mesh,
        in_specs=(
            P(("groups", "tile"), None, None),
            P(("groups", "tile", "inst"), None),
            P(("groups", "tile", "inst"), None),
            P(("groups", "tile", "inst"), None),
            P(),
            P(None, "inst"),
            P("inst", None),
        ),
        out_specs=P(("groups", "tile", "inst"), None),
        check_vma=False,
    )
```

profile of v0, /device:TPU:0, one launch (start us, length us, event | category | flops | bytes accessed | tf_op | source)
XLA Modules:
  0.0 140.6 jit_solution(1332032056514100739)
XLA Ops:
  6.5 15.4 %all_gather.14 = bf16[256,256]{1,0:T(8,128)(2,1)S(1)} all-gather(bf16[64,256]{1,0:T(8,128)(2,1)} %param.9), channel_id=1, replica_groups=mesh['groups'=2,'tile'=4,'inst'=4] {'tile'}, dimensions={0}, use_global_device_ids=true | all-gather | bytes 163840 | tf_op jit(solution)/shard_map/all_gather | solution.py:52
  21.9 0.7 fusion.93
  22.8 0.8 select_reduce_fusion.1
  23.6 0.7 fusion.94
  24.3 1.2 dynamic-slice
  26.5 12.0 %all-reduce = bf16[256]{0:T(256)(128)(2,1)S(1)} all-reduce(bf16[256]{0:T(256)(128)(2,1)S(1)} %dynamic-update-slice), channel_id=1, replica_groups=mesh['groups'=2,'tile'=4,'inst'=4] {'tile'}, use_global_device_ids=true, to_apply=%add | all-reduce | flops 256 | bytes 1024
  39.4 5.8 %fusion.97 = (bf16[32,32,256]{2,1,0:T(8,128)(2,1)S(1)}, bf16[32,32,256]{2,1,0:T(8,128)(2,1)S(1)}, bf16[32,32,256]{2,1,0:T(8,128)(2,1)S(1)}, bf16[32,32,256]{2,1,...) fusion(bf16[64,256,256]{2,1,0:T(8,128)(2,1)} %param.8), kind=kLoop, calls=%fused_computation.185 | loop fusion | bytes 16777216 | tf_op jit(solution)/shard_map/slice | solution.py:23
  45.2 7.6 %all-gather = bf16[4,64,4]{1,2,0:T(4,128)(2,1)S(1)} all-gather(bf16[1,64,4]{1,2,0:T(4,128)(2,1)S(1)} %convert_bitcast_fusion), channel_id=1, replica_groups=mesh['groups'=2,'tile'=4,'inst'=4] {'tile'}, dimensions={0}, use_global_device_ids=true | all-gather | bytes 2560 | tf_op jit(solution)/shard_map/all_gather | solution.py:53
  53.1 2.3 %convert_reduce_fusion.15 = (f32[160]{0:T(256)S(1)}, bf16[160,1024]{1,0:T(8,128)(2,1)}) fusion(bf16[160,256]{1,0:T(8,128)(2,1)S(1)} %bitcast.137, bf16[1024,256]{1,0:T(8,128)(2,1)} %bitcast.134, pred[160]{0:T(512)(128)(4,1)S(1)} %get-tuple-element.39), kind=kOutput, calls=%fused_computation.134 | convolution fusion | flops 85032800 | bytes 934688 | tf_op jit(solution)/shard_map/dot_general | solution.py:27
  55.4 2.2 %convert_reduce_fusion.14 = (f32[160]{0:T(256)S(1)}, bf16[160,1024]{1,0:T(8,128)(2,1)}) fusion(bf16[160,256]{1,0:T(8,128)(2,1)S(1)} %bitcast.138, bf16[1024,256]{1,0:T(8,128)(2,1)} %bitcast.132, pred[160]{0:T(512)(128)(4,1)S(1)} %get-tuple-element.40), kind=kOutput, calls=%fused_computation.133 | convolution fusion | flops 85032800 | bytes 934688 | tf_op jit(solution)/shard_map/dot_general | solution.py:27
  57.6 2.2 %convert_reduce_fusion.13 = (f32[160]{0:T(256)S(1)}, bf16[160,1024]{1,0:T(8,128)(2,1)}) fusion(bf16[160,256]{1,0:T(8,128)(2,1)S(1)} %bitcast.139, bf16[1024,256]{1,0:T(8,128)(2,1)} %bitcast.130, pred[160]{0:T(512)(128)(4,1)S(1)} %get-tuple-element.41), kind=kOutput, calls=%fused_computation.132 | convolution fusion | flops 85032800 | bytes 934688 | tf_op jit(solution)/shard_map/dot_general | solution.py:27
  59.8 1.1 convert_reduce_fusion.12
  61.0 1.2 convert_reduce_fusion.11
  62.2 1.2 convert_reduce_fusion.10
  63.3 1.2 convert_reduce_fusion.9
  64.5 1.1 convert_reduce_fusion.8
  65.6 1.1 convert_reduce_fusion.7
  66.8 1.1 convert_reduce_fusion.6
  67.9 1.1 convert_reduce_fusion.5
  69.0 1.1 convert_reduce_fusion.4
  70.1 1.1 convert_reduce_fusion.3
  71.3 1.1 convert_reduce_fusion.2
  72.4 1.1 convert_reduce_fusion.1
  73.5 1.1 convert_reduce_fusion
  74.7 0.7 reshape.346
  75.3 3.3 %all-to-all-start.1 = ((f32[4,1,40]{2,1,0:T(1,128)}), f32[4,1,40]{2,1,0:T(1,128)S(1)}, u32[]{:S(2)}, u32[]{:S(2)}) async-start(f32[4,1,40]{2,1,0:T(1,128)} %reshape.346), calls=%async_computation.1 | async-start | bytes 4096 | tf_op jit(solution)/shard_map/all_to_all | solution.py:92
  78.7 1.5 %fusion.98 = f32[160,256]{1,0:T(8,128)S(1)} fusion(bf16[160,1024]{1,0:T(8,128)(2,1)} %get-tuple-element.80, bf16[1024,256]{1,0:T(8,128)(2,1)} %bitcast.135), kind=kOutput, calls=%fused_computation.186 | convolution fusion | flops 83886080 | bytes 1015808 | tf_op jit(solution)/shard_map/dot_general | solution.py:39
  80.2 1.4 %convolution_add_fusion.14 = f32[160,256]{1,0:T(8,128)S(1)} fusion(f32[160,256]{1,0:T(8,128)S(1)} %fusion.98, bf16[160,1024]{1,0:T(8,128)(2,1)} %get-tuple-element.82, bf16[1024,256]{1,0:T(8,128)(2,1)} %bitcast.133), kind=kOutput, calls=%fused_computation.115 | convolution fusion | flops 83927040 | bytes 1179648 | tf_op jit(solution)/shard_map/dot_general | solution.py:39
  81.7 1.4 convolution_add_fusion.13
  83.1 1.4 convolution_add_fusion.12
  84.5 1.4 convolution_add_fusion.11
  85.9 1.4 convolution_add_fusion.10
  87.4 1.4 convolution_add_fusion.9
  88.8 1.2 convolution_add_fusion.8
  90.6 0.3 convolution_add_fusion.5
  90.9 0.3 convolution_add_fusion.4
  91.7 0.3 convolution_add_fusion.1
  91.9 0.9 convolution_add_fusion
  92.9 5.1 %all-to-all-start = ((f32[4,40,256]{2,1,0:T(8,128)}), f32[4,40,256]{2,1,0:T(8,128)S(1)}, u32[]{:S(2)}, u32[]{:S(2)}) async-start(f32[4,40,256]{2,1,0:T(8,128)} %bitcast.21), calls=%async_computation | async-start | bytes 327680 | tf_op jit(solution)/shard_map/all_to_all | solution.py:85
  98.0 0.5 broadcast.239
  98.5 0.7 reduce.35
  99.2 0.8 gather_fusion.1
  100.0 3.9 %all-to-all-done = f32[4,40,256]{2,1,0:T(8,128)S(1)} async-done(((f32[4,40,256]{2,1,0:T(8,128)}), f32[4,40,256]{2,1,0:T(8,128)S(1)}, u32[]{:S(2)}, u32[]{:S(2)}) %all-to-all-start) | async-done | bytes 163872 | tf_op jit(solution)/shard_map/all_to_all | solution.py:85
  103.9 0.7 gather_fusion
  105.1 5.4 %all_gather.15 = bf16[256,256]{1,0:T(8,128)(2,1)S(1)} all-gather(bf16[64,256]{1,0:T(8,128)(2,1)S(1)} %multiply_convert_fusion), channel_id=1, replica_groups=mesh['groups'=2,'tile'=4,'inst'=4] {'inst'}, dimensions={0}, use_global_device_ids=true | all-gather | bytes 163840 | tf_op jit(solution)/shard_map/all_gather | solution.py:102
  110.5 2.0 %fusion.81 = f32[256,256]{1,0:T(8,128)} fusion(bf16[512,256]{1,0:T(8,128)(2,1)S(1)} %copy-done, bf16[256,256]{1,0:T(8,128)(2,1)S(1)} %all_gather.15, bf16[256,512]{1,0:T(8,128)(2,1)} %param.13), kind=kOutput, calls=%fused_computation.100 | convolution fusion | flops 134479872 | bytes 917504 | tf_op jit(solution)/shard_map/dot_general | solution.py:107
  112.6 19.6 %reduce-scatter.2.cloned.1.call-done = f32[64,256]{1,0:T(8,128)} async-done(((f32[256,256]{1,0:T(8,128)}), f32[64,256]{1,0:T(8,128)}) %reduce-scatter.2.cloned.1.call-update) | async-done | bytes 65552 | tf_op jit(solution)/shard_map/reduce_scatter | solution.py:106
  132.2 1.5 %add_convert_fusion = bf16[64,256]{1,0:T(8,128)(2,1)} fusion(f32[64,256]{1,0:T(8,128)S(1)} %get-tuple-element.22, f32[64,256]{1,0:T(8,128)} %reduce-scatter.2.cloned.1.call-done), kind=kLoop, calls=%fused_computation.143 | loop fusion | flops 32768 | bytes 163840 | tf_op jit(solution)/shard_map/convert_element_type | solution.py:112
  (79 shorter events, 3.2 us)
Async XLA Ops:
  6.5 104.0 %copy-start = (bf16[512,256]{1,0:T(8,128)(2,1)S(1)}, bf16[512,256]{1,0:T(8,128)(2,1)}, u32[]{:S(2)}) copy-start(bf16[512,256]{1,0:T(8,128)(2,1)} %param.14) | copy-start | bytes 786436
  39.4 5.8 %copy-start.20 = (s32[64,4]{0,1:T(4,128)S(1)}, s32[64,4]{0,1:T(4,128)}, u32[]{:S(2)}) copy-start(s32[64,4]{0,1:T(4,128)} %param.11) | copy-start | bytes 3076
  39.4 13.4 %copy-start.22 = (f32[4]{0:T(128)S(1)}, f32[4]{0:T(128)}, u32[]{:S(2)}) copy-start(f32[4]{0:T(128)} %constant.51.clone) | copy-start | bytes 52
  53.0 6.8 %copy-start.10 = (bf16[32,32,256]{2,1,0:T(8,128)(2,1)S(1)}, bf16[32,32,256]{2,1,0:T(8,128)(2,1)}, u32[]{:S(2)}) copy-start(bf16[32,32,256]{2,1,0:T(8,128)(2,1)} %get-tuple-element.34) | copy-start | bytes 1572868
  53.0 8.0 %copy-start.9 = (bf16[32,32,256]{2,1,0:T(8,128)(2,1)S(1)}, bf16[32,32,256]{2,1,0:T(8,128)(2,1)}, u32[]{:S(2)}) copy-start(bf16[32,32,256]{2,1,0:T(8,128)(2,1)} %get-tuple-element.33) | copy-start | bytes 1572868
  53.1 9.0 %copy-start.8 = (bf16[32,32,256]{2,1,0:T(8,128)(2,1)S(1)}, bf16[32,32,256]{2,1,0:T(8,128)(2,1)}, u32[]{:S(2)}) copy-start(bf16[32,32,256]{2,1,0:T(8,128)(2,1)} %get-tuple-element.32) | copy-start | bytes 1572868
  55.4 7.9 %copy-start.7 = (bf16[32,32,256]{2,1,0:T(8,128)(2,1)S(1)}, bf16[32,32,256]{2,1,0:T(8,128)(2,1)}, u32[]{:S(2)}) copy-start(bf16[32,32,256]{2,1,0:T(8,128)(2,1)} %get-tuple-element.31) | copy-start | bytes 1572868
  57.6 6.9 %copy-start.5 = (bf16[32,32,256]{2,1,0:T(8,128)(2,1)S(1)}, bf16[32,32,256]{2,1,0:T(8,128)(2,1)}, u32[]{:S(2)}) copy-start(bf16[32,32,256]{2,1,0:T(8,128)(2,1)} %get-tuple-element.30) | copy-start | bytes 1572868
  59.8 5.8 %copy-start.3 = (bf16[32,32,256]{2,1,0:T(8,128)(2,1)S(1)}, bf16[32,32,256]{2,1,0:T(8,128)(2,1)}, u32[]{:S(2)}) copy-start(bf16[32,32,256]{2,1,0:T(8,128)(2,1)} %get-tuple-element.29) | copy-start | bytes 1572868
  61.0 5.8 %copy-start.1 = (bf16[32,32,256]{2,1,0:T(8,128)(2,1)S(1)}, bf16[32,32,256]{2,1,0:T(8,128)(2,1)}, u32[]{:S(2)}) copy-start(bf16[32,32,256]{2,1,0:T(8,128)(2,1)} %get-tuple-element.28) | copy-start | bytes 1572868
  75.3 17.5 %all-to-all-start.1 = ((f32[4,1,40]{2,1,0:T(1,128)}), f32[4,1,40]{2,1,0:T(1,128)S(1)}, u32[]{:S(2)}, u32[]{:S(2)}) async-start(f32[4,1,40]{2,1,0:T(1,128)} %reshape.346), calls=%async_computation.1 | async-start | bytes 4096 | tf_op jit(solution)/shard_map/all_to_all | solution.py:92
  78.6 10.2 %copy-start.6 = (bf16[32,32,256]{2,1,0:T(8,128)(2,1)S(1)}, bf16[32,32,256]{2,1,0:T(8,128)(2,1)}, u32[]{:S(2)}) copy-start(bf16[32,32,256]{2,1,0:T(8,128)(2,1)} %get-tuple-element.30) | copy-start | bytes 1572868
  78.6 11.4 %copy-start.4 = (bf16[32,32,256]{2,1,0:T(8,128)(2,1)S(1)}, bf16[32,32,256]{2,1,0:T(8,128)(2,1)}, u32[]{:S(2)}) copy-start(bf16[32,32,256]{2,1,0:T(8,128)(2,1)} %get-tuple-element.29) | copy-start | bytes 1572868
  78.6 11.4 %copy-start.18 = (bf16[160,1024]{1,0:T(8,128)(2,1)S(1)}, bf16[160,1024]{1,0:T(8,128)(2,1)}, u32[]{:S(2)}) copy-start(bf16[160,1024]{1,0:T(8,128)(2,1)} %get-tuple-element.66) | copy-start | bytes 983044
  78.6 11.7 %copy-start.2 = (bf16[32,32,256]{2,1,0:T(8,128)(2,1)S(1)}, bf16[32,32,256]{2,1,0:T(8,128)(2,1)}, u32[]{:S(2)}) copy-start(bf16[32,32,256]{2,1,0:T(8,128)(2,1)} %get-tuple-element.28) | copy-start | bytes 1572868
  78.6 11.7 %copy-start.17 = (bf16[160,1024]{1,0:T(8,128)(2,1)S(1)}, bf16[160,1024]{1,0:T(8,128)(2,1)}, u32[]{:S(2)}) copy-start(bf16[160,1024]{1,0:T(8,128)(2,1)} %get-tuple-element.64) | copy-start | bytes 983044
  78.6 11.9 %copy-start.16 = (bf16[160,1024]{1,0:T(8,128)(2,1)S(1)}, bf16[160,1024]{1,0:T(8,128)(2,1)}, u32[]{:S(2)}) copy-start(bf16[160,1024]{1,0:T(8,128)(2,1)} %get-tuple-element.62) | copy-start | bytes 983044
  78.6 12.2 %copy-start.15 = (bf16[160,1024]{1,0:T(8,128)(2,1)S(1)}, bf16[160,1024]{1,0:T(8,128)(2,1)}, u32[]{:S(2)}) copy-start(bf16[160,1024]{1,0:T(8,128)(2,1)} %get-tuple-element.60) | copy-start | bytes 983044
  78.7 12.5 %copy-start.14 = (bf16[160,1024]{1,0:T(8,128)(2,1)S(1)}, bf16[160,1024]{1,0:T(8,128)(2,1)}, u32[]{:S(2)}) copy-start(bf16[160,1024]{1,0:T(8,128)(2,1)} %get-tuple-element.58) | copy-start | bytes 983044
  78.7 12.7 %copy-start.12 = (bf16[160,1024]{1,0:T(8,128)(2,1)S(1)}, bf16[160,1024]{1,0:T(8,128)(2,1)}, u32[]{:S(2)}) copy-start(bf16[160,1024]{1,0:T(8,128)(2,1)} %get-tuple-element.56) | copy-start | bytes 983044
  78.7 13.0 %copy-start.11 = (bf16[160,1024]{1,0:T(8,128)(2,1)S(1)}, bf16[160,1024]{1,0:T(8,128)(2,1)}, u32[]{:S(2)}) copy-start(bf16[160,1024]{1,0:T(8,128)(2,1)} %get-tuple-element.54) | copy-start | bytes 983044
  80.2 11.7 %copy-start.13 = (bf16[160,1024]{1,0:T(8,128)(2,1)S(1)}, bf16[160,1024]{1,0:T(8,128)(2,1)}, u32[]{:S(2)}) copy-start(bf16[160,1024]{1,0:T(8,128)(2,1)} %get-tuple-element.52) | copy-start | bytes 983044
  83.1 21.5 %copy-start.19 = (bf16[64,256]{1,0:T(8,128)(2,1)S(1)}, bf16[64,256]{1,0:T(8,128)(2,1)}, u32[]{:S(2)}) copy-start(bf16[64,256]{1,0:T(8,128)(2,1)} %param.9) | copy-start | bytes 98308
  83.1 21.9 %copy-start.21 = (f32[256]{0:T(256)S(1)}, f32[256]{0:T(256)}, u32[]{:S(2)}) copy-start(f32[256]{0:T(256)} %param.12) | copy-start | bytes 3076
  92.9 11.1 %all-to-all-start = ((f32[4,40,256]{2,1,0:T(8,128)}), f32[4,40,256]{2,1,0:T(8,128)S(1)}, u32[]{:S(2)}, u32[]{:S(2)}) async-start(f32[4,40,256]{2,1,0:T(8,128)} %bitcast.21), calls=%async_computation | async-start | bytes 327680 | tf_op jit(solution)/shard_map/all_to_all | solution.py:85
  97.9 34.3 %reduce-scatter.2.cloned.1.call-start = ((), (), s32[]{:S(2)}) async-start(), calls=%async_computation.3 | async-start | bytes 327680 | tf_op jit(solution)/shard_map/reduce_scatter | solution.py:106
Sparse Core Ops, SparseCore 0:
  112.7 19.4 reduce-scatter.1
where the time goes:
time: 141 us
  blocking collectives  40.4 us (29%)
  matrix products  37.7 us (27%)
  waiting for transfers between devices  23.6 us (17%)
  between operations  14.5 us (10%)
  local copies, waits for them, and re-layouts  10.3 us (7%)
  starting transfers between devices  8.36 us (6%)
  other arithmetic  5.68 us (4%)
    dot_general x16, matrix products, tile_pool(): lax.dot_general(kernel_rows, block, (((1,), (1,)), ((), ())), preferred_e...  21.5 us
    reduce_scatter x1, waiting for transfers between devices, local(): lax.psum_scatter(jnp.dot(hidden, w_out, preferred_element_type=jnp.float3...  19.6 us
    all_gather x1, blocking collectives, local(): lax.all_gather(kernels, 'tile', axis=0, tiled=True)  15.4 us
    dot_general x16, matrix products, tile_pool(): pooled = pooled + jnp.dot(masked, block, preferred_element_type=jnp.float32)  13.9 us
    unnamed x1, blocking collectives  12 us
    all_gather x1, blocking collectives, local(): lax.all_gather(boxes.astype(jnp.bfloat16), 'tile', axis=0, tiled=True)  7.57 us
    slice x1, local copies, waits for them, and re-layouts, tile_pool(): strip_feats[tile_row * TS:(tile_row + 1) * TS, tile_col * TS:(tile_col +...  5.8 us
    all_gather x1, blocking collectives, local(): all_normed = lax.all_gather(normed, 'inst', axis=0, tiled=True)  5.43 us
  transfers between devices with their start and end apart: 3, of which 2 were waited for; matrix products, arithmetic and copies ran while one was open for 11% of the time, Pallas kernels for 0%

commit v1 on v0

v1 whole, which is shorter than its diff:
```python
import functools

import jax
import jax.numpy as jnp
from jax import lax
from jax.experimental import pallas as pl
from jax.experimental.pallas import tpu as pltpu
from jax.sharding import PartitionSpec as P

TS = 32
SR = 2
WC = 8
META = 16
ROWS_PER_STEP = 4
VMEM = pltpu.VMEM


def pack_kernel(kernels_ref, home_ref, boxes_ref, out_ref):
    count = kernels_ref.shape[0]
    out_ref[:count, :] = kernels_ref[...]
    out_ref[count:, :] = jnp.zeros((META, out_ref.shape[1]), out_ref.dtype)
    line = lax.broadcasted_iota(jnp.int32, (META, count), 0)
    meta = jnp.where(line == 0, home_ref[...], 0)
    for i in range(4):
        meta = jnp.where(line == i + 1, boxes_ref[i : i + 1, :], meta)
    out_ref[count:, :count] = meta.astype(jnp.float32).astype(out_ref.dtype)


def update_kernel(blocks, shards, slots, count, *refs):
    block_refs, refs = refs[:blocks], refs[blocks:]
    features_ref, gain_ref, refs = refs[0], refs[1], refs[2:]
    in_refs, out_w_refs, out_refs = refs[:shards], refs[shards : 2 * shards], refs[2 * shards :]
    bf16, f32 = jnp.bfloat16, jnp.float32
    mine = lax.axis_index("tile")
    stride, feat = count + META, block_refs[0].shape[1]
    sources = [
        (ref, i) for ref in block_refs for i in range(ref.shape[0] // stride)
    ]

    earlier = (
        lax.broadcasted_iota(jnp.int32, (count, count), 0)
        < lax.broadcasted_iota(jnp.int32, (count, count), 1)
    ).astype(bf16)
    slot = lax.broadcasted_iota(jnp.int32, (slots, count), 0).astype(f32)
    base = jnp.zeros((1, 1), f32)
    rows = jnp.zeros((slots, feat), f32)
    bounds = jnp.zeros((slots, META), f32)
    select = []
    for ref, i in sources:
        meta = ref[i * stride + count : (i + 1) * stride, :count]
        member = jnp.where(meta[0:1].astype(f32) == mine.astype(f32), 1.0, 0.0)
        rank = jnp.dot(
            jnp.broadcast_to(member, (8, count)).astype(bf16), earlier, preferred_element_type=f32
        )[0:1]
        pick = jnp.where((rank + base == slot) & (member > 0.0), 1.0, 0.0)
        pick16 = pick.astype(bf16)
        rows = rows + jnp.dot(
            pick16, ref[i * stride : i * stride + count, :], preferred_element_type=f32
        )
        bounds = bounds + lax.dot_general(
            pick16, meta, (((1,), (1,)), ((), ())), preferred_element_type=f32
        )
        select.append(pick.T.astype(bf16))
        base = base + jnp.sum(member, axis=1, keepdims=True)
    rows16 = rows.astype(bf16)

    width = WC * TS
    tile_col = (lax.broadcasted_iota(jnp.int32, (slots, width), 1) // TS).astype(f32)
    column = (bounds[:, 3:4] <= tile_col) & (tile_col <= bounds[:, 4:5])
    inside = [
        jnp.where(column & (bounds[:, 1:2] <= r) & (r <= bounds[:, 2:3]), 1.0, 0.0)
        for r in range(SR)
    ]

    steps = features_ref.shape[0] // ROWS_PER_STEP

    def cells(step):
        return features_ref[step * ROWS_PER_STEP : (step + 1) * ROWS_PER_STEP].reshape(
            ROWS_PER_STEP * width, feat
        )

    def logits(step):
        return lax.dot_general(
            rows16, cells(step), (((1,), (1,)), ((), ())), preferred_element_type=f32
        )

    pooled = jnp.zeros((slots, feat), f32)
    covered = jnp.zeros((slots, width), f32)
    now = logits(0)
    for step in range(steps):
        later = logits(step + 1) if step + 1 < steps else None
        mask = inside[step * ROWS_PER_STEP // TS]
        parts = []
        for j in range(ROWS_PER_STEP):
            part = mask * pl.reciprocal(
                1.0 + jnp.exp(-now[:, j * width : (j + 1) * width]), approx=True
            )
            covered = covered + part
            parts.append(part.astype(bf16))
        pooled = pooled + jnp.dot(
            jnp.concatenate(parts, axis=1), cells(step), preferred_element_type=f32
        )
        now = later
    area = jnp.sum(covered, axis=1, keepdims=True)

    merged = rows + pooled / area
    centred = merged - jnp.mean(merged, axis=1, keepdims=True)
    spread = jnp.mean(centred * centred, axis=1, keepdims=True)
    normed = (centred * lax.rsqrt(spread + 1e-05) * gain_ref[...]).astype(bf16)
    total = merged
    for w_in_ref, w_out_ref in zip(in_refs, out_w_refs):
        hidden = jnp.maximum(jnp.dot(normed, w_in_ref[...], preferred_element_type=f32), 0.0)
        total = total + jnp.dot(hidden.astype(bf16), w_out_ref[...], preferred_element_type=f32)
    updated = total.astype(bf16)

    for k, pick in enumerate(select):
        back = jnp.dot(pick, updated, preferred_element_type=f32).astype(bf16)
        ref, i = out_refs[k * len(out_refs) // len(select)], k % (len(select) // len(out_refs))
        ref[i * count : (i + 1) * count, :] = back


def shifted(x, axis, shift):
    size = lax.axis_size(axis)
    return lax.ppermute(x, axis, [(i, (i + shift) % size) for i in range(size)])


def local(features, kernels, home, boxes, gain, w_in, w_out):
    strips, holders = lax.axis_size("tile"), lax.axis_size("inst")
    count, feat = kernels.shape
    slots = strips * min(count, max(2, 5 * count // (2 * strips)))
    near = strips <= 8

    block = pl.pallas_call(
        pack_kernel,
        out_shape=jax.ShapeDtypeStruct((count + META, feat), kernels.dtype),
        in_specs=[pl.BlockSpec(memory_space=VMEM)] * 3,
        out_specs=pl.BlockSpec(memory_space=VMEM),
        name="pack",
    )(kernels, home.T, boxes.T)
    if near:
        blocks = [block] + [shifted(block, "tile", s) for s in range(1, strips)]
        outs = [jax.ShapeDtypeStruct((count, feat), kernels.dtype)] * strips
    else:
        blocks = [lax.all_gather(block, "tile", axis=0, tiled=True)]
        outs = [jax.ShapeDtypeStruct((strips * count, feat), kernels.dtype)]

    shards_in = [w_in] + [shifted(w_in, "inst", s) for s in range(1, holders)]
    shards_out = [w_out] + [shifted(w_out, "inst", s) for s in range(1, holders)]

    back = pl.pallas_call(
        functools.partial(update_kernel, len(blocks), holders, slots, count),
        out_shape=outs,
        in_specs=[pl.BlockSpec(memory_space=VMEM)] * (len(blocks) + 2 + 2 * holders),
        out_specs=[pl.BlockSpec(memory_space=VMEM)] * len(outs),
        compiler_params=pltpu.CompilerParams(vmem_limit_bytes=40 << 20),
        name="update",
    )(*blocks, features, gain.reshape(1, feat), *shards_in, *shards_out)
    if near:
        mine = back[0]
        for s in range(1, strips):
            mine = mine + shifted(back[s], "tile", strips - s)
        return mine
    got = lax.all_to_all(
        back[0].reshape(strips, count, feat), "tile", split_axis=0, concat_axis=0, tiled=True
    )
    return jnp.sum(got.astype(jnp.float32), axis=0).astype(kernels.dtype)


def solution(mesh):
    return jax.shard_map(
        local,
        mesh=mesh,
        in_specs=(
            P(("groups", "tile"), None, None),
            P(("groups", "tile", "inst"), None),
            P(("groups", "tile", "inst"), None),
            P(("groups", "tile", "inst"), None),
            P(),
            P(None, "inst"),
            P("inst", None),
        ),
        out_specs=P(("groups", "tile", "inst"), None),
        check_vma=False,
    )
```

time: 141 us -> 51.8 us (0.37)
  blocking collectives: 40.4 us -> 0 us
  matrix products: 37.7 us -> 0 us
  between operations: 14.5 us -> 0.03 us
  Pallas kernels: 0 us -> 7.6 us
  starting transfers between devices: 8.36 us -> 14.6 us
  other arithmetic: 5.68 us -> 0.62 us
  local copies, waits for them, and re-layouts: 10.3 us -> 6.74 us
  waiting for transfers between devices: 23.6 us -> 21.9 us
    dot_general x35 -> x0, matrix products: 37.7 us -> none  [the longest x16 21.5 us: tile_pool(): lax.dot_general(kernel_rows, block, (((1,), (1,)), ((), ())), preferred_e...]
    all_gather x3 -> x0, blocking collectives: 28.4 us -> none  [the longest x1 15.4 us: local(): lax.all_gather(kernels, 'tile', axis=0, tiled=True)]
    ppermute x0 -> x12, waiting for transfers between devices: none -> 21.9 us  [shifted(): return lax.ppermute(x, axis, [(i, (i + shift) % size) for i in range(size)])]
    reduce_scatter x1 -> x0, waiting for transfers between devices: 19.6 us -> none  [local(): lax.psum_scatter(jnp.dot(hidden, w_out, preferred_element_type=jnp.float3...]
    ppermute x0 -> x12, starting transfers between devices: none -> 14.6 us  [shifted(): return lax.ppermute(x, axis, [(i, (i + shift) % size) for i in range(size)])]
    unnamed x1 -> x0, blocking collectives: 12 us -> none
    all_to_all x2 -> x0, starting transfers between devices: 8.36 us -> none  [the longest x1 5.09 us: local(): lax.all_to_all(pooled.reshape(strips, capacity, feat_width), 'tile', spli...]
    pallas_call x0 -> x2, Pallas kernels: none -> 7.6 us  [the longest x1 6.21 us: local(): pl.pallas_call(functools.partial(update_kernel, len(blocks), holders, slo...]
  transfers between devices with their start and end apart: 3 -> 12, of which waited for: 2 -> 10; matrix products, arithmetic and copies ran while one was open for 11% -> 0% of each run, Pallas kernels for 0% -> 3%
where the time goes in v1:
time: 51.8 us; the launch traced here: 51.5 us
  waiting for transfers between devices  21.9 us (42%)
  starting transfers between devices  14.6 us (28%)
  Pallas kernels  7.6 us (15%)
  local copies, waits for them, and re-layouts  6.74 us (13%)
  other arithmetic  0.62 us (1%)
    ppermute x12, waiting for transfers between devices, shifted(): return lax.ppermute(x, axis, [(i, (i + shift) % size) for i in range(size)])  21.9 us
    ppermute x12, starting transfers between devices, shifted(): return lax.ppermute(x, axis, [(i, (i + shift) % size) for i in range(size)])  14.6 us
    unnamed x10, local copies, waits for them, and re-layouts  6.74 us
    pallas_call x1, Pallas kernels, local(): pl.pallas_call(functools.partial(update_kernel, len(blocks), holders, slo...  6.21 us
    pallas_call x1, Pallas kernels, local(): pl.pallas_call(pack_kernel, out_shape=jax.ShapeDtypeStruct((count + META,...  1.39 us
  transfers between devices with their start and end apart: 12, of which 10 were waited for; matrix products, arithmetic and copies ran while one was open for 0% of the time, Pallas kernels for 3%

profile of v1, /device:TPU:0, one launch (start us, length us, event | category | flops | bytes accessed | tf_op | source)
XLA Modules:
  0.0 51.5 jit_solution(13019024741182792598)
XLA Ops:
  0.0 2.9 %collective-permute-start.4 = (bf16[256,512]{1,0:T(8,128)(2,1)}, bf16[256,512]{1,0:T(8,128)(2,1)S(1)}, u32[]{:S(2)}, u32[]{:S(2)}) collective-permute-start(bf16[256,512]{1,0:T(8,128)(2,1)} %refs_6_.1), channel_id=1, source_target_pairs={{0,2},{1,3},{2,0},{3,1},{4,6},{5,7},{6,4},{7,5},{8,10},{9,11},{10,... | collective-permute-start | bytes 786440 | tf_op jit(solution)/shard_map/ppermute | solution.py:124
  2.9 1.4 %pack.1.refs_0_ = bf16[80,256]{1,0:T(8,128)(2,1)} custom-call(bf16[64,256]{1,0:T(8,128)(2,1)} %kernels_ref.1, s32[1,64]{1,0:T(1,128)} %bitcast.5, s32[4,64]{1,0:T(4,128)} %bitcast.4), custom_call_target="tpu_custom_call" | custom-call | tf_op jit(solution)/shard_map/pack/pallas_call | solution.py:133
  4.3 3.6 %collective-permute-start.2 = (bf16[80,256]{1,0:T(8,128)(2,1)}, bf16[80,256]{1,0:T(8,128)(2,1)S(1)}, u32[]{:S(2)}, u32[]{:S(2)}) collective-permute-start(bf16[80,256]{1,0:T(8,128)(2,1)} %pack.1.refs_0_), channel_id=1, source_target_pairs={{0,12},{4,0},{8,4},{12,8},{1,13},{5,1},{9,5},{13,9},{2,14},{6,2},{... | collective-permute-start | bytes 122888 | tf_op jit(solution)/shard_map/ppermute | solution.py:124
  7.9 0.0 collective-permute-start.1
  7.9 1.0 %collective-permute-start = (bf16[80,256]{1,0:T(8,128)(2,1)}, bf16[80,256]{1,0:T(8,128)(2,1)S(1)}, u32[]{:S(2)}, u32[]{:S(2)}) collective-permute-start(bf16[80,256]{1,0:T(8,128)(2,1)} %pack.1.refs_0_), channel_id=1, source_target_pairs={{0,4},{4,8},{8,12},{12,0},{1,5},{5,9},{9,13},{13,1},{2,6},{6,10},{... | collective-permute-start | bytes 122888 | tf_op jit(solution)/shard_map/ppermute | solution.py:124
  9.0 0.0 collective-permute-start.3
  9.0 1.0 %collective-permute-done.2.refs_3_ = bf16[80,256]{1,0:T(8,128)(2,1)S(1)} collective-permute-done((bf16[80,256]{1,0:T(8,128)(2,1)}, bf16[80,256]{1,0:T(8,128)(2,1)S(1)}, u32[]{:S(2)}, u32[]{:S(2)}) %collective-permute-start.2) | collective-permute-done | bytes 40992 | tf_op jit(solution)/shard_map/ppermute | solution.py:124
  9.9 0.8 %collective-permute-start.5 = (bf16[256,512]{1,0:T(8,128)(2,1)}, bf16[256,512]{1,0:T(8,128)(2,1)S(1)}, u32[]{:S(2)}, u32[]{:S(2)}) collective-permute-start(bf16[256,512]{1,0:T(8,128)(2,1)} %refs_6_.1), channel_id=1, source_target_pairs={{0,3},{1,0},{2,1},{3,2},{4,7},{5,4},{6,5},{7,6},{8,11},{9,8},{10,9... | collective-permute-start | bytes 786440 | tf_op jit(solution)/shard_map/ppermute | solution.py:124
  10.7 2.3 %collective-permute-done.1.refs_2_ = bf16[80,256]{1,0:T(8,128)(2,1)S(1)} collective-permute-done((bf16[80,256]{1,0:T(8,128)(2,1)}, bf16[80,256]{1,0:T(8,128)(2,1)S(1)}, u32[]{:S(2)}, u32[]{:S(2)}) %collective-permute-start.1) | collective-permute-done | bytes 40992 | tf_op jit(solution)/shard_map/ppermute | solution.py:124
  13.0 0.5 %collective-permute-start.7 = (bf16[512,256]{1,0:T(8,128)(2,1)}, bf16[512,256]{1,0:T(8,128)(2,1)S(1)}, u32[]{:S(2)}, u32[]{:S(2)}) collective-permute-start(bf16[512,256]{1,0:T(8,128)(2,1)} %refs_10_.1), channel_id=1, source_target_pairs={{0,2},{1,3},{2,0},{3,1},{4,6},{5,7},{6,4},{7,5},{8,10},{9,11},{10,... | collective-permute-start | bytes 786440 | tf_op jit(solution)/shard_map/ppermute | solution.py:124
  13.6 0.4 collective-permute-done.refs_1_
  14.0 0.0 collective-permute-start.6
  14.0 0.0 collective-permute-done.4.refs_8_
  14.0 1.7 %collective-permute-start.8 = (bf16[512,256]{1,0:T(8,128)(2,1)}, bf16[512,256]{1,0:T(8,128)(2,1)S(1)}, u32[]{:S(2)}, u32[]{:S(2)}) collective-permute-start(bf16[512,256]{1,0:T(8,128)(2,1)} %refs_10_.1), channel_id=1, source_target_pairs={{0,3},{1,0},{2,1},{3,2},{4,7},{5,4},{6,5},{7,6},{8,11},{9,8},{10,9... | collective-permute-start | bytes 786440 | tf_op jit(solution)/shard_map/ppermute | solution.py:124
  15.7 1.3 %collective-permute-done.3.refs_7_ = bf16[256,512]{1,0:T(8,128)(2,1)S(1)} collective-permute-done((bf16[256,512]{1,0:T(8,128)(2,1)}, bf16[256,512]{1,0:T(8,128)(2,1)S(1)}, u32[]{:S(2)}, u32[]{:S(2)}) %collective-permute-start.3) | collective-permute-done | bytes 262176 | tf_op jit(solution)/shard_map/ppermute | solution.py:124
  17.0 0.8 %collective-permute-done.5.refs_9_ = bf16[256,512]{1,0:T(8,128)(2,1)S(1)} collective-permute-done((bf16[256,512]{1,0:T(8,128)(2,1)}, bf16[256,512]{1,0:T(8,128)(2,1)S(1)}, u32[]{:S(2)}, u32[]{:S(2)}) %collective-permute-start.5) | collective-permute-done | bytes 262176 | tf_op jit(solution)/shard_map/ppermute | solution.py:124
  17.8 6.4 %collective-permute-done.7.refs_12_ = bf16[512,256]{1,0:T(8,128)(2,1)S(1)} collective-permute-done((bf16[512,256]{1,0:T(8,128)(2,1)}, bf16[512,256]{1,0:T(8,128)(2,1)S(1)}, u32[]{:S(2)}, u32[]{:S(2)}) %collective-permute-start.7) | collective-permute-done | bytes 262176 | tf_op jit(solution)/shard_map/ppermute | solution.py:124
  24.2 4.0 %collective-permute-done.6.refs_11_ = bf16[512,256]{1,0:T(8,128)(2,1)S(1)} collective-permute-done((bf16[512,256]{1,0:T(8,128)(2,1)}, bf16[512,256]{1,0:T(8,128)(2,1)S(1)}, u32[]{:S(2)}, u32[]{:S(2)}) %collective-permute-start.6) | collective-permute-done | bytes 262176 | tf_op jit(solution)/shard_map/ppermute | solution.py:124
  28.2 0.0 collective-permute-done.8.refs_13_
  28.2 0.0 copy-start
  28.2 3.4 %copy-done = bf16[64,256,256]{2,1,0:T(8,128)(2,1)S(1)} copy-done((bf16[64,256,256]{2,1,0:T(8,128)(2,1)S(1)}, bf16[64,256,256]{2,1,0:T(8,128)(2,1)}, u32[]{:S(2)}) %copy-start) | copy-done | bytes 8388632
  31.6 0.0 copy-start.1
  31.6 0.9 %copy-done.1 = bf16[256,512]{1,0:T(8,128)(2,1)S(1)} copy-done((bf16[256,512]{1,0:T(8,128)(2,1)S(1)}, bf16[256,512]{1,0:T(8,128)(2,1)}, u32[]{:S(2)}) %copy-start.1) | copy-done | bytes 262168
  32.5 0.0 copy-start.2
  32.5 0.9 %copy-done.2 = bf16[512,256]{1,0:T(8,128)(2,1)S(1)} copy-done((bf16[512,256]{1,0:T(8,128)(2,1)S(1)}, bf16[512,256]{1,0:T(8,128)(2,1)}, u32[]{:S(2)}) %copy-start.2) | copy-done | bytes 262168
  33.5 0.0 copy-start.3
  33.5 0.8 %copy-done.3 = bf16[80,256]{1,0:T(8,128)(2,1)S(1)} copy-done((bf16[80,256]{1,0:T(8,128)(2,1)S(1)}, bf16[80,256]{1,0:T(8,128)(2,1)}, u32[]{:S(2)}) %copy-start.3) | copy-done | bytes 40984
  34.3 0.0 copy-start.4
  34.3 0.7 %copy-done.4 = f32[256]{0:T(256)S(1)} copy-done((f32[256]{0:T(256)S(1)}, f32[256]{0:T(256)}, u32[]{:S(2)}) %copy-start.4) | copy-done | bytes 1048
  34.9 6.2 %update.1 = (bf16[64,256]{1,0:T(8,128)(2,1)S(1)}, bf16[64,256]{1,0:T(8,128)(2,1)S(1)}, bf16[64,256]{1,0:T(8,128)(2,1)S(1)}, bf16[64,256]{1,0:T(8,128)(2,1)S(1)}) custom-call(bf16[80,256]{1,0:T(8,128)(2,1)S(1)} %copy-done.3, bf16[80,256]{1,0:T(8,128)(2,1)S(1)} %collective-permute-done.refs_1_, bf16[80,256]{1,0:T(8,128)(2,1)S(1)} %collective-permute-done.1.refs_2_, ...), custom_call_target="tpu_custom_call" | custom-call | tf_op jit(solution)/shard_map/update/pallas_call | solution.py:150
  41.2 2.3 %collective-permute-start.9 = (bf16[64,256]{1,0:T(8,128)(2,1)S(1)}, bf16[64,256]{1,0:T(8,128)(2,1)S(1)}, u32[]{:S(2)}, u32[]{:S(2)}) collective-permute-start(bf16[64,256]{1,0:T(8,128)(2,1)S(1)} %get-tuple-element.10), channel_id=1, source_target_pairs={{0,12},{4,0},{8,4},{12,8},{1,13},{5,1},{9,5},{13,9},{2,14},{6,2},{... | collective-permute-start | bytes 98312 | tf_op jit(solution)/shard_map/ppermute | solution.py:124
  43.5 1.7 %collective-permute-start.10 = (bf16[64,256]{1,0:T(8,128)(2,1)S(1)}, bf16[64,256]{1,0:T(8,128)(2,1)S(1)}, u32[]{:S(2)}, u32[]{:S(2)}) collective-permute-start(bf16[64,256]{1,0:T(8,128)(2,1)S(1)} %get-tuple-element.11), channel_id=1, source_target_pairs={{0,8},{4,12},{8,0},{12,4},{1,9},{5,13},{9,1},{13,5},{2,10},{6,14},... | collective-permute-start | bytes 98312 | tf_op jit(solution)/shard_map/ppermute | solution.py:124
  45.2 0.0 collective-permute-start.11
  45.2 0.7 %collective-permute-done.9 = bf16[64,256]{1,0:T(8,128)(2,1)S(1)} collective-permute-done((bf16[64,256]{1,0:T(8,128)(2,1)S(1)}, bf16[64,256]{1,0:T(8,128)(2,1)S(1)}, u32[]{:S(2)}, u32[]{:S(2)}) %collective-permute-start.9) | collective-permute-done | bytes 32800 | tf_op jit(solution)/shard_map/ppermute | solution.py:124
  45.9 2.9 %collective-permute-done.10 = bf16[64,256]{1,0:T(8,128)(2,1)S(1)} collective-permute-done((bf16[64,256]{1,0:T(8,128)(2,1)S(1)}, bf16[64,256]{1,0:T(8,128)(2,1)S(1)}, u32[]{:S(2)}, u32[]{:S(2)}) %collective-permute-start.10) | collective-permute-done | bytes 32800 | tf_op jit(solution)/shard_map/ppermute | solution.py:124
  48.7 2.1 %collective-permute-done.11 = bf16[64,256]{1,0:T(8,128)(2,1)S(1)} collective-permute-done((bf16[64,256]{1,0:T(8,128)(2,1)S(1)}, bf16[64,256]{1,0:T(8,128)(2,1)S(1)}, u32[]{:S(2)}, u32[]{:S(2)}) %collective-permute-start.11) | collective-permute-done | bytes 32800 | tf_op jit(solution)/shard_map/ppermute | solution.py:124
  50.9 0.6 %add_add_fusion = bf16[64,256]{1,0:T(8,128)(2,1)} fusion(bf16[64,256]{1,0:T(8,128)(2,1)S(1)} %collective-permute-done.11, bf16[64,256]{1,0:T(8,128)(2,1)S(1)} %collective-permute-done.10, bf16[64,256]{1,0:T(8,128)(2,1)S(1)} %get-tuple-element.9, bf16[64,256]{1,0:T(8,128)(2,1)S(1)} %collective-permute-done.9), kind=kLoop, calls=%fused_computation | loop fusion | flops 49152 | bytes 163840 | tf_op jit(solution)/shard_map/add | solution.py:161
Async XLA Ops:
  0.0 14.0 %collective-permute-start.4 = (bf16[256,512]{1,0:T(8,128)(2,1)}, bf16[256,512]{1,0:T(8,128)(2,1)S(1)}, u32[]{:S(2)}, u32[]{:S(2)}) collective-permute-start(bf16[256,512]{1,0:T(8,128)(2,1)} %refs_6_.1), channel_id=1, source_target_pairs={{0,2},{1,3},{2,0},{3,1},{4,6},{5,7},{6,4},{7,5},{8,10},{9,11},{10,... | collective-permute-start | bytes 786440 | tf_op jit(solution)/shard_map/ppermute | solution.py:124
  4.3 5.6 %collective-permute-start.2 = (bf16[80,256]{1,0:T(8,128)(2,1)}, bf16[80,256]{1,0:T(8,128)(2,1)S(1)}, u32[]{:S(2)}, u32[]{:S(2)}) collective-permute-start(bf16[80,256]{1,0:T(8,128)(2,1)} %pack.1.refs_0_), channel_id=1, source_target_pairs={{0,12},{4,0},{8,4},{12,8},{1,13},{5,1},{9,5},{13,9},{2,14},{6,2},{... | collective-permute-start | bytes 122888 | tf_op jit(solution)/shard_map/ppermute | solution.py:124
  7.9 5.1 %collective-permute-start.1 = (bf16[80,256]{1,0:T(8,128)(2,1)}, bf16[80,256]{1,0:T(8,128)(2,1)S(1)}, u32[]{:S(2)}, u32[]{:S(2)}) collective-permute-start(bf16[80,256]{1,0:T(8,128)(2,1)} %pack.1.refs_0_), channel_id=1, source_target_pairs={{0,8},{4,12},{8,0},{12,4},{1,9},{5,13},{9,1},{13,5},{2,10},{6,14},... | collective-permute-start | bytes 122888 | tf_op jit(solution)/shard_map/ppermute | solution.py:124
  7.9 6.0 %collective-permute-start = (bf16[80,256]{1,0:T(8,128)(2,1)}, bf16[80,256]{1,0:T(8,128)(2,1)S(1)}, u32[]{:S(2)}, u32[]{:S(2)}) collective-permute-start(bf16[80,256]{1,0:T(8,128)(2,1)} %pack.1.refs_0_), channel_id=1, source_target_pairs={{0,4},{4,8},{8,12},{12,0},{1,5},{5,9},{9,13},{13,1},{2,6},{6,10},{... | collective-permute-start | bytes 122888 | tf_op jit(solution)/shard_map/ppermute | solution.py:124
  9.0 8.0 %collective-permute-start.3 = (bf16[256,512]{1,0:T(8,128)(2,1)}, bf16[256,512]{1,0:T(8,128)(2,1)S(1)}, u32[]{:S(2)}, u32[]{:S(2)}) collective-permute-start(bf16[256,512]{1,0:T(8,128)(2,1)} %refs_6_.1), channel_id=1, source_target_pairs={{0,1},{1,2},{2,3},{3,0},{4,5},{5,6},{6,7},{7,4},{8,9},{9,10},{10,1... | collective-permute-start | bytes 786440 | tf_op jit(solution)/shard_map/ppermute | solution.py:124
  9.9 7.9 %collective-permute-start.5 = (bf16[256,512]{1,0:T(8,128)(2,1)}, bf16[256,512]{1,0:T(8,128)(2,1)S(1)}, u32[]{:S(2)}, u32[]{:S(2)}) collective-permute-start(bf16[256,512]{1,0:T(8,128)(2,1)} %refs_6_.1), channel_id=1, source_target_pairs={{0,3},{1,0},{2,1},{3,2},{4,7},{5,4},{6,5},{7,6},{8,11},{9,8},{10,9... | collective-permute-start | bytes 786440 | tf_op jit(solution)/shard_map/ppermute | solution.py:124
  13.0 11.1 %collective-permute-start.7 = (bf16[512,256]{1,0:T(8,128)(2,1)}, bf16[512,256]{1,0:T(8,128)(2,1)S(1)}, u32[]{:S(2)}, u32[]{:S(2)}) collective-permute-start(bf16[512,256]{1,0:T(8,128)(2,1)} %refs_10_.1), channel_id=1, source_target_pairs={{0,2},{1,3},{2,0},{3,1},{4,6},{5,7},{6,4},{7,5},{8,10},{9,11},{10,... | collective-permute-start | bytes 786440 | tf_op jit(solution)/shard_map/ppermute | solution.py:124
  14.0 14.2 %collective-permute-start.6 = (bf16[512,256]{1,0:T(8,128)(2,1)}, bf16[512,256]{1,0:T(8,128)(2,1)S(1)}, u32[]{:S(2)}, u32[]{:S(2)}) collective-permute-start(bf16[512,256]{1,0:T(8,128)(2,1)} %refs_10_.1), channel_id=1, source_target_pairs={{0,1},{1,2},{2,3},{3,0},{4,5},{5,6},{6,7},{7,4},{8,9},{9,10},{10,1... | collective-permute-start | bytes 786440 | tf_op jit(solution)/shard_map/ppermute | solution.py:124
  14.0 14.2 %collective-permute-start.8 = (bf16[512,256]{1,0:T(8,128)(2,1)}, bf16[512,256]{1,0:T(8,128)(2,1)S(1)}, u32[]{:S(2)}, u32[]{:S(2)}) collective-permute-start(bf16[512,256]{1,0:T(8,128)(2,1)} %refs_10_.1), channel_id=1, source_target_pairs={{0,3},{1,0},{2,1},{3,2},{4,7},{5,4},{6,5},{7,6},{8,11},{9,8},{10,9... | collective-permute-start | bytes 786440 | tf_op jit(solution)/shard_map/ppermute | solution.py:124
  28.2 3.4 %copy-start = (bf16[64,256,256]{2,1,0:T(8,128)(2,1)S(1)}, bf16[64,256,256]{2,1,0:T(8,128)(2,1)}, u32[]{:S(2)}) copy-start(bf16[64,256,256]{2,1,0:T(8,128)(2,1)} %refs_4_.1) | copy-start | bytes 25165828
  31.6 0.9 %copy-start.1 = (bf16[256,512]{1,0:T(8,128)(2,1)S(1)}, bf16[256,512]{1,0:T(8,128)(2,1)}, u32[]{:S(2)}) copy-start(bf16[256,512]{1,0:T(8,128)(2,1)} %refs_6_.1) | copy-start | bytes 786436
  32.5 0.9 %copy-start.2 = (bf16[512,256]{1,0:T(8,128)(2,1)S(1)}, bf16[512,256]{1,0:T(8,128)(2,1)}, u32[]{:S(2)}) copy-start(bf16[512,256]{1,0:T(8,128)(2,1)} %refs_10_.1) | copy-start | bytes 786436
  33.5 0.8 %copy-start.3 = (bf16[80,256]{1,0:T(8,128)(2,1)S(1)}, bf16[80,256]{1,0:T(8,128)(2,1)}, u32[]{:S(2)}) copy-start(bf16[80,256]{1,0:T(8,128)(2,1)} %pack.1.refs_0_) | copy-start | bytes 122884
  34.3 0.7 %copy-start.4 = (f32[256]{0:T(256)S(1)}, f32[256]{0:T(256)}, u32[]{:S(2)}) copy-start(f32[256]{0:T(256)} %param.11) | copy-start | bytes 3076
  41.2 4.7 %collective-permute-start.9 = (bf16[64,256]{1,0:T(8,128)(2,1)S(1)}, bf16[64,256]{1,0:T(8,128)(2,1)S(1)}, u32[]{:S(2)}, u32[]{:S(2)}) collective-permute-start(bf16[64,256]{1,0:T(8,128)(2,1)S(1)} %get-tuple-element.10), channel_id=1, source_target_pairs={{0,12},{4,0},{8,4},{12,8},{1,13},{5,1},{9,5},{13,9},{2,14},{6,2},{... | collective-permute-start | bytes 98312 | tf_op jit(solution)/shard_map/ppermute | solution.py:124
  43.5 5.2 %collective-permute-start.10 = (bf16[64,256]{1,0:T(8,128)(2,1)S(1)}, bf16[64,256]{1,0:T(8,128)(2,1)S(1)}, u32[]{:S(2)}, u32[]{:S(2)}) collective-permute-start(bf16[64,256]{1,0:T(8,128)(2,1)S(1)} %get-tuple-element.11), channel_id=1, source_target_pairs={{0,8},{4,12},{8,0},{12,4},{1,9},{5,13},{9,1},{13,5},{2,10},{6,14},... | collective-permute-start | bytes 98312 | tf_op jit(solution)/shard_map/ppermute | solution.py:124
  45.2 5.7 %collective-permute-start.11 = (bf16[64,256]{1,0:T(8,128)(2,1)S(1)}, bf16[64,256]{1,0:T(8,128)(2,1)S(1)}, u32[]{:S(2)}, u32[]{:S(2)}) collective-permute-start(bf16[64,256]{1,0:T(8,128)(2,1)S(1)} %get-tuple-element.12), channel_id=1, source_target_pairs={{0,4},{4,8},{8,12},{12,0},{1,5},{5,9},{9,13},{13,1},{2,6},{6,10},{... | collective-permute-start | bytes 98312 | tf_op jit(solution)/shard_map/ppermute | solution.py:124

commit v2 on v1

v2 whole, which is shorter than its diff:
```python
import functools

import jax
import jax.numpy as jnp
from jax import lax
from jax.experimental import pallas as pl
from jax.experimental.pallas import tpu as pltpu
from jax.sharding import PartitionSpec as P

TS = 32
SR = 2
WC = 8
META = 16
ROWS_PER_STEP = 4
ARRIVALS = (16, 16, 32)
VMEM = pltpu.VMEM


def write_block(kernels_ref, home_ref, boxes_ref, out_ref):
    count = kernels_ref.shape[0]
    out_ref[:count, :] = kernels_ref[...]
    out_ref[count:, :] = jnp.zeros((META, out_ref.shape[1]), out_ref.dtype)
    line = lax.broadcasted_iota(jnp.int32, (META, count), 0)
    meta = jnp.where(line == 0, home_ref[...], 0)
    for i in range(4):
        meta = jnp.where(line == i + 1, boxes_ref[i : i + 1, :], meta)
    out_ref[count:, :count] = meta.astype(jnp.float32).astype(out_ref.dtype)


def pack_kernel(kernels_ref, home_ref, boxes_ref, w_in_hbm, w_out_hbm, block_ref, shard_ref, sems):
    hidden, feat = w_out_hbm.shape
    copies = [pltpu.make_async_copy(w_out_hbm, shard_ref.at[pl.ds(0, hidden)], sems.at[0])]
    for i in range(hidden // feat):
        copies.append(
            pltpu.make_async_copy(
                w_in_hbm.at[:, pl.ds(i * feat, feat)],
                shard_ref.at[pl.ds(hidden + i * feat, feat)],
                sems.at[i + 1],
            )
        )
    for copy in copies:
        copy.start()
    write_block(kernels_ref, home_ref, boxes_ref, block_ref)
    for copy in copies:
        copy.wait()


def pool_kernel(blocks, slots, count, *refs):
    block_refs, features_hbm, refs = refs[:blocks], refs[blocks], refs[blocks + 1 :]
    out_refs, (features_ref, sems) = refs[:-2], refs[-2:]
    bf16, f32 = jnp.bfloat16, jnp.float32
    mine = lax.axis_index("tile")
    stride, feat = count + META, block_refs[0].shape[1]
    steps = features_ref.shape[0] // ROWS_PER_STEP
    copies, at = {}, 0
    for i, size in enumerate(ARRIVALS):
        part = pl.ds(at, size)
        copies[at // ROWS_PER_STEP] = pltpu.make_async_copy(
            features_hbm.at[part], features_ref.at[part], sems.at[i]
        )
        copies[at // ROWS_PER_STEP].start()
        at += size

    sources = [(ref, i) for ref in block_refs for i in range(ref.shape[0] // stride)]
    earlier = (
        lax.broadcasted_iota(jnp.int32, (count, count), 0)
        < lax.broadcasted_iota(jnp.int32, (count, count), 1)
    ).astype(bf16)
    slot = lax.broadcasted_iota(jnp.int32, (slots, count), 0).astype(f32)
    base = jnp.zeros((1, 1), f32)
    rows = jnp.zeros((slots, feat), f32)
    bounds = jnp.zeros((slots, META), f32)
    select = [None] * len(sources)
    for k in range(len(sources)):
        ref, i = sources[k]
        meta = ref[i * stride + count : (i + 1) * stride, :count]
        member = jnp.where(meta[0:1].astype(f32) == mine.astype(f32), 1.0, 0.0)
        rank = jnp.dot(
            jnp.broadcast_to(member, (8, count)).astype(bf16), earlier, preferred_element_type=f32
        )[0:1]
        pick = jnp.where((rank + base == slot) & (member > 0.0), 1.0, 0.0)
        pick16 = pick.astype(bf16)
        rows = rows + jnp.dot(
            pick16, ref[i * stride : i * stride + count, :], preferred_element_type=f32
        )
        bounds = bounds + lax.dot_general(
            pick16, meta, (((1,), (1,)), ((), ())), preferred_element_type=f32
        )
        select[k] = pick.T.astype(bf16)
        base = base + jnp.sum(member, axis=1, keepdims=True)
    rows16 = rows.astype(bf16)

    width = WC * TS
    tile_col = (lax.broadcasted_iota(jnp.int32, (slots, width), 1) // TS).astype(f32)
    column = (bounds[:, 3:4] <= tile_col) & (tile_col <= bounds[:, 4:5])
    inside = [
        jnp.where(column & (bounds[:, 1:2] <= r) & (r <= bounds[:, 2:3]), 1.0, 0.0)
        for r in range(SR)
    ]

    def cells(step):
        return features_ref[step * ROWS_PER_STEP : (step + 1) * ROWS_PER_STEP].reshape(
            ROWS_PER_STEP * width, feat
        )

    def logits(step):
        if step in copies:
            copies[step].wait()
        return lax.dot_general(
            rows16, cells(step), (((1,), (1,)), ((), ())), preferred_element_type=f32
        )

    pooled = jnp.zeros((slots, feat), f32)
    covered = jnp.zeros((slots, width), f32)
    now = logits(0)
    for step in range(steps):
        later = logits(step + 1) if step + 1 < steps else None
        mask = inside[step * ROWS_PER_STEP // TS]
        parts = []
        for j in range(ROWS_PER_STEP):
            part = mask * pl.reciprocal(
                1.0 + jnp.exp(-now[:, j * width : (j + 1) * width]), approx=True
            )
            covered = covered + part
            parts.append(part.astype(bf16))
        pooled = pooled + jnp.dot(
            jnp.concatenate(parts, axis=1), cells(step), preferred_element_type=f32
        )
        now = later
    area = jnp.sum(covered, axis=1, keepdims=True)
    ratio = (pooled / area).astype(bf16)

    for k, pick in enumerate(select):
        back = jnp.dot(pick, ratio, preferred_element_type=f32).astype(bf16)
        ref, i = out_refs[k * len(out_refs) // len(select)], k % (len(select) // len(out_refs))
        ref[i * count : (i + 1) * count, :] = back


def through(normed, total, shard_refs):
    feat = total.shape[1]
    for ref in shard_refs:
        width = ref.shape[0] // 2
        for i in range(0, width, feat):
            hidden = jnp.dot(
                normed, ref[width + i : width + i + feat, :], preferred_element_type=jnp.float32
            )
            total = total + jnp.dot(
                jnp.maximum(hidden, 0.0).astype(normed.dtype),
                ref[i : i + feat, :],
                preferred_element_type=jnp.float32,
            )
    return total


def update_kernel(backs, shards, *refs):
    back_refs, refs = refs[:backs], refs[backs:]
    own_hbm, shard_refs, refs = refs[:2], refs[2 : 2 + shards], refs[2 + shards :]
    normed_ref, total_ref, kernels_ref, gain_ref, sems = refs
    own = (kernels_ref, gain_ref)
    f32 = jnp.float32
    copies = [pltpu.make_async_copy(a, b, sems.at[i]) for i, (a, b) in enumerate(zip(own_hbm, own))]
    for copy in copies:
        copy.start()
    ratio = back_refs[0][...].astype(f32)
    for ref in back_refs[1:]:
        ratio = ratio + ref[...].astype(f32)
    copies[0].wait()
    merged = kernels_ref[...].astype(f32) + ratio
    centred = merged - jnp.mean(merged, axis=1, keepdims=True)
    spread = jnp.mean(centred * centred, axis=1, keepdims=True)
    copies[1].wait()
    normed = (centred * lax.rsqrt(spread + 1e-05) * gain_ref[...]).astype(normed_ref.dtype)
    normed_ref[...] = normed
    total_ref[...] = through(normed, merged, shard_refs)


def finish_kernel(normed_ref, total_ref, *refs):
    out_ref = refs[-1]
    out_ref[...] = through(normed_ref[...], total_ref[...], refs[:-1]).astype(out_ref.dtype)


def exchanged(x, axis, distance):
    return lax.ppermute(x, axis, [(i, i ^ distance) for i in range(lax.axis_size(axis))])


def local(features, kernels, home, boxes, gain, w_in, w_out):
    strips, holders = lax.axis_size("tile"), lax.axis_size("inst")
    count, feat = kernels.shape
    slots = strips * min(count, max(2, 5 * count // (2 * strips)))
    near = strips <= 8
    any_, hbm = pl.BlockSpec(memory_space=VMEM), pl.BlockSpec(memory_space=pltpu.HBM)

    block, shard = pl.pallas_call(
        pack_kernel,
        out_shape=[
            pltpu.VMEM((count + META, feat), kernels.dtype),
            pltpu.VMEM((2 * w_out.shape[0], feat), w_out.dtype),
        ],
        in_specs=[any_] * 3 + [hbm] * 2,
        out_specs=[any_] * 2,
        scratch_shapes=[pltpu.SemaphoreType.DMA((1 + w_out.shape[0] // feat,))],
        name="pack",
    )(kernels, home.T, boxes.T, w_in, w_out)
    if near:
        blocks = [block] + [exchanged(block, "tile", d) for d in range(1, strips)]
        outs = [jax.ShapeDtypeStruct((count, feat), kernels.dtype)] * strips
    else:
        blocks = [lax.all_gather(block, "tile", axis=0, tiled=True)]
        outs = [jax.ShapeDtypeStruct((strips * count, feat), kernels.dtype)]

    shards = [shard]
    distance = holders // 2
    while distance > 1:
        shards += [exchanged(x, "inst", distance) for x in shards]
        distance //= 2

    back = pl.pallas_call(
        functools.partial(pool_kernel, len(blocks), slots, count),
        out_shape=outs,
        in_specs=[any_] * len(blocks) + [hbm],
        out_specs=[any_] * len(outs),
        scratch_shapes=[
            pltpu.VMEM(features.shape, features.dtype),
            pltpu.SemaphoreType.DMA((len(ARRIVALS),)),
        ],
        compiler_params=pltpu.CompilerParams(vmem_limit_bytes=48 << 20),
        cost_estimate=pl.CostEstimate(
            flops=40 * slots * features.size, bytes_accessed=2 * features.size, transcendentals=0
        ),
        name="pool",
    )(*blocks, features)
    if near:
        backs = [back[0]] + [exchanged(back[d], "tile", d) for d in range(1, strips)]
    else:
        got = lax.all_to_all(
            back[0].reshape(strips, count, feat), "tile", split_axis=0, concat_axis=0, tiled=True
        )
        backs = [jnp.sum(got.astype(jnp.float32), axis=0).astype(kernels.dtype)]

    late = [exchanged(x, "inst", 1) for x in shards]

    normed, total = pl.pallas_call(
        functools.partial(update_kernel, len(backs), len(shards)),
        out_shape=[
            jax.ShapeDtypeStruct((count, feat), kernels.dtype),
            jax.ShapeDtypeStruct((count, feat), jnp.float32),
        ],
        in_specs=[any_] * len(backs) + [hbm] * 2 + [any_] * len(shards),
        out_specs=[any_] * 2,
        scratch_shapes=[
            pltpu.VMEM((count, feat), kernels.dtype),
            pltpu.VMEM((1, feat), gain.dtype),
            pltpu.SemaphoreType.DMA((2,)),
        ],
        compiler_params=pltpu.CompilerParams(vmem_limit_bytes=48 << 20),
        cost_estimate=pl.CostEstimate(
            flops=40 * slots * features.size, bytes_accessed=2 * features.size, transcendentals=0
        ),
        name="update",
    )(*backs, kernels, gain.reshape(1, feat), *shards)
    return pl.pallas_call(
        finish_kernel,
        out_shape=jax.ShapeDtypeStruct((count, feat), kernels.dtype),
        in_specs=[any_] * (2 + len(late)),
        out_specs=any_,
        compiler_params=pltpu.CompilerParams(vmem_limit_bytes=48 << 20),
        name="finish",
    )(normed, total, *late)


def solution(mesh):
    return jax.shard_map(
        local,
        mesh=mesh,
        in_specs=(
            P(("groups", "tile"), None, None),
            P(("groups", "tile", "inst"), None),
            P(("groups", "tile", "inst"), None),
            P(("groups", "tile", "inst"), None),
            P(),
            P(None, "inst"),
            P("inst", None),
        ),
        out_specs=P(("groups", "tile", "inst"), None),
        check_vma=False,
    )
```

time: 51.8 us -> 28.9 us (0.56)
  waiting for transfers between devices: 21.9 us -> 6 us
  local copies, waits for them, and re-layouts: 6.74 us -> 0.01 us
  Pallas kernels: 7.6 us -> 10.3 us
  starting transfers between devices: 14.6 us -> 12.3 us
  other arithmetic: 0.62 us -> 0 us
    ppermute x12 -> x9, waiting for transfers between devices: 21.9 us -> 6 us  [exchanged(): lax.ppermute(x, axis, [(i, i ^ distance) for i in range(lax.axis_size(axi...]
    unnamed x10 -> x4, local copies, waits for them, and re-layouts: 6.74 us -> 0.01 us
    pallas_call x2 -> x4, Pallas kernels: 7.6 us -> 10.3 us  [the longest x1 6.8 us: local(): pl.pallas_call(functools.partial(pool_kernel, len(blocks), slots, count),...]
    ppermute x12 -> x9, starting transfers between devices: 14.6 us -> 12.3 us  [exchanged(): lax.ppermute(x, axis, [(i, i ^ distance) for i in range(lax.axis_size(axi...]
    add x1 -> x0, other arithmetic: 0.62 us -> none  [local(): mine = mine + shifted(back[s], 'tile', strips - s)]
  transfers between devices with their start and end apart: 12 -> 9, of which waited for: 10 -> 3; matrix products, arithmetic and copies ran while one was open for 0% -> 0% of each run, Pallas kernels for 3% -> 26%
where the time goes in v2:
time: 28.9 us; the launch traced here: 28.7 us
  starting transfers between devices  12.3 us (43%)
  Pallas kernels  10.3 us (36%)
  waiting for transfers between devices  6 us (21%)
    ppermute x9, starting transfers between devices, exchanged(): lax.ppermute(x, axis, [(i, i ^ distance) for i in range(lax.axis_size(axi...  12.3 us
    pallas_call x1, Pallas kernels, local(): pl.pallas_call(functools.partial(pool_kernel, len(blocks), slots, count),...  6.8 us
    ppermute x9, waiting for transfers between devices, exchanged(): lax.ppermute(x, axis, [(i, i ^ distance) for i in range(lax.axis_size(axi...  6 us
    pallas_call x1, Pallas kernels, local(): pl.pallas_call(pack_kernel, out_shape=[pltpu.VMEM((count + META, feat), k...  1.85 us
    pallas_call x1, Pallas kernels, local(): pl.pallas_call(finish_kernel, out_shape=jax.ShapeDtypeStruct((count, feat...  1.02 us
    pallas_call x1, Pallas kernels, local(): pl.pallas_call(functools.partial(update_kernel, len(backs), len(shards)),...  0.64 us
  transfers between devices with their start and end apart: 9, of which 3 were waited for; matrix products, arithmetic and copies ran while one was open for 0% of the time, Pallas kernels for 26%

profile of v2, /device:TPU:0, one launch (start us, length us, event | category | flops | bytes accessed | tf_op | source)
XLA Modules:
  0.0 28.7 jit_solution(5313981302756527928)
XLA Ops:
  0.0 1.8 %pack.1 = (bf16[80,256]{1,0:T(8,128)(2,1)S(1)}, bf16[1024,256]{1,0:T(8,128)(2,1)S(1)}) custom-call(bf16[64,256]{1,0:T(8,128)(2,1)} %refs_4_.3, s32[1,64]{1,0:T(1,128)} %bitcast.5, s32[4,64]{1,0:T(4,128)} %bitcast.4, bf16[256,512]{1,0:T(8,128)(2,1)} %w_in_hbm.1, bf16[512,256]{1,0:T(8,128)(2,1)} %w_out_hbm.1), custom_call_target="tpu_custom_call" | custom-call | tf_op jit(solution)/shard_map/pack/pallas_call | solution.py:193
  1.9 3.1 %collective-permute-start = (bf16[80,256]{1,0:T(8,128)(2,1)S(1)}, bf16[80,256]{1,0:T(8,128)(2,1)S(1)}, u32[]{:S(2)}, u32[]{:S(2)}) collective-permute-start(bf16[80,256]{1,0:T(8,128)(2,1)S(1)} %get-tuple-element.13.refs_0_), channel_id=1, source_target_pairs={{0,4},{4,0},{8,12},{12,8},{1,5},{5,1},{9,13},{13,9},{2,6},{6,2},{1... | collective-permute-start | bytes 122888 | tf_op jit(solution)/shard_map/ppermute | solution.py:183
  4.9 2.6 %collective-permute-start.1 = (bf16[80,256]{1,0:T(8,128)(2,1)S(1)}, bf16[80,256]{1,0:T(8,128)(2,1)S(1)}, u32[]{:S(2)}, u32[]{:S(2)}) collective-permute-start(bf16[80,256]{1,0:T(8,128)(2,1)S(1)} %get-tuple-element.13.refs_0_), channel_id=1, source_target_pairs={{0,8},{4,12},{8,0},{12,4},{1,9},{5,13},{9,1},{13,5},{2,10},{6,14},... | collective-permute-start | bytes 122888 | tf_op jit(solution)/shard_map/ppermute | solution.py:183
  7.5 0.0 collective-permute-start.2
  7.5 0.0 copy-start
  7.5 0.0 copy-start.1
  7.5 1.7 %collective-permute-start.6 = (bf16[1024,256]{1,0:T(8,128)(2,1)S(1)}, bf16[1024,256]{1,0:T(8,128)(2,1)S(1)}, u32[]{:S(2)}, u32[]{:S(2)}) collective-permute-start(bf16[1024,256]{1,0:T(8,128)(2,1)S(1)} %get-tuple-element.18.refs_6_), channel_id=1, source_target_pairs={{0,2},{1,3},{2,0},{3,1},{4,6},{5,7},{6,4},{7,5},{8,10},{9,11},{10,... | collective-permute-start | bytes 1572872 | tf_op jit(solution)/shard_map/ppermute | solution.py:183
  9.3 0.0 collective-permute-done.refs_1_
  9.3 1.3 %collective-permute-done.1.refs_2_ = bf16[80,256]{1,0:T(8,128)(2,1)S(1)} collective-permute-done((bf16[80,256]{1,0:T(8,128)(2,1)S(1)}, bf16[80,256]{1,0:T(8,128)(2,1)S(1)}, u32[]{:S(2)}, u32[]{:S(2)}) %collective-permute-start.1) | collective-permute-done | bytes 40992 | tf_op jit(solution)/shard_map/ppermute | solution.py:183
  10.6 2.7 %collective-permute-done.2.refs_3_ = bf16[80,256]{1,0:T(8,128)(2,1)S(1)} collective-permute-done((bf16[80,256]{1,0:T(8,128)(2,1)S(1)}, bf16[80,256]{1,0:T(8,128)(2,1)S(1)}, u32[]{:S(2)}, u32[]{:S(2)}) %collective-permute-start.2) | collective-permute-done | bytes 40992 | tf_op jit(solution)/shard_map/ppermute | solution.py:183
  13.3 6.8 %pool.1 = (bf16[64,256]{1,0:T(8,128)(2,1)S(1)}, bf16[64,256]{1,0:T(8,128)(2,1)S(1)}, bf16[64,256]{1,0:T(8,128)(2,1)S(1)}, bf16[64,256]{1,0:T(8,128)(2,1)S(1)}) custom-call(bf16[80,256]{1,0:T(8,128)(2,1)S(1)} %get-tuple-element.13.refs_0_, bf16[80,256]{1,0:T(8,128)(2,1)S(1)} %collective-permute-done.refs_1_, ...), custom_call_target="tpu_custom_call" | custom-call | flops 26843545600 | bytes 8388608 | tf_op jit(solution)/shard_map/pool/pallas_call | solution.py:217
  20.1 0.1 collective-permute-start.3
  20.2 1.1 %collective-permute-start.4 = (bf16[64,256]{1,0:T(8,128)(2,1)S(1)}, bf16[64,256]{1,0:T(8,128)(2,1)S(1)}, u32[]{:S(2)}, u32[]{:S(2)}) collective-permute-start(bf16[64,256]{1,0:T(8,128)(2,1)S(1)} %get-tuple-element.16), channel_id=1, source_target_pairs={{0,8},{4,12},{8,0},{12,4},{1,9},{5,13},{9,1},{13,5},{2,10},{6,14},... | collective-permute-start | bytes 98312 | tf_op jit(solution)/shard_map/ppermute | solution.py:183
  21.3 3.3 %collective-permute-start.5 = (bf16[64,256]{1,0:T(8,128)(2,1)S(1)}, bf16[64,256]{1,0:T(8,128)(2,1)S(1)}, u32[]{:S(2)}, u32[]{:S(2)}) collective-permute-start(bf16[64,256]{1,0:T(8,128)(2,1)S(1)} %get-tuple-element.17), channel_id=1, source_target_pairs={{0,12},{4,8},{8,4},{12,0},{1,13},{5,9},{9,5},{13,1},{2,14},{6,10},... | collective-permute-start | bytes 98312 | tf_op jit(solution)/shard_map/ppermute | solution.py:183
  24.6 0.0 collective-permute-start.7
  24.6 0.0 collective-permute-done.6.refs_7_
  24.6 0.5 %collective-permute-start.8 = (bf16[1024,256]{1,0:T(8,128)(2,1)S(1)}, bf16[1024,256]{1,0:T(8,128)(2,1)S(1)}, u32[]{:S(2)}, u32[]{:S(2)}) collective-permute-start(bf16[1024,256]{1,0:T(8,128)(2,1)S(1)} %collective-permute-done.6.refs_7_), channel_id=1, source_target_pairs={{0,1},{1,0},{2,3},{3,2},{4,5},{5,4},{6,7},{7,6},{8,9},{9,8},{10,11... | collective-permute-start | bytes 1572872 | tf_op jit(solution)/shard_map/ppermute | solution.py:183
  25.1 0.0 collective-permute-done.3.refs_1_
  25.1 0.0 collective-permute-done.4.refs_2_
  25.1 1.9 %collective-permute-done.5.refs_3_ = bf16[64,256]{1,0:T(8,128)(2,1)S(1)} collective-permute-done((bf16[64,256]{1,0:T(8,128)(2,1)S(1)}, bf16[64,256]{1,0:T(8,128)(2,1)S(1)}, u32[]{:S(2)}, u32[]{:S(2)}) %collective-permute-start.5) | collective-permute-done | bytes 32800 | tf_op jit(solution)/shard_map/ppermute | solution.py:183
  27.0 0.0 copy-done
  27.0 0.0 copy-done.1
  27.0 0.6 %update.1 = (bf16[64,256]{1,0:T(8,128)(2,1)S(1)}, f32[64,256]{1,0:T(8,128)S(1)}) custom-call(bf16[64,256]{1,0:T(8,128)(2,1)S(1)} %get-tuple-element.14.refs_0_, bf16[64,256]{1,0:T(8,128)(2,1)S(1)} %collective-permute-done.3.refs_1_, bf16[64,256]{1,0:T(8,128)(2,1)S(1)} %collective-permute-done.4.refs_2_, bf16[64,256]{1,0:T(8,128)(2,1)S(1)} %collective-permute-done.5.refs_3_, ...), custom_call_target="tpu_custom_call" | custom-call | flops 26843545600 | bytes 8388608 | tf_op jit(solution)/shard_map/update/pallas_call | solution.py:242
  27.7 0.0 collective-permute-done.7.refs_0_
  27.7 0.0 collective-permute-done.8.refs_1_
  27.7 1.0 %finish.1 = bf16[64,256]{1,0:T(8,128)(2,1)} custom-call(bf16[64,256]{1,0:T(8,128)(2,1)S(1)} %get-tuple-element.19.normed_ref, f32[64,256]{1,0:T(8,128)S(1)} %get-tuple-element.20.total_ref, bf16[1024,256]{1,0:T(8,128)(2,1)S(1)} %collective-permute-done.7.refs_0_, bf16[1024,256]{1,0:T(8,128)(2,1)S(1)} %collective-permute-done.8.refs_1_), custom_call_target="tpu_custom_call" | custom-call | tf_op jit(solution)/shard_map/finish/pallas_call | solution.py:261
Async XLA Ops:
  1.9 7.4 %collective-permute-start = (bf16[80,256]{1,0:T(8,128)(2,1)S(1)}, bf16[80,256]{1,0:T(8,128)(2,1)S(1)}, u32[]{:S(2)}, u32[]{:S(2)}) collective-permute-start(bf16[80,256]{1,0:T(8,128)(2,1)S(1)} %get-tuple-element.13.refs_0_), channel_id=1, source_target_pairs={{0,4},{4,0},{8,12},{12,8},{1,5},{5,1},{9,13},{13,9},{2,6},{6,2},{1... | collective-permute-start | bytes 122888 | tf_op jit(solution)/shard_map/ppermute | solution.py:183
  4.9 5.7 %collective-permute-start.1 = (bf16[80,256]{1,0:T(8,128)(2,1)S(1)}, bf16[80,256]{1,0:T(8,128)(2,1)S(1)}, u32[]{:S(2)}, u32[]{:S(2)}) collective-permute-start(bf16[80,256]{1,0:T(8,128)(2,1)S(1)} %get-tuple-element.13.refs_0_), channel_id=1, source_target_pairs={{0,8},{4,12},{8,0},{12,4},{1,9},{5,13},{9,1},{13,5},{2,10},{6,14},... | collective-permute-start | bytes 122888 | tf_op jit(solution)/shard_map/ppermute | solution.py:183
  7.5 5.8 %collective-permute-start.2 = (bf16[80,256]{1,0:T(8,128)(2,1)S(1)}, bf16[80,256]{1,0:T(8,128)(2,1)S(1)}, u32[]{:S(2)}, u32[]{:S(2)}) collective-permute-start(bf16[80,256]{1,0:T(8,128)(2,1)S(1)} %get-tuple-element.13.refs_0_), channel_id=1, source_target_pairs={{0,12},{4,8},{8,4},{12,0},{1,13},{5,9},{9,5},{13,1},{2,14},{6,10},... | collective-permute-start | bytes 122888 | tf_op jit(solution)/shard_map/ppermute | solution.py:183
  7.5 19.5 %copy-start = (bf16[64,256]{1,0:T(8,128)(2,1)S(1)}, bf16[64,256]{1,0:T(8,128)(2,1)}, u32[]{:S(2)}) copy-start(bf16[64,256]{1,0:T(8,128)(2,1)} %refs_4_.3) | copy-start | bytes 98308
  7.5 19.5 %copy-start.1 = (f32[256]{0:T(256)S(1)}, f32[256]{0:T(256)}, u32[]{:S(2)}) copy-start(f32[256]{0:T(256)} %param.11) | copy-start | bytes 3076
  7.5 17.1 %collective-permute-start.6 = (bf16[1024,256]{1,0:T(8,128)(2,1)S(1)}, bf16[1024,256]{1,0:T(8,128)(2,1)S(1)}, u32[]{:S(2)}, u32[]{:S(2)}) collective-permute-start(bf16[1024,256]{1,0:T(8,128)(2,1)S(1)} %get-tuple-element.18.refs_6_), channel_id=1, source_target_pairs={{0,2},{1,3},{2,0},{3,1},{4,6},{5,7},{6,4},{7,5},{8,10},{9,11},{10,... | collective-permute-start | bytes 1572872 | tf_op jit(solution)/shard_map/ppermute | solution.py:183
  20.1 5.0 %collective-permute-start.3 = (bf16[64,256]{1,0:T(8,128)(2,1)S(1)}, bf16[64,256]{1,0:T(8,128)(2,1)S(1)}, u32[]{:S(2)}, u32[]{:S(2)}) collective-permute-start(bf16[64,256]{1,0:T(8,128)(2,1)S(1)} %get-tuple-element.15), channel_id=1, source_target_pairs={{0,4},{4,0},{8,12},{12,8},{1,5},{5,1},{9,13},{13,9},{2,6},{6,2},{1... | collective-permute-start | bytes 98312 | tf_op jit(solution)/shard_map/ppermute | solution.py:183
  20.2 4.9 %collective-permute-start.4 = (bf16[64,256]{1,0:T(8,128)(2,1)S(1)}, bf16[64,256]{1,0:T(8,128)(2,1)S(1)}, u32[]{:S(2)}, u32[]{:S(2)}) collective-permute-start(bf16[64,256]{1,0:T(8,128)(2,1)S(1)} %get-tuple-element.16), channel_id=1, source_target_pairs={{0,8},{4,12},{8,0},{12,4},{1,9},{5,13},{9,1},{13,5},{2,10},{6,14},... | collective-permute-start | bytes 98312 | tf_op jit(solution)/shard_map/ppermute | solution.py:183
  21.3 5.7 %collective-permute-start.5 = (bf16[64,256]{1,0:T(8,128)(2,1)S(1)}, bf16[64,256]{1,0:T(8,128)(2,1)S(1)}, u32[]{:S(2)}, u32[]{:S(2)}) collective-permute-start(bf16[64,256]{1,0:T(8,128)(2,1)S(1)} %get-tuple-element.17), channel_id=1, source_target_pairs={{0,12},{4,8},{8,4},{12,0},{1,13},{5,9},{9,5},{13,1},{2,14},{6,10},... | collective-permute-start | bytes 98312 | tf_op jit(solution)/shard_map/ppermute | solution.py:183
  24.6 3.1 %collective-permute-start.7 = (bf16[1024,256]{1,0:T(8,128)(2,1)S(1)}, bf16[1024,256]{1,0:T(8,128)(2,1)S(1)}, u32[]{:S(2)}, u32[]{:S(2)}) collective-permute-start(bf16[1024,256]{1,0:T(8,128)(2,1)S(1)} %get-tuple-element.18.refs_6_), channel_id=1, source_target_pairs={{0,1},{1,0},{2,3},{3,2},{4,5},{5,4},{6,7},{7,6},{8,9},{9,8},{10,11... | collective-permute-start | bytes 1572872 | tf_op jit(solution)/shard_map/ppermute | solution.py:183
  24.6 3.1 %collective-permute-start.8 = (bf16[1024,256]{1,0:T(8,128)(2,1)S(1)}, bf16[1024,256]{1,0:T(8,128)(2,1)S(1)}, u32[]{:S(2)}, u32[]{:S(2)}) collective-permute-start(bf16[1024,256]{1,0:T(8,128)(2,1)S(1)} %collective-permute-done.6.refs_7_), channel_id=1, source_target_pairs={{0,1},{1,0},{2,3},{3,2},{4,5},{5,4},{6,7},{7,6},{8,9},{9,8},{10,11... | collective-permute-start | bytes 1572872 | tf_op jit(solution)/shard_map/ppermute | solution.py:183

commit v3 on v2

v3 whole, which is shorter than its diff:
```python
import functools

import jax
import jax.numpy as jnp
from jax import lax
from jax.experimental import pallas as pl
from jax.experimental.pallas import tpu as pltpu
from jax.sharding import PartitionSpec as P

TS = 32
SR = 2
WC = 8
META = 8
ROWS_PER_STEP = 4
ARRIVALS = (16, 16, 32)
VMEM = pltpu.VMEM


def start_all(copies):
    for copy in copies:
        copy.start()
    return copies


def pack_kernel(near, groups, room, *refs):
    home_hbm, boxes_hbm, kernels_hbm, w_out_hbm, w_in_hbm, block_refs = *refs[:5], refs[5:-6]
    pick_ref, shard_ref, home_ref, boxes_ref, kernels_ref, sems = refs[-6:]
    bf16, f32 = jnp.bfloat16, jnp.float32
    count, feat = kernels_ref.shape
    hidden = w_out_hbm.shape[0]
    pairs = [(home_hbm, home_ref), (boxes_hbm, boxes_ref), (kernels_hbm, kernels_ref)]
    pairs.append((w_out_hbm, shard_ref.at[pl.ds(0, hidden)]))
    for i in range(hidden // feat):
        part = shard_ref.at[pl.ds(hidden + i * feat, feat)]
        pairs.append((w_in_hbm.at[:, pl.ds(i * feat, feat)], part))
    copies = start_all(
        [pltpu.make_async_copy(a, b, sems.at[i]) for i, (a, b) in enumerate(pairs)]
    )

    earlier = (
        lax.broadcasted_iota(jnp.int32, (count, count), 0)
        < lax.broadcasted_iota(jnp.int32, (count, count), 1)
    ).astype(bf16)
    rows = -(-groups // 8) * 8
    line = lax.broadcasted_iota(jnp.int32, (rows, count), 0)
    slot = lax.broadcasted_iota(jnp.int32, (groups * room, count), 0)
    copies[0].wait()
    group = home_ref[...]
    if near:
        group = group ^ lax.axis_index("tile")
    member = jnp.where(group == line, 1.0, 0.0)
    rank = jnp.dot(member.astype(bf16), earlier, preferred_element_type=f32)
    rank = jnp.sum(rank * member, axis=0, keepdims=True).astype(jnp.int32)
    select = jnp.where(group * room + rank == slot, 1.0, 0.0)
    select16 = select.astype(bf16)
    pick_ref[...] = select.T.astype(bf16)
    copies[1].wait()
    bounds = jnp.concatenate(
        [boxes_ref[...], jnp.zeros((META - boxes_ref.shape[0], count), jnp.int32)], axis=0
    )
    bounds = lax.dot_general(
        bounds.astype(f32).astype(bf16),
        select16,
        (((1,), (1,)), ((), ())),
        preferred_element_type=f32,
    )
    copies[2].wait()
    placed = jnp.dot(select16, kernels_ref[...], preferred_element_type=f32)
    stride = block_refs[0].shape[0] * len(block_refs) // groups
    for g in range(groups):
        ref, at = (block_refs[g], 0) if len(block_refs) > 1 else (block_refs[0], g * stride)
        part = slice(g * room, (g + 1) * room)
        ref[at : at + stride, :] = jnp.concatenate(
            [
                placed[part],
                jnp.concatenate([bounds[:, part], jnp.zeros((META, feat - room), f32)], axis=1),
            ]
            + [jnp.zeros((stride - room - META, feat), f32)] * (stride > room + META),
            axis=0,
        ).astype(bf16)
    for copy in copies[3:]:
        copy.wait()


def pool_kernel(blocks, groups, room, *refs):
    block_refs, features_hbm, refs = refs[:blocks], refs[blocks], refs[blocks + 1 :]
    out_refs, (features_ref, sems) = refs[:-2], refs[-2:]
    bf16, f32 = jnp.bfloat16, jnp.float32
    slots, feat = groups * room, features_ref.shape[2]
    steps = features_ref.shape[0] // ROWS_PER_STEP
    copies, at = {}, 0
    for i, size in enumerate(ARRIVALS):
        part = pl.ds(at, size)
        copies[at // ROWS_PER_STEP] = pltpu.make_async_copy(
            features_hbm.at[part], features_ref.at[part], sems.at[i]
        )
        copies[at // ROWS_PER_STEP].start()
        at += size

    stride = block_refs[0].shape[0] * blocks // groups
    unit = jnp.where(
        lax.broadcasted_iota(jnp.int32, (room, room), 0)
        == lax.broadcasted_iota(jnp.int32, (room, room), 1),
        1.0,
        0.0,
    ).astype(bf16)
    rows, bounds = [], []
    for g in range(groups):
        block = block_refs[g][...] if blocks > 1 else block_refs[0][g * stride : (g + 1) * stride, :]
        rows.append(block[:room].astype(f32))
        bounds.append(
            lax.dot_general(
                unit,
                block[room : room + META, :room],
                (((1,), (1,)), ((), ())),
                preferred_element_type=f32,
            )
        )
    rows16 = jnp.concatenate(rows, axis=0).astype(bf16)
    bounds = jnp.concatenate(bounds, axis=0)

    width = WC * TS
    tile_col = (lax.broadcasted_iota(jnp.int32, (slots, width), 1) // TS).astype(f32)
    column = (bounds[:, 2:3] <= tile_col) & (tile_col <= bounds[:, 3:4])
    inside = [
        jnp.where(column & (bounds[:, 0:1] <= r) & (r <= bounds[:, 1:2]), 1.0, 0.0)
        for r in range(SR)
    ]

    def cells(step):
        return features_ref[step * ROWS_PER_STEP : (step + 1) * ROWS_PER_STEP].reshape(
            ROWS_PER_STEP * width, feat
        )

    def logits(step):
        if step in copies:
            copies[step].wait()
        return lax.dot_general(
            rows16, cells(step), (((1,), (1,)), ((), ())), preferred_element_type=f32
        )

    pooled = jnp.zeros((slots, feat), f32)
    covered = jnp.zeros((slots, width), f32)
    now = logits(0)
    for step in range(steps):
        later = logits(step + 1) if step + 1 < steps else None
        mask = inside[step * ROWS_PER_STEP // TS]
        parts = []
        for j in range(ROWS_PER_STEP):
            part = mask * pl.reciprocal(
                1.0 + jnp.exp(-now[:, j * width : (j + 1) * width]), approx=True
            )
            covered = covered + part
            parts.append(part.astype(bf16))
        pooled = pooled + jnp.dot(
            jnp.concatenate(parts, axis=1), cells(step), preferred_element_type=f32
        )
        now = later
    area = jnp.sum(covered, axis=1, keepdims=True)
    ratio = (pooled / area).astype(bf16).astype(f32)

    for g in range(groups):
        part = ratio[g * room : (g + 1) * room]
        if len(out_refs) > 1:
            out_refs[g][...] = part.astype(bf16)
        else:
            out_refs[0][g * room : (g + 1) * room, :] = part.astype(bf16)


def through(normed, total, shard_refs):
    feat = total.shape[1]
    for ref in shard_refs:
        width = ref.shape[0] // 2
        for i in range(0, width, feat):
            hidden = jnp.dot(
                normed, ref[width + i : width + i + feat, :], preferred_element_type=jnp.float32
            )
            total = total + jnp.dot(
                jnp.maximum(hidden, 0.0).astype(normed.dtype),
                ref[i : i + feat, :],
                preferred_element_type=jnp.float32,
            )
    return total


def update_kernel(backs, shards, *refs):
    back_refs, pick_ref, refs = refs[:backs], refs[backs], refs[backs + 1 :]
    own_hbm, shard_refs, refs = refs[:2], refs[2 : 2 + shards], refs[2 + shards :]
    normed_ref, total_ref, kernels_ref, gain_ref, sems = refs
    own = (kernels_ref, gain_ref)
    f32 = jnp.float32
    copies = start_all(
        [pltpu.make_async_copy(a, b, sems.at[i]) for i, (a, b) in enumerate(zip(own_hbm, own))]
    )
    back = jnp.concatenate([ref[...].astype(f32) for ref in back_refs], axis=0)
    ratio = jnp.dot(pick_ref[...], back.astype(pick_ref.dtype), preferred_element_type=f32)
    copies[0].wait()
    merged = kernels_ref[...].astype(f32) + ratio
    centred = merged - jnp.mean(merged, axis=1, keepdims=True)
    spread = jnp.mean(centred * centred, axis=1, keepdims=True)
    copies[1].wait()
    normed = (centred * lax.rsqrt(spread + 1e-05) * gain_ref[...]).astype(normed_ref.dtype)
    normed_ref[...] = normed
    total_ref[...] = through(normed, merged, shard_refs)


def finish_kernel(normed_ref, total_ref, *refs):
    out_ref = refs[-1]
    out_ref[...] = through(normed_ref[...], total_ref[...], refs[:-1]).astype(out_ref.dtype)


def exchanged(x, axis, distance):
    return lax.ppermute(x, axis, [(i, i ^ distance) for i in range(lax.axis_size(axis))])


def local(features, kernels, home, boxes, gain, w_in, w_out):
    strips, holders = lax.axis_size("tile"), lax.axis_size("inst")
    count, feat = kernels.shape
    hidden = w_out.shape[0]
    most = min(count, max(2, 5 * count // (2 * strips)))
    room = -(-most // 8) * 8
    stride = -(-(room + META) // 16) * 16
    slots = strips * room
    near = strips & (strips - 1) == 0 and strips <= 8
    any_, hbm = pl.BlockSpec(memory_space=VMEM), pl.BlockSpec(memory_space=pltpu.HBM)

    parts = strips if near else 1
    *blocks, pick, shard = pl.pallas_call(
        functools.partial(pack_kernel, near, strips, room),
        out_shape=[pltpu.VMEM((strips // parts * stride, feat), kernels.dtype)] * parts
        + [
            pltpu.VMEM((count, slots), kernels.dtype),
            pltpu.VMEM((2 * hidden, feat), w_out.dtype),
        ],
        in_specs=[hbm] * 5,
        out_specs=[any_] * (parts + 2),
        scratch_shapes=[
            pltpu.VMEM((1, count), home.dtype),
            pltpu.VMEM((boxes.shape[1], count), boxes.dtype),
            pltpu.VMEM((count, feat), kernels.dtype),
            pltpu.SemaphoreType.DMA((4 + hidden // feat,)),
        ],
        name="pack",
    )(home.T, boxes.T, kernels, w_out, w_in)
    if near:
        blocks = [blocks[0]] + [exchanged(blocks[d], "tile", d) for d in range(1, strips)]
        outs = [jax.ShapeDtypeStruct((room, feat), kernels.dtype)] * strips
    else:
        got = lax.all_to_all(
            blocks[0].reshape(strips, stride, feat), "tile", split_axis=0, concat_axis=0, tiled=True
        )
        blocks = [got.reshape(strips * stride, feat)]
        outs = [jax.ShapeDtypeStruct((slots, feat), kernels.dtype)]

    shards = [shard]
    distance = holders // 2
    while distance > 1:
        shards += [exchanged(x, "inst", distance) for x in shards]
        distance //= 2

    back = pl.pallas_call(
        functools.partial(pool_kernel, len(blocks), strips, room),
        out_shape=outs,
        in_specs=[any_] * len(blocks) + [hbm],
        out_specs=[any_] * len(outs),
        scratch_shapes=[
            pltpu.VMEM(features.shape, features.dtype),
            pltpu.SemaphoreType.DMA((len(ARRIVALS),)),
        ],
        compiler_params=pltpu.CompilerParams(vmem_limit_bytes=48 << 20),
        cost_estimate=pl.CostEstimate(
            flops=40 * slots * features.size, bytes_accessed=2 * features.size, transcendentals=0
        ),
        name="pool",
    )(*blocks, features)
    if near:
        backs = [back[0]] + [exchanged(back[d], "tile", d) for d in range(1, strips)]
    else:
        got = lax.all_to_all(
            back[0].reshape(strips, room, feat), "tile", split_axis=0, concat_axis=0, tiled=True
        )
        backs = [got.reshape(slots, feat)]
    late = [exchanged(x, "inst", 1) for x in shards]

    normed, total = pl.pallas_call(
        functools.partial(update_kernel, len(backs), len(shards)),
        out_shape=[
            jax.ShapeDtypeStruct((count, feat), kernels.dtype),
            jax.ShapeDtypeStruct((count, feat), jnp.float32),
        ],
        in_specs=[any_] * (len(backs) + 1) + [hbm] * 2 + [any_] * len(shards),
        out_specs=[any_] * 2,
        scratch_shapes=[
            pltpu.VMEM((count, feat), kernels.dtype),
            pltpu.VMEM((1, feat), gain.dtype),
            pltpu.SemaphoreType.DMA((2,)),
        ],
        compiler_params=pltpu.CompilerParams(vmem_limit_bytes=48 << 20),
        cost_estimate=pl.CostEstimate(
            flops=40 * slots * features.size, bytes_accessed=2 * features.size, transcendentals=0
        ),
        name="update",
    )(*backs, pick, kernels, gain.reshape(1, feat), *shards)
    return pl.pallas_call(
        finish_kernel,
        out_shape=jax.ShapeDtypeStruct((count, feat), kernels.dtype),
        in_specs=[any_] * (2 + len(late)),
        out_specs=any_,
        compiler_params=pltpu.CompilerParams(vmem_limit_bytes=48 << 20),
        name="finish",
    )(normed, total, *late)


def solution(mesh):
    return jax.shard_map(
        local,
        mesh=mesh,
        in_specs=(
            P(("groups", "tile"), None, None),
            P(("groups", "tile", "inst"), None),
            P(("groups", "tile", "inst"), None),
            P(("groups", "tile", "inst"), None),
            P(),
            P(None, "inst"),
            P("inst", None),
        ),
        out_specs=P(("groups", "tile", "inst"), None),
        check_vma=False,
    )
```

time: 28.9 us -> 27.2 us (0.941)
  Pallas kernels: 10.3 us -> 9.23 us
  waiting for transfers between devices: 6 us -> 5.42 us
    pallas_call x2, Pallas kernels: 8.65 us -> 7.44 us  [the longest x1 6.18 us: local(): pl.pallas_call(functools.partial(pool_kernel, len(blocks), strips, room),...]
    ppermute x9, waiting for transfers between devices: 6 us -> 5.42 us  [exchanged(): lax.ppermute(x, axis, [(i, i ^ distance) for i in range(lax.axis_size(axi...]
where the time goes in v3:
time: 27.2 us; the launch traced here: 27.1 us
  starting transfers between devices  12.3 us (45%)
  Pallas kernels  9.23 us (34%)
  waiting for transfers between devices  5.42 us (20%)
    ppermute x9, starting transfers between devices, exchanged(): lax.ppermute(x, axis, [(i, i ^ distance) for i in range(lax.axis_size(axi...  12.3 us
    pallas_call x1, Pallas kernels, local(): pl.pallas_call(functools.partial(pool_kernel, len(blocks), strips, room),...  6.18 us
    ppermute x9, waiting for transfers between devices, exchanged(): lax.ppermute(x, axis, [(i, i ^ distance) for i in range(lax.axis_size(axi...  5.42 us
    pallas_call x1, Pallas kernels, local(): pl.pallas_call(functools.partial(pack_kernel, near, strips, room), out_sh...  1.26 us
    pallas_call x1, Pallas kernels, local(): pl.pallas_call(finish_kernel, out_shape=jax.ShapeDtypeStruct((count, feat...  1.02 us
    pallas_call x1, Pallas kernels, local(): pl.pallas_call(functools.partial(update_kernel, len(backs), len(shards)),...  0.77 us
  transfers between devices with their start and end apart: 9, of which 3 were waited for; matrix products, arithmetic and copies ran while one was open for 0% of the time, Pallas kernels for 26%

profile of v3, /device:TPU:0, one launch (start us, length us, event | category | flops | bytes accessed | tf_op | source)
XLA Modules:
  0.0 27.1 jit_solution(14377298023349860206)
XLA Ops:
  0.0 1.3 %pack.1 = (bf16[48,256]{1,0:T(8,128)(2,1)S(1)}, bf16[48,256]{1,0:T(8,128)(2,1)S(1)}, bf16[48,256]{1,0:T(8,128)(2,1)S(1)}, bf16[48,256]{1,0:T(8,128)(2,1)S(1)}, b...) custom-call(s32[1,64]{1,0:T(1,128)} %bitcast.5, s32[4,64]{1,0:T(4,128)} %bitcast.4, bf16[64,256]{1,0:T(8,128)(2,1)} %refs_5_.1, ...), custom_call_target="tpu_custom_call" | custom-call | tf_op jit(solution)/shard_map/pack/pallas_call | solution.py:228
  1.3 3.1 %collective-permute-start = (bf16[48,256]{1,0:T(8,128)(2,1)S(1)}, bf16[48,256]{1,0:T(8,128)(2,1)S(1)}, u32[]{:S(2)}, u32[]{:S(2)}) collective-permute-start(bf16[48,256]{1,0:T(8,128)(2,1)S(1)} %get-tuple-element.18), channel_id=1, source_target_pairs={{0,4},{4,0},{8,12},{12,8},{1,5},{5,1},{9,13},{13,9},{2,6},{6,2},{1... | collective-permute-start | bytes 73736 | tf_op jit(solution)/shard_map/ppermute | solution.py:213
  4.4 2.6 %collective-permute-start.1 = (bf16[48,256]{1,0:T(8,128)(2,1)S(1)}, bf16[48,256]{1,0:T(8,128)(2,1)S(1)}, u32[]{:S(2)}, u32[]{:S(2)}) collective-permute-start(bf16[48,256]{1,0:T(8,128)(2,1)S(1)} %get-tuple-element.19), channel_id=1, source_target_pairs={{0,8},{4,12},{8,0},{12,4},{1,9},{5,13},{9,1},{13,5},{2,10},{6,14},... | collective-permute-start | bytes 73736 | tf_op jit(solution)/shard_map/ppermute | solution.py:213
  6.9 0.0 collective-permute-start.2
  6.9 1.7 %collective-permute-start.6 = (bf16[1024,256]{1,0:T(8,128)(2,1)S(1)}, bf16[1024,256]{1,0:T(8,128)(2,1)S(1)}, u32[]{:S(2)}, u32[]{:S(2)}) collective-permute-start(bf16[1024,256]{1,0:T(8,128)(2,1)S(1)} %get-tuple-element.26.refs_7_), channel_id=1, source_target_pairs={{0,2},{1,3},{2,0},{3,1},{4,6},{5,7},{6,4},{7,5},{8,10},{9,11},{10,... | collective-permute-start | bytes 1572872 | tf_op jit(solution)/shard_map/ppermute | solution.py:213
  8.7 0.0 collective-permute-done.refs_1_
  8.7 0.8 %collective-permute-done.1.refs_2_ = bf16[48,256]{1,0:T(8,128)(2,1)S(1)} collective-permute-done((bf16[48,256]{1,0:T(8,128)(2,1)S(1)}, bf16[48,256]{1,0:T(8,128)(2,1)S(1)}, u32[]{:S(2)}, u32[]{:S(2)}) %collective-permute-start.1) | collective-permute-done | bytes 24608 | tf_op jit(solution)/shard_map/ppermute | solution.py:213
  9.4 3.1 %collective-permute-done.2.refs_3_ = bf16[48,256]{1,0:T(8,128)(2,1)S(1)} collective-permute-done((bf16[48,256]{1,0:T(8,128)(2,1)S(1)}, bf16[48,256]{1,0:T(8,128)(2,1)S(1)}, u32[]{:S(2)}, u32[]{:S(2)}) %collective-permute-start.2) | collective-permute-done | bytes 24608 | tf_op jit(solution)/shard_map/ppermute | solution.py:213
  12.6 0.0 copy-start
  12.6 0.0 copy-start.1
  12.6 6.2 %pool.1 = (bf16[40,256]{1,0:T(8,128)(2,1)S(1)}, bf16[40,256]{1,0:T(8,128)(2,1)S(1)}, bf16[40,256]{1,0:T(8,128)(2,1)S(1)}, bf16[40,256]{1,0:T(8,128)(2,1)S(1)}) custom-call(bf16[48,256]{1,0:T(8,128)(2,1)S(1)} %get-tuple-element.17.refs_0_, bf16[48,256]{1,0:T(8,128)(2,1)S(1)} %collective-permute-done.refs_1_, ...), custom_call_target="tpu_custom_call" | custom-call | flops 26843545600 | bytes 8388608 | tf_op jit(solution)/shard_map/pool/pallas_call | solution.py:261
  18.8 0.1 collective-permute-start.3
  18.8 0.8 %collective-permute-start.4 = (bf16[40,256]{1,0:T(8,128)(2,1)S(1)}, bf16[40,256]{1,0:T(8,128)(2,1)S(1)}, u32[]{:S(2)}, u32[]{:S(2)}) collective-permute-start(bf16[40,256]{1,0:T(8,128)(2,1)S(1)} %get-tuple-element.23), channel_id=1, source_target_pairs={{0,8},{4,12},{8,0},{12,4},{1,9},{5,13},{9,1},{13,5},{2,10},{6,14},... | collective-permute-start | bytes 61448 | tf_op jit(solution)/shard_map/ppermute | solution.py:213
  19.7 3.6 %collective-permute-start.5 = (bf16[40,256]{1,0:T(8,128)(2,1)S(1)}, bf16[40,256]{1,0:T(8,128)(2,1)S(1)}, u32[]{:S(2)}, u32[]{:S(2)}) collective-permute-start(bf16[40,256]{1,0:T(8,128)(2,1)S(1)} %get-tuple-element.24), channel_id=1, source_target_pairs={{0,12},{4,8},{8,4},{12,0},{1,13},{5,9},{9,5},{13,1},{2,14},{6,10},... | collective-permute-start | bytes 61448 | tf_op jit(solution)/shard_map/ppermute | solution.py:213
  23.2 0.0 collective-permute-start.7
  23.2 0.0 collective-permute-done.6.refs_8_
  23.2 0.5 %collective-permute-start.8 = (bf16[1024,256]{1,0:T(8,128)(2,1)S(1)}, bf16[1024,256]{1,0:T(8,128)(2,1)S(1)}, u32[]{:S(2)}, u32[]{:S(2)}) collective-permute-start(bf16[1024,256]{1,0:T(8,128)(2,1)S(1)} %collective-permute-done.6.refs_8_), channel_id=1, source_target_pairs={{0,1},{1,0},{2,3},{3,2},{4,5},{5,4},{6,7},{7,6},{8,9},{9,8},{10,11... | collective-permute-start | bytes 1572872 | tf_op jit(solution)/shard_map/ppermute | solution.py:213
  23.7 0.0 collective-permute-done.3.refs_1_
  23.7 0.0 collective-permute-done.4.refs_2_
  23.7 1.5 %collective-permute-done.5.refs_3_ = bf16[40,256]{1,0:T(8,128)(2,1)S(1)} collective-permute-done((bf16[40,256]{1,0:T(8,128)(2,1)S(1)}, bf16[40,256]{1,0:T(8,128)(2,1)S(1)}, u32[]{:S(2)}, u32[]{:S(2)}) %collective-permute-start.5) | collective-permute-done | bytes 20512 | tf_op jit(solution)/shard_map/ppermute | solution.py:213
  25.2 0.0 copy-done
  25.2 0.0 copy-done.1
  25.2 0.8 %update.1 = (bf16[64,256]{1,0:T(8,128)(2,1)S(1)}, f32[64,256]{1,0:T(8,128)S(1)}) custom-call(bf16[40,256]{1,0:T(8,128)(2,1)S(1)} %get-tuple-element.21.refs_0_, bf16[40,256]{1,0:T(8,128)(2,1)S(1)} %collective-permute-done.3.refs_1_, bf16[40,256]{1,0:T(8,128)(2,1)S(1)} %collective-permute-done.4.refs_2_, bf16[40,256]{1,0:T(8,128)(2,1)S(1)} %collective-permute-done.5.refs_3_, ...), custom_call_target="tpu_custom_call" | custom-call | flops 26843545600 | bytes 8388608 | tf_op jit(solution)/shard_map/update/pallas_call | solution.py:285
  26.0 0.0 collective-permute-done.7.refs_0_
  26.0 0.0 collective-permute-done.8.refs_1_
  26.0 1.0 %finish.1 = bf16[64,256]{1,0:T(8,128)(2,1)} custom-call(bf16[64,256]{1,0:T(8,128)(2,1)S(1)} %get-tuple-element.27.normed_ref, f32[64,256]{1,0:T(8,128)S(1)} %get-tuple-element.28.total_ref, bf16[1024,256]{1,0:T(8,128)(2,1)S(1)} %collective-permute-done.7.refs_0_, bf16[1024,256]{1,0:T(8,128)(2,1)S(1)} %collective-permute-done.8.refs_1_), custom_call_target="tpu_custom_call" | custom-call | tf_op jit(solution)/shard_map/finish/pallas_call | solution.py:304
Async XLA Ops:
  1.3 7.4 %collective-permute-start = (bf16[48,256]{1,0:T(8,128)(2,1)S(1)}, bf16[48,256]{1,0:T(8,128)(2,1)S(1)}, u32[]{:S(2)}, u32[]{:S(2)}) collective-permute-start(bf16[48,256]{1,0:T(8,128)(2,1)S(1)} %get-tuple-element.18), channel_id=1, source_target_pairs={{0,4},{4,0},{8,12},{12,8},{1,5},{5,1},{9,13},{13,9},{2,6},{6,2},{1... | collective-permute-start | bytes 73736 | tf_op jit(solution)/shard_map/ppermute | solution.py:213
  4.4 5.1 %collective-permute-start.1 = (bf16[48,256]{1,0:T(8,128)(2,1)S(1)}, bf16[48,256]{1,0:T(8,128)(2,1)S(1)}, u32[]{:S(2)}, u32[]{:S(2)}) collective-permute-start(bf16[48,256]{1,0:T(8,128)(2,1)S(1)} %get-tuple-element.19), channel_id=1, source_target_pairs={{0,8},{4,12},{8,0},{12,4},{1,9},{5,13},{9,1},{13,5},{2,10},{6,14},... | collective-permute-start | bytes 73736 | tf_op jit(solution)/shard_map/ppermute | solution.py:213
  6.9 5.6 %collective-permute-start.2 = (bf16[48,256]{1,0:T(8,128)(2,1)S(1)}, bf16[48,256]{1,0:T(8,128)(2,1)S(1)}, u32[]{:S(2)}, u32[]{:S(2)}) collective-permute-start(bf16[48,256]{1,0:T(8,128)(2,1)S(1)} %get-tuple-element.20), channel_id=1, source_target_pairs={{0,12},{4,8},{8,4},{12,0},{1,13},{5,9},{9,5},{13,1},{2,14},{6,10},... | collective-permute-start | bytes 73736 | tf_op jit(solution)/shard_map/ppermute | solution.py:213
  6.9 16.3 %collective-permute-start.6 = (bf16[1024,256]{1,0:T(8,128)(2,1)S(1)}, bf16[1024,256]{1,0:T(8,128)(2,1)S(1)}, u32[]{:S(2)}, u32[]{:S(2)}) collective-permute-start(bf16[1024,256]{1,0:T(8,128)(2,1)S(1)} %get-tuple-element.26.refs_7_), channel_id=1, source_target_pairs={{0,2},{1,3},{2,0},{3,1},{4,6},{5,7},{6,4},{7,5},{8,10},{9,11},{10,... | collective-permute-start | bytes 1572872 | tf_op jit(solution)/shard_map/ppermute | solution.py:213
  12.6 12.7 %copy-start = (bf16[64,256]{1,0:T(8,128)(2,1)S(1)}, bf16[64,256]{1,0:T(8,128)(2,1)}, u32[]{:S(2)}) copy-start(bf16[64,256]{1,0:T(8,128)(2,1)} %refs_5_.1) | copy-start | bytes 98308
  12.6 12.7 %copy-start.1 = (f32[256]{0:T(256)S(1)}, f32[256]{0:T(256)}, u32[]{:S(2)}) copy-start(f32[256]{0:T(256)} %param.11) | copy-start | bytes 3076
  18.8 5.0 %collective-permute-start.3 = (bf16[40,256]{1,0:T(8,128)(2,1)S(1)}, bf16[40,256]{1,0:T(8,128)(2,1)S(1)}, u32[]{:S(2)}, u32[]{:S(2)}) collective-permute-start(bf16[40,256]{1,0:T(8,128)(2,1)S(1)} %get-tuple-element.22), channel_id=1, source_target_pairs={{0,4},{4,0},{8,12},{12,8},{1,5},{5,1},{9,13},{13,9},{2,6},{6,2},{1... | collective-permute-start | bytes 61448 | tf_op jit(solution)/shard_map/ppermute | solution.py:213
  18.8 4.9 %collective-permute-start.4 = (bf16[40,256]{1,0:T(8,128)(2,1)S(1)}, bf16[40,256]{1,0:T(8,128)(2,1)S(1)}, u32[]{:S(2)}, u32[]{:S(2)}) collective-permute-start(bf16[40,256]{1,0:T(8,128)(2,1)S(1)} %get-tuple-element.23), channel_id=1, source_target_pairs={{0,8},{4,12},{8,0},{12,4},{1,9},{5,13},{9,1},{13,5},{2,10},{6,14},... | collective-permute-start | bytes 61448 | tf_op jit(solution)/shard_map/ppermute | solution.py:213
  19.7 5.6 %collective-permute-start.5 = (bf16[40,256]{1,0:T(8,128)(2,1)S(1)}, bf16[40,256]{1,0:T(8,128)(2,1)S(1)}, u32[]{:S(2)}, u32[]{:S(2)}) collective-permute-start(bf16[40,256]{1,0:T(8,128)(2,1)S(1)} %get-tuple-element.24), channel_id=1, source_target_pairs={{0,12},{4,8},{8,4},{12,0},{1,13},{5,9},{9,5},{13,1},{2,14},{6,10},... | collective-permute-start | bytes 61448 | tf_op jit(solution)/shard_map/ppermute | solution.py:213
  23.2 2.8 %collective-permute-start.7 = (bf16[1024,256]{1,0:T(8,128)(2,1)S(1)}, bf16[1024,256]{1,0:T(8,128)(2,1)S(1)}, u32[]{:S(2)}, u32[]{:S(2)}) collective-permute-start(bf16[1024,256]{1,0:T(8,128)(2,1)S(1)} %get-tuple-element.26.refs_7_), channel_id=1, source_target_pairs={{0,1},{1,0},{2,3},{3,2},{4,5},{5,4},{6,7},{7,6},{8,9},{9,8},{10,11... | collective-permute-start | bytes 1572872 | tf_op jit(solution)/shard_map/ppermute | solution.py:213
  23.2 2.8 %collective-permute-start.8 = (bf16[1024,256]{1,0:T(8,128)(2,1)S(1)}, bf16[1024,256]{1,0:T(8,128)(2,1)S(1)}, u32[]{:S(2)}, u32[]{:S(2)}) collective-permute-start(bf16[1024,256]{1,0:T(8,128)(2,1)S(1)} %collective-permute-done.6.refs_8_), channel_id=1, source_target_pairs={{0,1},{1,0},{2,3},{3,2},{4,5},{5,4},{6,7},{7,6},{8,9},{9,8},{10,11... | collective-permute-start | bytes 1572872 | tf_op jit(solution)/shard_map/ppermute | solution.py:213

commit v4 on v3

--- a/solution.py
+++ b/solution.py
@@ -12,7 +12,6 @@
 WC = 8
 META = 8
 ROWS_PER_STEP = 4
-ARRIVALS = (16, 16, 32)
 VMEM = pltpu.VMEM
 
 
@@ -83,20 +82,10 @@
 
 
 def pool_kernel(blocks, groups, room, *refs):
-    block_refs, features_hbm, refs = refs[:blocks], refs[blocks], refs[blocks + 1 :]
-    out_refs, (features_ref, sems) = refs[:-2], refs[-2:]
+    block_refs, features_ref, out_refs = refs[:blocks][::-1], refs[blocks], refs[blocks + 1 :]
     bf16, f32 = jnp.bfloat16, jnp.float32
     slots, feat = groups * room, features_ref.shape[2]
     steps = features_ref.shape[0] // ROWS_PER_STEP
-    copies, at = {}, 0
-    for i, size in enumerate(ARRIVALS):
-        part = pl.ds(at, size)
-        copies[at // ROWS_PER_STEP] = pltpu.make_async_copy(
-            features_hbm.at[part], features_ref.at[part], sems.at[i]
-        )
-        copies[at // ROWS_PER_STEP].start()
-        at += size
-
     stride = block_refs[0].shape[0] * blocks // groups
     unit = jnp.where(
         lax.broadcasted_iota(jnp.int32, (room, room), 0)
@@ -133,8 +122,6 @@
         )
 
     def logits(step):
-        if step in copies:
-            copies[step].wait()
         return lax.dot_general(
             rows16, cells(step), (((1,), (1,)), ((), ())), preferred_element_type=f32
         )
@@ -185,20 +172,14 @@
 
 def update_kernel(backs, shards, *refs):
     back_refs, pick_ref, refs = refs[:backs], refs[backs], refs[backs + 1 :]
-    own_hbm, shard_refs, refs = refs[:2], refs[2 : 2 + shards], refs[2 + shards :]
-    normed_ref, total_ref, kernels_ref, gain_ref, sems = refs
-    own = (kernels_ref, gain_ref)
+    (kernels_ref, gain_ref), shard_refs, refs = refs[:2], refs[2 : 2 + shards], refs[2 + shards :]
+    normed_ref, total_ref = refs
     f32 = jnp.float32
-    copies = start_all(
-        [pltpu.make_async_copy(a, b, sems.at[i]) for i, (a, b) in enumerate(zip(own_hbm, own))]
-    )
-    back = jnp.concatenate([ref[...].astype(f32) for ref in back_refs], axis=0)
+    back = jnp.concatenate([ref[...].astype(f32) for ref in back_refs[::-1]], axis=0)
     ratio = jnp.dot(pick_ref[...], back.astype(pick_ref.dtype), preferred_element_type=f32)
-    copies[0].wait()
     merged = kernels_ref[...].astype(f32) + ratio
     centred = merged - jnp.mean(merged, axis=1, keepdims=True)
     spread = jnp.mean(centred * centred, axis=1, keepdims=True)
-    copies[1].wait()
     normed = (centred * lax.rsqrt(spread + 1e-05) * gain_ref[...]).astype(normed_ref.dtype)
     normed_ref[...] = normed
     total_ref[...] = through(normed, merged, shard_refs)
@@ -211,6 +192,20 @@
 
 def exchanged(x, axis, distance):
     return lax.ppermute(x, axis, [(i, i ^ distance) for i in range(lax.axis_size(axis))])
+
+
+def all_exchanged(xs):
+    strips, holders = lax.axis_size("tile"), lax.axis_size("inst")
+    beside = 1 if holders % 2 == 0 else 0
+    pairs = [(t, i) for t in range(strips) for i in range(holders)]
+    return [
+        lax.ppermute(
+            xs[d],
+            ("tile", "inst"),
+            [(t * holders + i, (t ^ d) * holders + (i ^ beside)) for t, i in pairs],
+        )
+        for d in range(len(xs) - 1, 0, -1)
+    ]
 
 
 def local(features, kernels, home, boxes, gain, w_in, w_out):
@@ -240,10 +235,14 @@
             pltpu.VMEM((count, feat), kernels.dtype),
             pltpu.SemaphoreType.DMA((4 + hidden // feat,)),
         ],
+        cost_estimate=pl.CostEstimate(
+            flops=40 * slots * features.size, bytes_accessed=2 * features.size, transcendentals=0
+        ),
+        compiler_params=pltpu.CompilerParams(vmem_limit_bytes=24 << 20),
         name="pack",
-    )(home.T, boxes.T, kernels, w_out, w_in)
+    )(*[pltpu.with_memory_space_constraint(x, pltpu.HBM) for x in (home.T, boxes.T, kernels, w_out, w_in)])
     if near:
-        blocks = [blocks[0]] + [exchanged(blocks[d], "tile", d) for d in range(1, strips)]
+        blocks = all_exchanged(blocks) + [blocks[0]]
         outs = [jax.ShapeDtypeStruct((room, feat), kernels.dtype)] * strips
     else:
         got = lax.all_to_all(
@@ -261,20 +260,16 @@
     back = pl.pallas_call(
         functools.partial(pool_kernel, len(blocks), strips, room),
         out_shape=outs,
-        in_specs=[any_] * len(blocks) + [hbm],
+        in_specs=[any_] * (len(blocks) + 1),
         out_specs=[any_] * len(outs),
-        scratch_shapes=[
-            pltpu.VMEM(features.shape, features.dtype),
-            pltpu.SemaphoreType.DMA((len(ARRIVALS),)),
-        ],
-        compiler_params=pltpu.CompilerParams(vmem_limit_bytes=48 << 20),
+        compiler_params=pltpu.CompilerParams(vmem_limit_bytes=24 << 20),
         cost_estimate=pl.CostEstimate(
             flops=40 * slots * features.size, bytes_accessed=2 * features.size, transcendentals=0
         ),
         name="pool",
     )(*blocks, features)
     if near:
-        backs = [back[0]] + [exchanged(back[d], "tile", d) for d in range(1, strips)]
+        backs = all_exchanged(back) + [back[0]]
     else:
         got = lax.all_to_all(
             back[0].reshape(strips, room, feat), "tile", split_axis=0, concat_axis=0, tiled=True
@@ -288,14 +283,9 @@
             jax.ShapeDtypeStruct((count, feat), kernels.dtype),
             jax.ShapeDtypeStruct((count, feat), jnp.float32),
         ],
-        in_specs=[any_] * (len(backs) + 1) + [hbm] * 2 + [any_] * len(shards),
+        in_specs=[any_] * (len(backs) + 3 + len(shards)),
         out_specs=[any_] * 2,
-        scratch_shapes=[
-            pltpu.VMEM((count, feat), kernels.dtype),
-            pltpu.VMEM((1, feat), gain.dtype),
-            pltpu.SemaphoreType.DMA((2,)),
-        ],
-        compiler_params=pltpu.CompilerParams(vmem_limit_bytes=48 << 20),
+        compiler_params=pltpu.CompilerParams(vmem_limit_bytes=24 << 20),
         cost_estimate=pl.CostEstimate(
             flops=40 * slots * features.size, bytes_accessed=2 * features.size, transcendentals=0
         ),
@@ -306,7 +296,7 @@
         out_shape=jax.ShapeDtypeStruct((count, feat), kernels.dtype),
         in_specs=[any_] * (2 + len(late)),
         out_specs=any_,
-        compiler_params=pltpu.CompilerParams(vmem_limit_bytes=48 << 20),
+        compiler_params=pltpu.CompilerParams(vmem_limit_bytes=24 << 20),
         name="finish",
     )(normed, total, *late)
 

time: 27.2 us -> 23.8 us (0.88)
  Pallas kernels: 9.23 us -> 7.66 us
  starting transfers between devices: 12.3 us -> 11.3 us
  waiting for transfers between devices: 5.42 us -> 4.68 us
    ppermute x9 -> x3, starting transfers between devices: 12.3 us -> 1.55 us  [exchanged(): lax.ppermute(x, axis, [(i, i ^ distance) for i in range(lax.axis_size(axi...]
    ppermute x0 -> x6, starting transfers between devices: none -> 9.71 us  [all_exchanged(): lax.ppermute(xs[d], ('tile', 'inst'), [(t * holders + i, (t ^ d) * holder...]
    ppermute x9 -> x3, waiting for transfers between devices: 5.42 us -> 2 us  [exchanged(): lax.ppermute(x, axis, [(i, i ^ distance) for i in range(lax.axis_size(axi...]
    ppermute x0 -> x6, waiting for transfers between devices: none -> 2.68 us  [all_exchanged(): lax.ppermute(xs[d], ('tile', 'inst'), [(t * holders + i, (t ^ d) * holder...]
    pallas_call x1, Pallas kernels: 6.18 us -> 4.56 us  [local(): pl.pallas_call(functools.partial(pool_kernel, len(blocks), strips, room),...]
  transfers between devices with their start and end apart: 9 -> 9, of which waited for: 3 -> 5; matrix products, arithmetic and copies ran while one was open for 0% -> 0% of each run, Pallas kernels for 26% -> 22%
where the time goes in v4:
time: 23.8 us; the launch traced here: 23.7 us
  starting transfers between devices  11.3 us (47%)
  Pallas kernels  7.66 us (32%)
  waiting for transfers between devices  4.68 us (20%)
    ppermute x6, starting transfers between devices, all_exchanged(): lax.ppermute(xs[d], ('tile', 'inst'), [(t * holders + i, (t ^ d) * holder...  9.71 us
    pallas_call x1, Pallas kernels, local(): pl.pallas_call(functools.partial(pool_kernel, len(blocks), strips, room),...  4.56 us
    ppermute x6, waiting for transfers between devices, all_exchanged(): lax.ppermute(xs[d], ('tile', 'inst'), [(t * holders + i, (t ^ d) * holder...  2.68 us
    ppermute x3, waiting for transfers between devices, exchanged(): lax.ppermute(x, axis, [(i, i ^ distance) for i in range(lax.axis_size(axi...  2 us
    ppermute x3, starting transfers between devices, exchanged(): lax.ppermute(x, axis, [(i, i ^ distance) for i in range(lax.axis_size(axi...  1.55 us
    pallas_call x1, Pallas kernels, local(): pl.pallas_call(functools.partial(pack_kernel, near, strips, room), out_sh...  1.41 us
    pallas_call x1, Pallas kernels, local(): pl.pallas_call(finish_kernel, out_shape=jax.ShapeDtypeStruct((count, feat...  1.02 us
    pallas_call x1, Pallas kernels, local(): pl.pallas_call(functools.partial(update_kernel, len(backs), len(shards)),...  0.67 us
  transfers between devices with their start and end apart: 9, of which 5 were waited for; matrix products, arithmetic and copies ran while one was open for 0% of the time, Pallas kernels for 22%

profile of v4, /device:TPU:0, one launch (start us, length us, event | category | flops | bytes accessed | tf_op | source)
XLA Modules:
  0.0 23.7 jit_solution(16087182876614491153)
XLA Ops:
  0.0 0.0 copy-start
  0.0 1.4 %pack.1 = (bf16[48,256]{1,0:T(8,128)(2,1)S(1)}, bf16[48,256]{1,0:T(8,128)(2,1)S(1)}, bf16[48,256]{1,0:T(8,128)(2,1)S(1)}, bf16[48,256]{1,0:T(8,128)(2,1)S(1)}, b...) custom-call(s32[1,64]{1,0:T(1,128)} %bitcast.5, s32[4,64]{1,0:T(4,128)} %bitcast.4, bf16[64,256]{1,0:T(8,128)(2,1)} %refs_5_.1, ...), custom_call_target="tpu_custom_call" | custom-call | flops 26843545600 | bytes 8388608 | tf_op jit(solution)/shard_map/pack/pallas_call | solution.py:223
  1.4 4.6 %collective-permute-start = (bf16[48,256]{1,0:T(8,128)(2,1)S(1)}, bf16[48,256]{1,0:T(8,128)(2,1)S(1)}, u32[]{:S(2)}, u32[]{:S(2)}) collective-permute-start(bf16[48,256]{1,0:T(8,128)(2,1)S(1)} %get-tuple-element.17), channel_id=1, source_target_pairs={{0,13},{1,12},{2,15},{3,14},{4,9},{5,8},{6,11},{7,10},{8,5},{9,4},... | collective-permute-start | bytes 73736 | tf_op jit(solution)/shard_map/ppermute | solution.py:202
  6.0 0.0 collective-permute-start.1
  6.0 0.9 %collective-permute-start.2 = (bf16[48,256]{1,0:T(8,128)(2,1)S(1)}, bf16[48,256]{1,0:T(8,128)(2,1)S(1)}, u32[]{:S(2)}, u32[]{:S(2)}) collective-permute-start(bf16[48,256]{1,0:T(8,128)(2,1)S(1)} %get-tuple-element.19), channel_id=1, source_target_pairs={{0,5},{1,4},{2,7},{3,6},{4,1},{5,0},{6,3},{7,2},{8,13},{9,12},{10,... | collective-permute-start | bytes 73736 | tf_op jit(solution)/shard_map/ppermute | solution.py:202
  6.9 1.5 %collective-permute-start.6 = (bf16[1024,256]{1,0:T(8,128)(2,1)S(1)}, bf16[1024,256]{1,0:T(8,128)(2,1)S(1)}, u32[]{:S(2)}, u32[]{:S(2)}) collective-permute-start(bf16[1024,256]{1,0:T(8,128)(2,1)S(1)} %get-tuple-element.26.refs_7_), channel_id=1, source_target_pairs={{0,2},{1,3},{2,0},{3,1},{4,6},{5,7},{6,4},{7,5},{8,10},{9,11},{10,... | collective-permute-start | bytes 1572872 | tf_op jit(solution)/shard_map/ppermute | solution.py:194
  8.4 0.0 collective-permute-done.refs_0_
  8.4 1.9 %collective-permute-done.1.refs_1_ = bf16[48,256]{1,0:T(8,128)(2,1)S(1)} collective-permute-done((bf16[48,256]{1,0:T(8,128)(2,1)S(1)}, bf16[48,256]{1,0:T(8,128)(2,1)S(1)}, u32[]{:S(2)}, u32[]{:S(2)}) %collective-permute-start.1) | collective-permute-done | bytes 24608 | tf_op jit(solution)/shard_map/ppermute | solution.py:202
  10.3 0.0 collective-permute-done.2.refs_2_
  10.3 0.0 copy-done
  10.3 0.0 copy-start.1
  10.4 0.0 copy-start.2
  10.4 4.6 %pool.1 = (bf16[40,256]{1,0:T(8,128)(2,1)S(1)}, bf16[40,256]{1,0:T(8,128)(2,1)S(1)}, bf16[40,256]{1,0:T(8,128)(2,1)S(1)}, bf16[40,256]{1,0:T(8,128)(2,1)S(1)}) custom-call(bf16[48,256]{1,0:T(8,128)(2,1)S(1)} %collective-permute-done.refs_0_, bf16[48,256]{1,0:T(8,128)(2,1)S(1)} %collective-permute-done.1.refs_1_, ...), custom_call_target="tpu_custom_call" | custom-call | flops 26843545600 | bytes 8388608 | tf_op jit(solution)/shard_map/pool/pallas_call | solution.py:260
  14.9 1.6 %collective-permute-start.3 = (bf16[40,256]{1,0:T(8,128)(2,1)S(1)}, bf16[40,256]{1,0:T(8,128)(2,1)S(1)}, u32[]{:S(2)}, u32[]{:S(2)}) collective-permute-start(bf16[40,256]{1,0:T(8,128)(2,1)S(1)} %get-tuple-element.21), channel_id=1, source_target_pairs={{0,13},{1,12},{2,15},{3,14},{4,9},{5,8},{6,11},{7,10},{8,5},{9,4},... | collective-permute-start | bytes 61448 | tf_op jit(solution)/shard_map/ppermute | solution.py:202
  16.5 0.6 %collective-permute-start.4 = (bf16[40,256]{1,0:T(8,128)(2,1)S(1)}, bf16[40,256]{1,0:T(8,128)(2,1)S(1)}, u32[]{:S(2)}, u32[]{:S(2)}) collective-permute-start(bf16[40,256]{1,0:T(8,128)(2,1)S(1)} %get-tuple-element.22), channel_id=1, source_target_pairs={{0,9},{1,8},{2,11},{3,10},{4,13},{5,12},{6,15},{7,14},{8,1},{9,0},... | collective-permute-start | bytes 61448 | tf_op jit(solution)/shard_map/ppermute | solution.py:202
  17.1 2.1 %collective-permute-start.5 = (bf16[40,256]{1,0:T(8,128)(2,1)S(1)}, bf16[40,256]{1,0:T(8,128)(2,1)S(1)}, u32[]{:S(2)}, u32[]{:S(2)}) collective-permute-start(bf16[40,256]{1,0:T(8,128)(2,1)S(1)} %get-tuple-element.23), channel_id=1, source_target_pairs={{0,5},{1,4},{2,7},{3,6},{4,1},{5,0},{6,3},{7,2},{8,13},{9,12},{10,... | collective-permute-start | bytes 61448 | tf_op jit(solution)/shard_map/ppermute | solution.py:202
  19.2 0.1 collective-permute-start.7
  19.2 1.5 %collective-permute-done.6.refs_8_ = bf16[1024,256]{1,0:T(8,128)(2,1)S(1)} collective-permute-done((bf16[1024,256]{1,0:T(8,128)(2,1)S(1)}, bf16[1024,256]{1,0:T(8,128)(2,1)S(1)}, u32[]{:S(2)}, u32[]{:S(2)}) %collective-permute-start.6) | collective-permute-done | bytes 524320 | tf_op jit(solution)/shard_map/ppermute | solution.py:194
  20.7 0.0 collective-permute-start.8
  20.7 0.0 collective-permute-done.3.refs_0_
  20.7 0.1 collective-permute-done.4.refs_1_
  20.9 0.6 %collective-permute-done.5.refs_2_ = bf16[40,256]{1,0:T(8,128)(2,1)S(1)} collective-permute-done((bf16[40,256]{1,0:T(8,128)(2,1)S(1)}, bf16[40,256]{1,0:T(8,128)(2,1)S(1)}, u32[]{:S(2)}, u32[]{:S(2)}) %collective-permute-start.5) | collective-permute-done | bytes 20512 | tf_op jit(solution)/shard_map/ppermute | solution.py:202
  21.5 0.0 copy-done.1
  21.5 0.0 copy-done.2
  21.5 0.7 %update.1 = (bf16[64,256]{1,0:T(8,128)(2,1)S(1)}, f32[64,256]{1,0:T(8,128)S(1)}) custom-call(bf16[40,256]{1,0:T(8,128)(2,1)S(1)} %collective-permute-done.3.refs_0_, bf16[40,256]{1,0:T(8,128)(2,1)S(1)} %collective-permute-done.4.refs_1_, bf16[40,256]{1,0:T(8,128)(2,1)S(1)} %collective-permute-done.5.refs_2_, bf16[40,256]{1,0:T(8,128)(2,1)S(1)} %get-tuple-element.24.refs_3_, ...), custom_call_target="tpu_custom_call" | custom-call | flops 26843545600 | bytes 8388608 | tf_op jit(solution)/shard_map/update/pallas_call | solution.py:280
  22.2 0.0 collective-permute-done.7.refs_0_
  22.2 0.5 %collective-permute-done.8.refs_1_ = bf16[1024,256]{1,0:T(8,128)(2,1)S(1)} collective-permute-done((bf16[1024,256]{1,0:T(8,128)(2,1)S(1)}, bf16[1024,256]{1,0:T(8,128)(2,1)S(1)}, u32[]{:S(2)}, u32[]{:S(2)}) %collective-permute-start.8) | collective-permute-done | bytes 524320 | tf_op jit(solution)/shard_map/ppermute | solution.py:194
  22.6 1.0 %finish.1 = bf16[64,256]{1,0:T(8,128)(2,1)} custom-call(bf16[64,256]{1,0:T(8,128)(2,1)S(1)} %get-tuple-element.27.normed_ref, f32[64,256]{1,0:T(8,128)S(1)} %get-tuple-element.28.total_ref, bf16[1024,256]{1,0:T(8,128)(2,1)S(1)} %collective-permute-done.7.refs_0_, bf16[1024,256]{1,0:T(8,128)(2,1)S(1)} %collective-permute-done.8.refs_1_), custom_call_target="tpu_custom_call" | custom-call | tf_op jit(solution)/shard_map/finish/pallas_call | solution.py:294
Async XLA Ops:
  0.0 10.3 %copy-start = (bf16[64,256,256]{2,1,0:T(8,128)(2,1)S(1)}, bf16[64,256,256]{2,1,0:T(8,128)(2,1)}, u32[]{:S(2)}) copy-start(bf16[64,256,256]{2,1,0:T(8,128)(2,1)} %refs_4_.3) | copy-start | bytes 25165828
  1.4 7.0 %collective-permute-start = (bf16[48,256]{1,0:T(8,128)(2,1)S(1)}, bf16[48,256]{1,0:T(8,128)(2,1)S(1)}, u32[]{:S(2)}, u32[]{:S(2)}) collective-permute-start(bf16[48,256]{1,0:T(8,128)(2,1)S(1)} %get-tuple-element.17), channel_id=1, source_target_pairs={{0,13},{1,12},{2,15},{3,14},{4,9},{5,8},{6,11},{7,10},{8,5},{9,4},... | collective-permute-start | bytes 73736 | tf_op jit(solution)/shard_map/ppermute | solution.py:202
  6.0 4.4 %collective-permute-start.1 = (bf16[48,256]{1,0:T(8,128)(2,1)S(1)}, bf16[48,256]{1,0:T(8,128)(2,1)S(1)}, u32[]{:S(2)}, u32[]{:S(2)}) collective-permute-start(bf16[48,256]{1,0:T(8,128)(2,1)S(1)} %get-tuple-element.18), channel_id=1, source_target_pairs={{0,9},{1,8},{2,11},{3,10},{4,13},{5,12},{6,15},{7,14},{8,1},{9,0},... | collective-permute-start | bytes 73736 | tf_op jit(solution)/shard_map/ppermute | solution.py:202
  6.0 4.4 %collective-permute-start.2 = (bf16[48,256]{1,0:T(8,128)(2,1)S(1)}, bf16[48,256]{1,0:T(8,128)(2,1)S(1)}, u32[]{:S(2)}, u32[]{:S(2)}) collective-permute-start(bf16[48,256]{1,0:T(8,128)(2,1)S(1)} %get-tuple-element.19), channel_id=1, source_target_pairs={{0,5},{1,4},{2,7},{3,6},{4,1},{5,0},{6,3},{7,2},{8,13},{9,12},{10,... | collective-permute-start | bytes 73736 | tf_op jit(solution)/shard_map/ppermute | solution.py:202
  6.9 13.8 %collective-permute-start.6 = (bf16[1024,256]{1,0:T(8,128)(2,1)S(1)}, bf16[1024,256]{1,0:T(8,128)(2,1)S(1)}, u32[]{:S(2)}, u32[]{:S(2)}) collective-permute-start(bf16[1024,256]{1,0:T(8,128)(2,1)S(1)} %get-tuple-element.26.refs_7_), channel_id=1, source_target_pairs={{0,2},{1,3},{2,0},{3,1},{4,6},{5,7},{6,4},{7,5},{8,10},{9,11},{10,... | collective-permute-start | bytes 1572872 | tf_op jit(solution)/shard_map/ppermute | solution.py:194
  10.3 11.1 %copy-start.1 = (bf16[64,256]{1,0:T(8,128)(2,1)S(1)}, bf16[64,256]{1,0:T(8,128)(2,1)}, u32[]{:S(2)}) copy-start(bf16[64,256]{1,0:T(8,128)(2,1)} %refs_5_.1) | copy-start | bytes 98308
  10.4 11.1 %copy-start.2 = (f32[256]{0:T(256)S(1)}, f32[256]{0:T(256)}, u32[]{:S(2)}) copy-start(f32[256]{0:T(256)} %param.11) | copy-start | bytes 3076
  14.9 5.8 %collective-permute-start.3 = (bf16[40,256]{1,0:T(8,128)(2,1)S(1)}, bf16[40,256]{1,0:T(8,128)(2,1)S(1)}, u32[]{:S(2)}, u32[]{:S(2)}) collective-permute-start(bf16[40,256]{1,0:T(8,128)(2,1)S(1)} %get-tuple-element.21), channel_id=1, source_target_pairs={{0,13},{1,12},{2,15},{3,14},{4,9},{5,8},{6,11},{7,10},{8,5},{9,4},... | collective-permute-start | bytes 61448 | tf_op jit(solution)/shard_map/ppermute | solution.py:202
  16.5 4.4 %collective-permute-start.4 = (bf16[40,256]{1,0:T(8,128)(2,1)S(1)}, bf16[40,256]{1,0:T(8,128)(2,1)S(1)}, u32[]{:S(2)}, u32[]{:S(2)}) collective-permute-start(bf16[40,256]{1,0:T(8,128)(2,1)S(1)} %get-tuple-element.22), channel_id=1, source_target_pairs={{0,9},{1,8},{2,11},{3,10},{4,13},{5,12},{6,15},{7,14},{8,1},{9,0},... | collective-permute-start | bytes 61448 | tf_op jit(solution)/shard_map/ppermute | solution.py:202
  17.1 4.4 %collective-permute-start.5 = (bf16[40,256]{1,0:T(8,128)(2,1)S(1)}, bf16[40,256]{1,0:T(8,128)(2,1)S(1)}, u32[]{:S(2)}, u32[]{:S(2)}) collective-permute-start(bf16[40,256]{1,0:T(8,128)(2,1)S(1)} %get-tuple-element.23), channel_id=1, source_target_pairs={{0,5},{1,4},{2,7},{3,6},{4,1},{5,0},{6,3},{7,2},{8,13},{9,12},{10,... | collective-permute-start | bytes 61448 | tf_op jit(solution)/shard_map/ppermute | solution.py:202
  19.2 3.0 %collective-permute-start.7 = (bf16[1024,256]{1,0:T(8,128)(2,1)S(1)}, bf16[1024,256]{1,0:T(8,128)(2,1)S(1)}, u32[]{:S(2)}, u32[]{:S(2)}) collective-permute-start(bf16[1024,256]{1,0:T(8,128)(2,1)S(1)} %get-tuple-element.26.refs_7_), channel_id=1, source_target_pairs={{0,1},{1,0},{2,3},{3,2},{4,5},{5,4},{6,7},{7,6},{8,9},{9,8},{10,11... | collective-permute-start | bytes 1572872 | tf_op jit(solution)/shard_map/ppermute | solution.py:194
  20.7 1.9 %collective-permute-start.8 = (bf16[1024,256]{1,0:T(8,128)(2,1)S(1)}, bf16[1024,256]{1,0:T(8,128)(2,1)S(1)}, u32[]{:S(2)}, u32[]{:S(2)}) collective-permute-start(bf16[1024,256]{1,0:T(8,128)(2,1)S(1)} %collective-permute-done.6.refs_8_), channel_id=1, source_target_pairs={{0,1},{1,0},{2,3},{3,2},{4,5},{5,4},{6,7},{7,6},{8,9},{9,8},{10,11... | collective-permute-start | bytes 1572872 | tf_op jit(solution)/shard_map/ppermute | solution.py:194

commit v5 on v4

--- a/solution.py
+++ b/solution.py
@@ -23,7 +23,7 @@
 
 def pack_kernel(near, groups, room, *refs):
     home_hbm, boxes_hbm, kernels_hbm, w_out_hbm, w_in_hbm, block_refs = *refs[:5], refs[5:-6]
-    pick_ref, shard_ref, home_ref, boxes_ref, kernels_ref, sems = refs[-6:]
+    at_ref, shard_ref, home_ref, boxes_ref, kernels_ref, sems = refs[-6:]
     bf16, f32 = jnp.bfloat16, jnp.float32
     count, feat = kernels_ref.shape
     hidden = w_out_hbm.shape[0]
@@ -50,9 +50,9 @@
     member = jnp.where(group == line, 1.0, 0.0)
     rank = jnp.dot(member.astype(bf16), earlier, preferred_element_type=f32)
     rank = jnp.sum(rank * member, axis=0, keepdims=True).astype(jnp.int32)
-    select = jnp.where(group * room + rank == slot, 1.0, 0.0)
-    select16 = select.astype(bf16)
-    pick_ref[...] = select.T.astype(bf16)
+    at = group * room + rank
+    select16 = jnp.where(at == slot, 1.0, 0.0).astype(bf16)
+    at_ref[...] = jnp.broadcast_to(at, at_ref.shape)
     copies[1].wait()
     bounds = jnp.concatenate(
         [boxes_ref[...], jnp.zeros((META - boxes_ref.shape[0], count), jnp.int32)], axis=0
@@ -146,12 +146,17 @@
     area = jnp.sum(covered, axis=1, keepdims=True)
     ratio = (pooled / area).astype(bf16).astype(f32)
 
-    for g in range(groups):
-        part = ratio[g * room : (g + 1) * room]
-        if len(out_refs) > 1:
-            out_refs[g][...] = part.astype(bf16)
-        else:
-            out_refs[0][g * room : (g + 1) * room, :] = part.astype(bf16)
+    if len(out_refs) > 1:
+        for g in range(groups):
+            out_refs[g][...] = ratio[g * room : (g + 1) * room].astype(bf16)
+    else:
+        out_refs[0][...] = ratio.astype(bf16)
+
+
+def place_kernel(at_ref, pick_ref):
+    count, slots = pick_ref.shape
+    slot = lax.broadcasted_iota(jnp.int32, (slots, count), 0)
+    pick_ref[...] = jnp.where(at_ref[:1, :] == slot, 1.0, 0.0).T.astype(pick_ref.dtype)
 
 
 def through(normed, total, shard_refs):
@@ -220,11 +225,11 @@
     any_, hbm = pl.BlockSpec(memory_space=VMEM), pl.BlockSpec(memory_space=pltpu.HBM)
 
     parts = strips if near else 1
-    *blocks, pick, shard = pl.pallas_call(
+    *blocks, places, shard = pl.pallas_call(
         functools.partial(pack_kernel, near, strips, room),
         out_shape=[pltpu.VMEM((strips // parts * stride, feat), kernels.dtype)] * parts
         + [
-            pltpu.VMEM((count, slots), kernels.dtype),
+            pltpu.VMEM((count, count), jnp.int32),
             pltpu.VMEM((2 * hidden, feat), w_out.dtype),
         ],
         in_specs=[hbm] * 5,
@@ -275,7 +280,16 @@
             back[0].reshape(strips, room, feat), "tile", split_axis=0, concat_axis=0, tiled=True
         )
         backs = [got.reshape(slots, feat)]
+    pick = pl.pallas_call(
+        place_kernel,
+        out_shape=pltpu.VMEM((count, slots), kernels.dtype),
+        in_specs=[any_],
+        out_specs=any_,
+        compiler_params=pltpu.CompilerParams(vmem_limit_bytes=24 << 20),
+        name="place",
+    )(places)
     late = [exchanged(x, "inst", 1) for x in shards]
+    shards.insert(1, late.pop(0))
 
     normed, total = pl.pallas_call(
         functools.partial(update_kernel, len(backs), len(shards)),

time: 23.8 us -> 23.6 us (level)
  transfers between devices with their start and end apart: 9 -> 9, of which waited for: 5 -> 5; matrix products, arithmetic and copies ran while one was open for 0% -> 0% of each run, Pallas kernels for 22% -> 23%
where the time goes in v5:
time: 23.6 us; the launch traced here: 23.5 us
  starting transfers between devices  11.2 us (47%)
  Pallas kernels  7.68 us (33%)
  waiting for transfers between devices  4.55 us (19%)
    ppermute x6, starting transfers between devices, all_exchanged(): lax.ppermute(xs[d], ('tile', 'inst'), [(t * holders + i, (t ^ d) * holder...  9.7 us
    pallas_call x1, Pallas kernels, local(): pl.pallas_call(functools.partial(pool_kernel, len(blocks), strips, room),...  4.58 us
    ppermute x6, waiting for transfers between devices, all_exchanged(): lax.ppermute(xs[d], ('tile', 'inst'), [(t * holders + i, (t ^ d) * holder...  2.69 us
    ppermute x3, waiting for transfers between devices, exchanged(): lax.ppermute(x, axis, [(i, i ^ distance) for i in range(lax.axis_size(axi...  1.86 us
    ppermute x3, starting transfers between devices, exchanged(): lax.ppermute(x, axis, [(i, i ^ distance) for i in range(lax.axis_size(axi...  1.5 us
    pallas_call x1, Pallas kernels, local(): pl.pallas_call(functools.partial(pack_kernel, near, strips, room), out_sh...  1.33 us
    pallas_call x1, Pallas kernels, local(): pl.pallas_call(finish_kernel, out_shape=jax.ShapeDtypeStruct((count, feat...  0.93 us
    pallas_call x1, Pallas kernels, local(): pl.pallas_call(functools.partial(update_kernel, len(backs), len(shards)),...  0.74 us
  transfers between devices with their start and end apart: 9, of which 5 were waited for; matrix products, arithmetic and copies ran while one was open for 0% of the time, Pallas kernels for 23%

profile of v5, /device:TPU:0, one launch (start us, length us, event | category | flops | bytes accessed | tf_op | source)
XLA Modules:
  0.0 23.5 jit_solution(15509308022459922336)
XLA Ops:
  0.0 0.0 copy-start
  0.0 1.3 %pack.1 = (bf16[48,256]{1,0:T(8,128)(2,1)S(1)}, bf16[48,256]{1,0:T(8,128)(2,1)S(1)}, bf16[48,256]{1,0:T(8,128)(2,1)S(1)}, bf16[48,256]{1,0:T(8,128)(2,1)S(1)}, s...) custom-call(s32[1,64]{1,0:T(1,128)} %bitcast.5, s32[4,64]{1,0:T(4,128)} %bitcast.4, bf16[64,256]{1,0:T(8,128)(2,1)} %refs_5_.1, ...), custom_call_target="tpu_custom_call" | custom-call | flops 26843545600 | bytes 8388608 | tf_op jit(solution)/shard_map/pack/pallas_call | solution.py:228
  1.3 4.6 %collective-permute-start = (bf16[48,256]{1,0:T(8,128)(2,1)S(1)}, bf16[48,256]{1,0:T(8,128)(2,1)S(1)}, u32[]{:S(2)}, u32[]{:S(2)}) collective-permute-start(bf16[48,256]{1,0:T(8,128)(2,1)S(1)} %get-tuple-element.17), channel_id=1, source_target_pairs={{0,13},{1,12},{2,15},{3,14},{4,9},{5,8},{6,11},{7,10},{8,5},{9,4},... | collective-permute-start | bytes 73736 | tf_op jit(solution)/shard_map/ppermute | solution.py:207
  5.9 0.0 collective-permute-start.1
  5.9 0.9 %collective-permute-start.2 = (bf16[48,256]{1,0:T(8,128)(2,1)S(1)}, bf16[48,256]{1,0:T(8,128)(2,1)S(1)}, u32[]{:S(2)}, u32[]{:S(2)}) collective-permute-start(bf16[48,256]{1,0:T(8,128)(2,1)S(1)} %get-tuple-element.19), channel_id=1, source_target_pairs={{0,5},{1,4},{2,7},{3,6},{4,1},{5,0},{6,3},{7,2},{8,13},{9,12},{10,... | collective-permute-start | bytes 73736 | tf_op jit(solution)/shard_map/ppermute | solution.py:207
  6.8 1.5 %collective-permute-start.7 = (bf16[1024,256]{1,0:T(8,128)(2,1)S(1)}, bf16[1024,256]{1,0:T(8,128)(2,1)S(1)}, u32[]{:S(2)}, u32[]{:S(2)}) collective-permute-start(bf16[1024,256]{1,0:T(8,128)(2,1)S(1)} %get-tuple-element.26.refs_7_), channel_id=1, source_target_pairs={{0,2},{1,3},{2,0},{3,1},{4,6},{5,7},{6,4},{7,5},{8,10},{9,11},{10,... | collective-permute-start | bytes 1572872 | tf_op jit(solution)/shard_map/ppermute | solution.py:199
  8.3 0.0 collective-permute-start.6
  8.3 0.0 collective-permute-done.refs_0_
  8.3 1.9 %collective-permute-done.1.refs_1_ = bf16[48,256]{1,0:T(8,128)(2,1)S(1)} collective-permute-done((bf16[48,256]{1,0:T(8,128)(2,1)S(1)}, bf16[48,256]{1,0:T(8,128)(2,1)S(1)}, u32[]{:S(2)}, u32[]{:S(2)}) %collective-permute-start.1) | collective-permute-done | bytes 24608 | tf_op jit(solution)/shard_map/ppermute | solution.py:207
  10.3 0.0 collective-permute-done.2.refs_2_
  10.3 0.0 copy-done
  10.3 0.0 copy-start.1
  10.3 0.0 copy-start.2
  10.3 4.6 %pool.1 = (bf16[40,256]{1,0:T(8,128)(2,1)S(1)}, bf16[40,256]{1,0:T(8,128)(2,1)S(1)}, bf16[40,256]{1,0:T(8,128)(2,1)S(1)}, bf16[40,256]{1,0:T(8,128)(2,1)S(1)}) custom-call(bf16[48,256]{1,0:T(8,128)(2,1)S(1)} %collective-permute-done.refs_0_, bf16[48,256]{1,0:T(8,128)(2,1)S(1)} %collective-permute-done.1.refs_1_, ...), custom_call_target="tpu_custom_call" | custom-call | flops 26843545600 | bytes 8388608 | tf_op jit(solution)/shard_map/pool/pallas_call | solution.py:265
  14.9 1.6 %collective-permute-start.3 = (bf16[40,256]{1,0:T(8,128)(2,1)S(1)}, bf16[40,256]{1,0:T(8,128)(2,1)S(1)}, u32[]{:S(2)}, u32[]{:S(2)}) collective-permute-start(bf16[40,256]{1,0:T(8,128)(2,1)S(1)} %get-tuple-element.21), channel_id=1, source_target_pairs={{0,13},{1,12},{2,15},{3,14},{4,9},{5,8},{6,11},{7,10},{8,5},{9,4},... | collective-permute-start | bytes 61448 | tf_op jit(solution)/shard_map/ppermute | solution.py:207
  16.5 0.6 %collective-permute-start.4 = (bf16[40,256]{1,0:T(8,128)(2,1)S(1)}, bf16[40,256]{1,0:T(8,128)(2,1)S(1)}, u32[]{:S(2)}, u32[]{:S(2)}) collective-permute-start(bf16[40,256]{1,0:T(8,128)(2,1)S(1)} %get-tuple-element.22), channel_id=1, source_target_pairs={{0,9},{1,8},{2,11},{3,10},{4,13},{5,12},{6,15},{7,14},{8,1},{9,0},... | collective-permute-start | bytes 61448 | tf_op jit(solution)/shard_map/ppermute | solution.py:207
  17.1 2.1 %collective-permute-start.5 = (bf16[40,256]{1,0:T(8,128)(2,1)S(1)}, bf16[40,256]{1,0:T(8,128)(2,1)S(1)}, u32[]{:S(2)}, u32[]{:S(2)}) collective-permute-start(bf16[40,256]{1,0:T(8,128)(2,1)S(1)} %get-tuple-element.23), channel_id=1, source_target_pairs={{0,5},{1,4},{2,7},{3,6},{4,1},{5,0},{6,3},{7,2},{8,13},{9,12},{10,... | collective-permute-start | bytes 61448 | tf_op jit(solution)/shard_map/ppermute | solution.py:207
  19.1 0.1 place.1.refs_4_
  19.2 1.5 %collective-permute-done.7.refs_9_ = bf16[1024,256]{1,0:T(8,128)(2,1)S(1)} collective-permute-done((bf16[1024,256]{1,0:T(8,128)(2,1)S(1)}, bf16[1024,256]{1,0:T(8,128)(2,1)S(1)}, u32[]{:S(2)}, u32[]{:S(2)}) %collective-permute-start.7) | collective-permute-done | bytes 524320 | tf_op jit(solution)/shard_map/ppermute | solution.py:199
  20.7 0.0 collective-permute-start.8
  20.7 0.0 collective-permute-done.3.refs_0_
  20.7 0.2 collective-permute-done.4.refs_1_
  20.8 0.6 %collective-permute-done.5.refs_2_ = bf16[40,256]{1,0:T(8,128)(2,1)S(1)} collective-permute-done((bf16[40,256]{1,0:T(8,128)(2,1)S(1)}, bf16[40,256]{1,0:T(8,128)(2,1)S(1)}, u32[]{:S(2)}, u32[]{:S(2)}) %collective-permute-start.5) | collective-permute-done | bytes 20512 | tf_op jit(solution)/shard_map/ppermute | solution.py:207
  21.4 0.0 collective-permute-done.6.refs_8_
  21.4 0.0 copy-done.1
  21.4 0.0 copy-done.2
  21.4 0.7 %update.1 = (bf16[64,256]{1,0:T(8,128)(2,1)S(1)}, f32[64,256]{1,0:T(8,128)S(1)}) custom-call(bf16[40,256]{1,0:T(8,128)(2,1)S(1)} %collective-permute-done.3.refs_0_, bf16[40,256]{1,0:T(8,128)(2,1)S(1)} %collective-permute-done.4.refs_1_, bf16[40,256]{1,0:T(8,128)(2,1)S(1)} %collective-permute-done.5.refs_2_, bf16[40,256]{1,0:T(8,128)(2,1)S(1)} %get-tuple-element.24.refs_3_, ...), custom_call_target="tpu_custom_call" | custom-call | flops 26843545600 | bytes 8388608 | tf_op jit(solution)/shard_map/update/pallas_call | solution.py:294
  22.2 0.4 %collective-permute-done.8.refs_0_ = bf16[1024,256]{1,0:T(8,128)(2,1)S(1)} collective-permute-done((bf16[1024,256]{1,0:T(8,128)(2,1)S(1)}, bf16[1024,256]{1,0:T(8,128)(2,1)S(1)}, u32[]{:S(2)}, u32[]{:S(2)}) %collective-permute-start.8) | collective-permute-done | bytes 524320 | tf_op jit(solution)/shard_map/ppermute | solution.py:199
  22.6 0.9 %finish.1 = bf16[64,256]{1,0:T(8,128)(2,1)} custom-call(bf16[64,256]{1,0:T(8,128)(2,1)S(1)} %get-tuple-element.27.normed_ref, f32[64,256]{1,0:T(8,128)S(1)} %get-tuple-element.28.total_ref, bf16[1024,256]{1,0:T(8,128)(2,1)S(1)} %collective-permute-done.8.refs_0_), custom_call_target="tpu_custom_call" | custom-call | tf_op jit(solution)/shard_map/finish/pallas_call | solution.py:308
Async XLA Ops:
  0.0 10.3 %copy-start = (bf16[64,256,256]{2,1,0:T(8,128)(2,1)S(1)}, bf16[64,256,256]{2,1,0:T(8,128)(2,1)}, u32[]{:S(2)}) copy-start(bf16[64,256,256]{2,1,0:T(8,128)(2,1)} %refs_4_.3) | copy-start | bytes 25165828
  1.3 7.0 %collective-permute-start = (bf16[48,256]{1,0:T(8,128)(2,1)S(1)}, bf16[48,256]{1,0:T(8,128)(2,1)S(1)}, u32[]{:S(2)}, u32[]{:S(2)}) collective-permute-start(bf16[48,256]{1,0:T(8,128)(2,1)S(1)} %get-tuple-element.17), channel_id=1, source_target_pairs={{0,13},{1,12},{2,15},{3,14},{4,9},{5,8},{6,11},{7,10},{8,5},{9,4},... | collective-permute-start | bytes 73736 | tf_op jit(solution)/shard_map/ppermute | solution.py:207
  5.9 4.4 %collective-permute-start.1 = (bf16[48,256]{1,0:T(8,128)(2,1)S(1)}, bf16[48,256]{1,0:T(8,128)(2,1)S(1)}, u32[]{:S(2)}, u32[]{:S(2)}) collective-permute-start(bf16[48,256]{1,0:T(8,128)(2,1)S(1)} %get-tuple-element.18), channel_id=1, source_target_pairs={{0,9},{1,8},{2,11},{3,10},{4,13},{5,12},{6,15},{7,14},{8,1},{9,0},... | collective-permute-start | bytes 73736 | tf_op jit(solution)/shard_map/ppermute | solution.py:207
  5.9 4.4 %collective-permute-start.2 = (bf16[48,256]{1,0:T(8,128)(2,1)S(1)}, bf16[48,256]{1,0:T(8,128)(2,1)S(1)}, u32[]{:S(2)}, u32[]{:S(2)}) collective-permute-start(bf16[48,256]{1,0:T(8,128)(2,1)S(1)} %get-tuple-element.19), channel_id=1, source_target_pairs={{0,5},{1,4},{2,7},{3,6},{4,1},{5,0},{6,3},{7,2},{8,13},{9,12},{10,... | collective-permute-start | bytes 73736 | tf_op jit(solution)/shard_map/ppermute | solution.py:207
  6.8 13.8 %collective-permute-start.7 = (bf16[1024,256]{1,0:T(8,128)(2,1)S(1)}, bf16[1024,256]{1,0:T(8,128)(2,1)S(1)}, u32[]{:S(2)}, u32[]{:S(2)}) collective-permute-start(bf16[1024,256]{1,0:T(8,128)(2,1)S(1)} %get-tuple-element.26.refs_7_), channel_id=1, source_target_pairs={{0,2},{1,3},{2,0},{3,1},{4,6},{5,7},{6,4},{7,5},{8,10},{9,11},{10,... | collective-permute-start | bytes 1572872 | tf_op jit(solution)/shard_map/ppermute | solution.py:199
  8.3 13.1 %collective-permute-start.6 = (bf16[1024,256]{1,0:T(8,128)(2,1)S(1)}, bf16[1024,256]{1,0:T(8,128)(2,1)S(1)}, u32[]{:S(2)}, u32[]{:S(2)}) collective-permute-start(bf16[1024,256]{1,0:T(8,128)(2,1)S(1)} %get-tuple-element.26.refs_7_), channel_id=1, source_target_pairs={{0,1},{1,0},{2,3},{3,2},{4,5},{5,4},{6,7},{7,6},{8,9},{9,8},{10,11... | collective-permute-start | bytes 1572872 | tf_op jit(solution)/shard_map/ppermute | solution.py:199
  10.3 11.1 %copy-start.1 = (bf16[64,256]{1,0:T(8,128)(2,1)S(1)}, bf16[64,256]{1,0:T(8,128)(2,1)}, u32[]{:S(2)}) copy-start(bf16[64,256]{1,0:T(8,128)(2,1)} %refs_5_.1) | copy-start | bytes 98308
  10.3 11.1 %copy-start.2 = (f32[256]{0:T(256)S(1)}, f32[256]{0:T(256)}, u32[]{:S(2)}) copy-start(f32[256]{0:T(256)} %param.11) | copy-start | bytes 3076
  14.9 5.8 %collective-permute-start.3 = (bf16[40,256]{1,0:T(8,128)(2,1)S(1)}, bf16[40,256]{1,0:T(8,128)(2,1)S(1)}, u32[]{:S(2)}, u32[]{:S(2)}) collective-permute-start(bf16[40,256]{1,0:T(8,128)(2,1)S(1)} %get-tuple-element.21), channel_id=1, source_target_pairs={{0,13},{1,12},{2,15},{3,14},{4,9},{5,8},{6,11},{7,10},{8,5},{9,4},... | collective-permute-start | bytes 61448 | tf_op jit(solution)/shard_map/ppermute | solution.py:207
  16.5 4.4 %collective-permute-start.4 = (bf16[40,256]{1,0:T(8,128)(2,1)S(1)}, bf16[40,256]{1,0:T(8,128)(2,1)S(1)}, u32[]{:S(2)}, u32[]{:S(2)}) collective-permute-start(bf16[40,256]{1,0:T(8,128)(2,1)S(1)} %get-tuple-element.22), channel_id=1, source_target_pairs={{0,9},{1,8},{2,11},{3,10},{4,13},{5,12},{6,15},{7,14},{8,1},{9,0},... | collective-permute-start | bytes 61448 | tf_op jit(solution)/shard_map/ppermute | solution.py:207
  17.1 4.4 %collective-permute-start.5 = (bf16[40,256]{1,0:T(8,128)(2,1)S(1)}, bf16[40,256]{1,0:T(8,128)(2,1)S(1)}, u32[]{:S(2)}, u32[]{:S(2)}) collective-permute-start(bf16[40,256]{1,0:T(8,128)(2,1)S(1)} %get-tuple-element.23), channel_id=1, source_target_pairs={{0,5},{1,4},{2,7},{3,6},{4,1},{5,0},{6,3},{7,2},{8,13},{9,12},{10,... | collective-permute-start | bytes 61448 | tf_op jit(solution)/shard_map/ppermute | solution.py:207
  20.7 1.9 %collective-permute-start.8 = (bf16[1024,256]{1,0:T(8,128)(2,1)S(1)}, bf16[1024,256]{1,0:T(8,128)(2,1)S(1)}, u32[]{:S(2)}, u32[]{:S(2)}) collective-permute-start(bf16[1024,256]{1,0:T(8,128)(2,1)S(1)} %collective-permute-done.7.refs_9_), channel_id=1, source_target_pairs={{0,1},{1,0},{2,3},{3,2},{4,5},{5,4},{6,7},{7,6},{8,9},{9,8},{10,11... | collective-permute-start | bytes 1572872 | tf_op jit(solution)/shard_map/ppermute | solution.py:199

commit v6 on v5

--- a/solution.py
+++ b/solution.py
@@ -144,13 +144,23 @@
         )
         now = later
     area = jnp.sum(covered, axis=1, keepdims=True)
-    ratio = (pooled / area).astype(bf16).astype(f32)
-
-    if len(out_refs) > 1:
-        for g in range(groups):
-            out_refs[g][...] = ratio[g * room : (g + 1) * room].astype(bf16)
-    else:
-        out_refs[0][...] = ratio.astype(bf16)
+    ratio = pooled / area
+
+    mean = jnp.mean(ratio, axis=1, keepdims=True)
+    rounded = mean.astype(bf16).astype(f32)
+    lane = lax.broadcasted_iota(jnp.int32, (slots, 128), 1)
+    side = jnp.where(lane == 0, rounded, jnp.where(lane == 1, mean - rounded, 0.0)).T[:META]
+    if feat > slots:
+        side = jnp.concatenate([side, jnp.zeros((META, feat - slots), f32)], axis=1)
+    owner = lax.broadcasted_iota(jnp.int32, (META, feat), 1) // room
+    centred = ratio - mean
+    for g in range(groups):
+        ref, at = (out_refs[g], 0) if len(out_refs) > 1 else (out_refs[0], g * stride)
+        ref[at : at + stride, :] = jnp.concatenate(
+            [centred[g * room : (g + 1) * room], jnp.where(owner == g, side, 0.0)]
+            + [jnp.zeros((stride - room - META, feat), f32)] * (stride > room + META),
+            axis=0,
+        ).astype(bf16)
 
 
 def place_kernel(at_ref, pick_ref):
@@ -175,13 +185,25 @@
     return total
 
 
-def update_kernel(backs, shards, *refs):
+def update_kernel(backs, shards, groups, room, *refs):
     back_refs, pick_ref, refs = refs[:backs], refs[backs], refs[backs + 1 :]
     (kernels_ref, gain_ref), shard_refs, refs = refs[:2], refs[2 : 2 + shards], refs[2 + shards :]
     normed_ref, total_ref = refs
     f32 = jnp.float32
-    back = jnp.concatenate([ref[...].astype(f32) for ref in back_refs[::-1]], axis=0)
-    ratio = jnp.dot(pick_ref[...], back.astype(pick_ref.dtype), preferred_element_type=f32)
+    stride = back_refs[0].shape[0] * backs // groups
+    blocks = [
+        (ref[...] if backs > 1 else ref[i * stride : (i + 1) * stride, :]).astype(f32)
+        for ref in back_refs[::-1]
+        for i in range(groups // backs)
+    ]
+    pick = pick_ref[...]
+    rows = jnp.concatenate([block[:room] for block in blocks], axis=0)
+    side = sum(block[room : room + META, : groups * room] for block in blocks)
+    means = lax.dot_general(
+        pick, side.astype(pick.dtype), (((1,), (1,)), ((), ())), preferred_element_type=f32
+    )
+    ratio = jnp.dot(pick, rows.astype(pick.dtype), preferred_element_type=f32)
+    ratio = ratio + (means[:, 0:1] + means[:, 1:2])
     merged = kernels_ref[...].astype(f32) + ratio
     centred = merged - jnp.mean(merged, axis=1, keepdims=True)
     spread = jnp.mean(centred * centred, axis=1, keepdims=True)
@@ -248,13 +270,13 @@
     )(*[pltpu.with_memory_space_constraint(x, pltpu.HBM) for x in (home.T, boxes.T, kernels, w_out, w_in)])
     if near:
         blocks = all_exchanged(blocks) + [blocks[0]]
-        outs = [jax.ShapeDtypeStruct((room, feat), kernels.dtype)] * strips
+        outs = [jax.ShapeDtypeStruct((stride, feat), kernels.dtype)] * strips
     else:
         got = lax.all_to_all(
             blocks[0].reshape(strips, stride, feat), "tile", split_axis=0, concat_axis=0, tiled=True
         )
         blocks = [got.reshape(strips * stride, feat)]
-        outs = [jax.ShapeDtypeStruct((slots, feat), kernels.dtype)]
+        outs = [jax.ShapeDtypeStruct((strips * stride, feat), kernels.dtype)]
 
     shards = [shard]
     distance = holders // 2
@@ -277,9 +299,9 @@
         backs = all_exchanged(back) + [back[0]]
     else:
         got = lax.all_to_all(
-            back[0].reshape(strips, room, feat), "tile", split_axis=0, concat_axis=0, tiled=True
-        )
-        backs = [got.reshape(slots, feat)]
+            back[0].reshape(strips, stride, feat), "tile", split_axis=0, concat_axis=0, tiled=True
+        )
+        backs = [got.reshape(strips * stride, feat)]
     pick = pl.pallas_call(
         place_kernel,
         out_shape=pltpu.VMEM((count, slots), kernels.dtype),
@@ -292,7 +314,7 @@
     shards.insert(1, late.pop(0))
 
     normed, total = pl.pallas_call(
-        functools.partial(update_kernel, len(backs), len(shards)),
+        functools.partial(update_kernel, len(backs), len(shards), strips, room),
         out_shape=[
             jax.ShapeDtypeStruct((count, feat), kernels.dtype),
             jax.ShapeDtypeStruct((count, feat), jnp.float32),

time: 23.6 us -> 23.7 us (level)
    ppermute x3, waiting for transfers between devices: 1.86 us -> 1.41 us  [exchanged(): lax.ppermute(x, axis, [(i, i ^ distance) for i in range(lax.axis_size(axi...]
    ppermute x6, waiting for transfers between devices: 2.69 us -> 2.97 us  [all_exchanged(): lax.ppermute(xs[d], ('tile', 'inst'), [(t * holders + i, (t ^ d) * holder...]
  transfers between devices with their start and end apart: 9 -> 9, of which waited for: 5 -> 4; matrix products, arithmetic and copies ran while one was open for 0% -> 0% of each run, Pallas kernels for 23% -> 24%
where the time goes in v6:
time: 23.7 us; the launch traced here: 23.5 us
  starting transfers between devices  11.2 us (47%)
  Pallas kernels  7.91 us (33%)
  waiting for transfers between devices  4.38 us (18%)
    ppermute x6, starting transfers between devices, all_exchanged(): lax.ppermute(xs[d], ('tile', 'inst'), [(t * holders + i, (t ^ d) * holder...  9.66 us
    pallas_call x1, Pallas kernels, local(): pl.pallas_call(functools.partial(pool_kernel, len(blocks), strips, room),...  4.69 us
    ppermute x6, waiting for transfers between devices, all_exchanged(): lax.ppermute(xs[d], ('tile', 'inst'), [(t * holders + i, (t ^ d) * holder...  2.97 us
    ppermute x3, starting transfers between devices, exchanged(): lax.ppermute(x, axis, [(i, i ^ distance) for i in range(lax.axis_size(axi...  1.5 us
    ppermute x3, waiting for transfers between devices, exchanged(): lax.ppermute(x, axis, [(i, i ^ distance) for i in range(lax.axis_size(axi...  1.41 us
    pallas_call x1, Pallas kernels, local(): pl.pallas_call(functools.partial(pack_kernel, near, strips, room), out_sh...  1.33 us
    pallas_call x1, Pallas kernels, local(): pl.pallas_call(finish_kernel, out_shape=jax.ShapeDtypeStruct((count, feat...  0.94 us
    pallas_call x1, Pallas kernels, local(): pl.pallas_call(functools.partial(update_kernel, len(backs), len(shards),...  0.87 us
  transfers between devices with their start and end apart: 9, of which 4 were waited for; matrix products, arithmetic and copies ran while one was open for 0% of the time, Pallas kernels for 24%

profile of v6, /device:TPU:0, one launch (start us, length us, event | category | flops | bytes accessed | tf_op | source)
XLA Modules:
  0.0 23.5 jit_solution(4879263667207682487)
XLA Ops:
  0.0 0.0 copy-start
  0.0 1.3 %pack.1 = (bf16[48,256]{1,0:T(8,128)(2,1)S(1)}, bf16[48,256]{1,0:T(8,128)(2,1)S(1)}, bf16[48,256]{1,0:T(8,128)(2,1)S(1)}, bf16[48,256]{1,0:T(8,128)(2,1)S(1)}, s...) custom-call(s32[1,64]{1,0:T(1,128)} %bitcast.5, s32[4,64]{1,0:T(4,128)} %bitcast.4, bf16[64,256]{1,0:T(8,128)(2,1)} %refs_5_.1, ...), custom_call_target="tpu_custom_call" | custom-call | flops 26843545600 | bytes 8388608 | tf_op jit(solution)/shard_map/pack/pallas_call | solution.py:250
  1.3 4.6 %collective-permute-start = (bf16[48,256]{1,0:T(8,128)(2,1)S(1)}, bf16[48,256]{1,0:T(8,128)(2,1)S(1)}, u32[]{:S(2)}, u32[]{:S(2)}) collective-permute-start(bf16[48,256]{1,0:T(8,128)(2,1)S(1)} %get-tuple-element.17), channel_id=1, source_target_pairs={{0,13},{1,12},{2,15},{3,14},{4,9},{5,8},{6,11},{7,10},{8,5},{9,4},... | collective-permute-start | bytes 73736 | tf_op jit(solution)/shard_map/ppermute | solution.py:229
  5.9 0.0 collective-permute-start.1
  5.9 0.9 %collective-permute-start.2 = (bf16[48,256]{1,0:T(8,128)(2,1)S(1)}, bf16[48,256]{1,0:T(8,128)(2,1)S(1)}, u32[]{:S(2)}, u32[]{:S(2)}) collective-permute-start(bf16[48,256]{1,0:T(8,128)(2,1)S(1)} %get-tuple-element.19), channel_id=1, source_target_pairs={{0,5},{1,4},{2,7},{3,6},{4,1},{5,0},{6,3},{7,2},{8,13},{9,12},{10,... | collective-permute-start | bytes 73736 | tf_op jit(solution)/shard_map/ppermute | solution.py:229
  6.8 1.5 %collective-permute-start.7 = (bf16[1024,256]{1,0:T(8,128)(2,1)S(1)}, bf16[1024,256]{1,0:T(8,128)(2,1)S(1)}, u32[]{:S(2)}, u32[]{:S(2)}) collective-permute-start(bf16[1024,256]{1,0:T(8,128)(2,1)S(1)} %get-tuple-element.26.refs_7_), channel_id=1, source_target_pairs={{0,2},{1,3},{2,0},{3,1},{4,6},{5,7},{6,4},{7,5},{8,10},{9,11},{10,... | collective-permute-start | bytes 1572872 | tf_op jit(solution)/shard_map/ppermute | solution.py:221
  8.3 0.0 collective-permute-start.6
  8.3 0.0 collective-permute-done.refs_0_
  8.3 1.9 %collective-permute-done.1.refs_1_ = bf16[48,256]{1,0:T(8,128)(2,1)S(1)} collective-permute-done((bf16[48,256]{1,0:T(8,128)(2,1)S(1)}, bf16[48,256]{1,0:T(8,128)(2,1)S(1)}, u32[]{:S(2)}, u32[]{:S(2)}) %collective-permute-start.1) | collective-permute-done | bytes 24608 | tf_op jit(solution)/shard_map/ppermute | solution.py:229
  10.3 0.0 collective-permute-done.2.refs_2_
  10.3 0.0 copy-done
  10.3 0.0 copy-start.1
  10.3 0.0 copy-start.2
  10.3 4.7 %pool.1 = (bf16[48,256]{1,0:T(8,128)(2,1)S(1)}, bf16[48,256]{1,0:T(8,128)(2,1)S(1)}, bf16[48,256]{1,0:T(8,128)(2,1)S(1)}, bf16[48,256]{1,0:T(8,128)(2,1)S(1)}) custom-call(bf16[48,256]{1,0:T(8,128)(2,1)S(1)} %collective-permute-done.refs_0_, bf16[48,256]{1,0:T(8,128)(2,1)S(1)} %collective-permute-done.1.refs_1_, ...), custom_call_target="tpu_custom_call" | custom-call | flops 26843545600 | bytes 8388608 | tf_op jit(solution)/shard_map/pool/pallas_call | solution.py:287
  15.0 1.5 %collective-permute-start.3 = (bf16[48,256]{1,0:T(8,128)(2,1)S(1)}, bf16[48,256]{1,0:T(8,128)(2,1)S(1)}, u32[]{:S(2)}, u32[]{:S(2)}) collective-permute-start(bf16[48,256]{1,0:T(8,128)(2,1)S(1)} %get-tuple-element.21), channel_id=1, source_target_pairs={{0,13},{1,12},{2,15},{3,14},{4,9},{5,8},{6,11},{7,10},{8,5},{9,4},... | collective-permute-start | bytes 73736 | tf_op jit(solution)/shard_map/ppermute | solution.py:229
  16.5 0.6 %collective-permute-start.4 = (bf16[48,256]{1,0:T(8,128)(2,1)S(1)}, bf16[48,256]{1,0:T(8,128)(2,1)S(1)}, u32[]{:S(2)}, u32[]{:S(2)}) collective-permute-start(bf16[48,256]{1,0:T(8,128)(2,1)S(1)} %get-tuple-element.22), channel_id=1, source_target_pairs={{0,9},{1,8},{2,11},{3,10},{4,13},{5,12},{6,15},{7,14},{8,1},{9,0},... | collective-permute-start | bytes 73736 | tf_op jit(solution)/shard_map/ppermute | solution.py:229
  17.1 2.1 %collective-permute-start.5 = (bf16[48,256]{1,0:T(8,128)(2,1)S(1)}, bf16[48,256]{1,0:T(8,128)(2,1)S(1)}, u32[]{:S(2)}, u32[]{:S(2)}) collective-permute-start(bf16[48,256]{1,0:T(8,128)(2,1)S(1)} %get-tuple-element.23), channel_id=1, source_target_pairs={{0,5},{1,4},{2,7},{3,6},{4,1},{5,0},{6,3},{7,2},{8,13},{9,12},{10,... | collective-permute-start | bytes 73736 | tf_op jit(solution)/shard_map/ppermute | solution.py:229
  19.2 0.1 place.1.refs_4_
  19.3 1.4 %collective-permute-done.7.refs_9_ = bf16[1024,256]{1,0:T(8,128)(2,1)S(1)} collective-permute-done((bf16[1024,256]{1,0:T(8,128)(2,1)S(1)}, bf16[1024,256]{1,0:T(8,128)(2,1)S(1)}, u32[]{:S(2)}, u32[]{:S(2)}) %collective-permute-start.7) | collective-permute-done | bytes 524320 | tf_op jit(solution)/shard_map/ppermute | solution.py:221
  20.7 0.0 collective-permute-start.8
  20.7 0.0 collective-permute-done.3.refs_0_
  20.7 0.3 %collective-permute-done.4.refs_1_ = bf16[48,256]{1,0:T(8,128)(2,1)S(1)} collective-permute-done((bf16[48,256]{1,0:T(8,128)(2,1)S(1)}, bf16[48,256]{1,0:T(8,128)(2,1)S(1)}, u32[]{:S(2)}, u32[]{:S(2)}) %collective-permute-start.4) | collective-permute-done | bytes 24608 | tf_op jit(solution)/shard_map/ppermute | solution.py:229
  21.0 0.7 %collective-permute-done.5.refs_2_ = bf16[48,256]{1,0:T(8,128)(2,1)S(1)} collective-permute-done((bf16[48,256]{1,0:T(8,128)(2,1)S(1)}, bf16[48,256]{1,0:T(8,128)(2,1)S(1)}, u32[]{:S(2)}, u32[]{:S(2)}) %collective-permute-start.5) | collective-permute-done | bytes 24608 | tf_op jit(solution)/shard_map/ppermute | solution.py:229
  21.7 0.0 collective-permute-done.6.refs_8_
  21.7 0.0 copy-done.1
  21.7 0.0 copy-done.2
  21.7 0.9 %update.1 = (bf16[64,256]{1,0:T(8,128)(2,1)S(1)}, f32[64,256]{1,0:T(8,128)S(1)}) custom-call(bf16[48,256]{1,0:T(8,128)(2,1)S(1)} %collective-permute-done.3.refs_0_, bf16[48,256]{1,0:T(8,128)(2,1)S(1)} %collective-permute-done.4.refs_1_, bf16[48,256]{1,0:T(8,128)(2,1)S(1)} %collective-permute-done.5.refs_2_, bf16[48,256]{1,0:T(8,128)(2,1)S(1)} %get-tuple-element.24.refs_3_, ...), custom_call_target="tpu_custom_call" | custom-call | flops 26843545600 | bytes 8388608 | tf_op jit(solution)/shard_map/update/pallas_call | solution.py:316
  22.6 0.0 collective-permute-done.8.refs_0_
  22.6 0.9 %finish.1 = bf16[64,256]{1,0:T(8,128)(2,1)} custom-call(bf16[64,256]{1,0:T(8,128)(2,1)S(1)} %get-tuple-element.27.normed_ref, f32[64,256]{1,0:T(8,128)S(1)} %get-tuple-element.28.total_ref, bf16[1024,256]{1,0:T(8,128)(2,1)S(1)} %collective-permute-done.8.refs_0_), custom_call_target="tpu_custom_call" | custom-call | tf_op jit(solution)/shard_map/finish/pallas_call | solution.py:330
Async XLA Ops:
  0.0 10.3 %copy-start = (bf16[64,256,256]{2,1,0:T(8,128)(2,1)S(1)}, bf16[64,256,256]{2,1,0:T(8,128)(2,1)}, u32[]{:S(2)}) copy-start(bf16[64,256,256]{2,1,0:T(8,128)(2,1)} %refs_4_.3) | copy-start | bytes 25165828
  1.3 7.0 %collective-permute-start = (bf16[48,256]{1,0:T(8,128)(2,1)S(1)}, bf16[48,256]{1,0:T(8,128)(2,1)S(1)}, u32[]{:S(2)}, u32[]{:S(2)}) collective-permute-start(bf16[48,256]{1,0:T(8,128)(2,1)S(1)} %get-tuple-element.17), channel_id=1, source_target_pairs={{0,13},{1,12},{2,15},{3,14},{4,9},{5,8},{6,11},{7,10},{8,5},{9,4},... | collective-permute-start | bytes 73736 | tf_op jit(solution)/shard_map/ppermute | solution.py:229
  5.9 4.4 %collective-permute-start.1 = (bf16[48,256]{1,0:T(8,128)(2,1)S(1)}, bf16[48,256]{1,0:T(8,128)(2,1)S(1)}, u32[]{:S(2)}, u32[]{:S(2)}) collective-permute-start(bf16[48,256]{1,0:T(8,128)(2,1)S(1)} %get-tuple-element.18), channel_id=1, source_target_pairs={{0,9},{1,8},{2,11},{3,10},{4,13},{5,12},{6,15},{7,14},{8,1},{9,0},... | collective-permute-start | bytes 73736 | tf_op jit(solution)/shard_map/ppermute | solution.py:229
  5.9 4.4 %collective-permute-start.2 = (bf16[48,256]{1,0:T(8,128)(2,1)S(1)}, bf16[48,256]{1,0:T(8,128)(2,1)S(1)}, u32[]{:S(2)}, u32[]{:S(2)}) collective-permute-start(bf16[48,256]{1,0:T(8,128)(2,1)S(1)} %get-tuple-element.19), channel_id=1, source_target_pairs={{0,5},{1,4},{2,7},{3,6},{4,1},{5,0},{6,3},{7,2},{8,13},{9,12},{10,... | collective-permute-start | bytes 73736 | tf_op jit(solution)/shard_map/ppermute | solution.py:229
  6.8 13.8 %collective-permute-start.7 = (bf16[1024,256]{1,0:T(8,128)(2,1)S(1)}, bf16[1024,256]{1,0:T(8,128)(2,1)S(1)}, u32[]{:S(2)}, u32[]{:S(2)}) collective-permute-start(bf16[1024,256]{1,0:T(8,128)(2,1)S(1)} %get-tuple-element.26.refs_7_), channel_id=1, source_target_pairs={{0,2},{1,3},{2,0},{3,1},{4,6},{5,7},{6,4},{7,5},{8,10},{9,11},{10,... | collective-permute-start | bytes 1572872 | tf_op jit(solution)/shard_map/ppermute | solution.py:221
  8.3 13.4 %collective-permute-start.6 = (bf16[1024,256]{1,0:T(8,128)(2,1)S(1)}, bf16[1024,256]{1,0:T(8,128)(2,1)S(1)}, u32[]{:S(2)}, u32[]{:S(2)}) collective-permute-start(bf16[1024,256]{1,0:T(8,128)(2,1)S(1)} %get-tuple-element.26.refs_7_), channel_id=1, source_target_pairs={{0,1},{1,0},{2,3},{3,2},{4,5},{5,4},{6,7},{7,6},{8,9},{9,8},{10,11... | collective-permute-start | bytes 1572872 | tf_op jit(solution)/shard_map/ppermute | solution.py:221
  10.3 11.4 %copy-start.1 = (bf16[64,256]{1,0:T(8,128)(2,1)S(1)}, bf16[64,256]{1,0:T(8,128)(2,1)}, u32[]{:S(2)}) copy-start(bf16[64,256]{1,0:T(8,128)(2,1)} %refs_5_.1) | copy-start | bytes 98308
  10.3 11.4 %copy-start.2 = (f32[256]{0:T(256)S(1)}, f32[256]{0:T(256)}, u32[]{:S(2)}) copy-start(f32[256]{0:T(256)} %param.11) | copy-start | bytes 3076
  15.0 5.7 %collective-permute-start.3 = (bf16[48,256]{1,0:T(8,128)(2,1)S(1)}, bf16[48,256]{1,0:T(8,128)(2,1)S(1)}, u32[]{:S(2)}, u32[]{:S(2)}) collective-permute-start(bf16[48,256]{1,0:T(8,128)(2,1)S(1)} %get-tuple-element.21), channel_id=1, source_target_pairs={{0,13},{1,12},{2,15},{3,14},{4,9},{5,8},{6,11},{7,10},{8,5},{9,4},... | collective-permute-start | bytes 73736 | tf_op jit(solution)/shard_map/ppermute | solution.py:229
  16.5 4.5 %collective-permute-start.4 = (bf16[48,256]{1,0:T(8,128)(2,1)S(1)}, bf16[48,256]{1,0:T(8,128)(2,1)S(1)}, u32[]{:S(2)}, u32[]{:S(2)}) collective-permute-start(bf16[48,256]{1,0:T(8,128)(2,1)S(1)} %get-tuple-element.22), channel_id=1, source_target_pairs={{0,9},{1,8},{2,11},{3,10},{4,13},{5,12},{6,15},{7,14},{8,1},{9,0},... | collective-permute-start | bytes 73736 | tf_op jit(solution)/shard_map/ppermute | solution.py:229
  17.1 4.6 %collective-permute-start.5 = (bf16[48,256]{1,0:T(8,128)(2,1)S(1)}, bf16[48,256]{1,0:T(8,128)(2,1)S(1)}, u32[]{:S(2)}, u32[]{:S(2)}) collective-permute-start(bf16[48,256]{1,0:T(8,128)(2,1)S(1)} %get-tuple-element.23), channel_id=1, source_target_pairs={{0,5},{1,4},{2,7},{3,6},{4,1},{5,0},{6,3},{7,2},{8,13},{9,12},{10,... | collective-permute-start | bytes 73736 | tf_op jit(solution)/shard_map/ppermute | solution.py:229
  20.7 1.9 %collective-permute-start.8 = (bf16[1024,256]{1,0:T(8,128)(2,1)S(1)}, bf16[1024,256]{1,0:T(8,128)(2,1)S(1)}, u32[]{:S(2)}, u32[]{:S(2)}) collective-permute-start(bf16[1024,256]{1,0:T(8,128)(2,1)S(1)} %collective-permute-done.7.refs_9_), channel_id=1, source_target_pairs={{0,1},{1,0},{2,3},{3,2},{4,5},{5,4},{6,7},{7,6},{8,9},{9,8},{10,11... | collective-permute-start | bytes 1572872 | tf_op jit(solution)/shard_map/ppermute | solution.py:221

commit v7 on v6

--- a/solution.py
+++ b/solution.py
@@ -11,7 +11,7 @@
 SR = 2
 WC = 8
 META = 8
-ROWS_PER_STEP = 4
+ROWS_PER_STEP = 2
 VMEM = pltpu.VMEM
 
 

time: 23.7 us -> 23.6 us (level)
    ppermute x3, waiting for transfers between devices: 1.41 us -> 1.67 us  [exchanged(): lax.ppermute(x, axis, [(i, i ^ distance) for i in range(lax.axis_size(axi...]
  transfers between devices with their start and end apart: 9 -> 9, of which waited for: 4 -> 5; matrix products, arithmetic and copies ran while one was open for 0% -> 0% of each run, Pallas kernels for 24% -> 23%
where the time goes in v7:
time: 23.6 us; the launch traced here: 23.5 us
  starting transfers between devices  11.2 us (47%)
  Pallas kernels  7.78 us (33%)
  waiting for transfers between devices  4.5 us (19%)
    ppermute x6, starting transfers between devices, all_exchanged(): lax.ppermute(xs[d], ('tile', 'inst'), [(t * holders + i, (t ^ d) * holder...  9.65 us
    pallas_call x1, Pallas kernels, local(): pl.pallas_call(functools.partial(pool_kernel, len(blocks), strips, room),...  4.56 us
    ppermute x6, waiting for transfers between devices, all_exchanged(): lax.ppermute(xs[d], ('tile', 'inst'), [(t * holders + i, (t ^ d) * holder...  2.84 us
    ppermute x3, waiting for transfers between devices, exchanged(): lax.ppermute(x, axis, [(i, i ^ distance) for i in range(lax.axis_size(axi...  1.67 us
    ppermute x3, starting transfers between devices, exchanged(): lax.ppermute(x, axis, [(i, i ^ distance) for i in range(lax.axis_size(axi...  1.5 us
    pallas_call x1, Pallas kernels, local(): pl.pallas_call(functools.partial(pack_kernel, near, strips, room), out_sh...  1.33 us
    pallas_call x1, Pallas kernels, local(): pl.pallas_call(finish_kernel, out_shape=jax.ShapeDtypeStruct((count, feat...  0.93 us
    pallas_call x1, Pallas kernels, local(): pl.pallas_call(functools.partial(update_kernel, len(backs), len(shards),...  0.87 us
  transfers between devices with their start and end apart: 9, of which 5 were waited for; matrix products, arithmetic and copies ran while one was open for 0% of the time, Pallas kernels for 23%

profile of v7, /device:TPU:0, one launch (start us, length us, event | category | flops | bytes accessed | tf_op | source)
XLA Modules:
  0.0 23.5 jit_solution(3454962306095363329)
XLA Ops:
  0.0 0.0 copy-start
  0.0 1.3 %pack.1 = (bf16[48,256]{1,0:T(8,128)(2,1)S(1)}, bf16[48,256]{1,0:T(8,128)(2,1)S(1)}, bf16[48,256]{1,0:T(8,128)(2,1)S(1)}, bf16[48,256]{1,0:T(8,128)(2,1)S(1)}, s...) custom-call(s32[1,64]{1,0:T(1,128)} %bitcast.5, s32[4,64]{1,0:T(4,128)} %bitcast.4, bf16[64,256]{1,0:T(8,128)(2,1)} %refs_5_.1, ...), custom_call_target="tpu_custom_call" | custom-call | flops 26843545600 | bytes 8388608 | tf_op jit(solution)/shard_map/pack/pallas_call | solution.py:250
  1.3 4.6 %collective-permute-start = (bf16[48,256]{1,0:T(8,128)(2,1)S(1)}, bf16[48,256]{1,0:T(8,128)(2,1)S(1)}, u32[]{:S(2)}, u32[]{:S(2)}) collective-permute-start(bf16[48,256]{1,0:T(8,128)(2,1)S(1)} %get-tuple-element.17), channel_id=1, source_target_pairs={{0,13},{1,12},{2,15},{3,14},{4,9},{5,8},{6,11},{7,10},{8,5},{9,4},... | collective-permute-start | bytes 73736 | tf_op jit(solution)/shard_map/ppermute | solution.py:229
  5.9 0.0 collective-permute-start.1
  5.9 0.9 %collective-permute-start.2 = (bf16[48,256]{1,0:T(8,128)(2,1)S(1)}, bf16[48,256]{1,0:T(8,128)(2,1)S(1)}, u32[]{:S(2)}, u32[]{:S(2)}) collective-permute-start(bf16[48,256]{1,0:T(8,128)(2,1)S(1)} %get-tuple-element.19), channel_id=1, source_target_pairs={{0,5},{1,4},{2,7},{3,6},{4,1},{5,0},{6,3},{7,2},{8,13},{9,12},{10,... | collective-permute-start | bytes 73736 | tf_op jit(solution)/shard_map/ppermute | solution.py:229
  6.8 1.5 %collective-permute-start.7 = (bf16[1024,256]{1,0:T(8,128)(2,1)S(1)}, bf16[1024,256]{1,0:T(8,128)(2,1)S(1)}, u32[]{:S(2)}, u32[]{:S(2)}) collective-permute-start(bf16[1024,256]{1,0:T(8,128)(2,1)S(1)} %get-tuple-element.26.refs_7_), channel_id=1, source_target_pairs={{0,2},{1,3},{2,0},{3,1},{4,6},{5,7},{6,4},{7,5},{8,10},{9,11},{10,... | collective-permute-start | bytes 1572872 | tf_op jit(solution)/shard_map/ppermute | solution.py:221
  8.3 0.0 collective-permute-start.6
  8.3 0.0 collective-permute-done.refs_0_
  8.3 1.9 %collective-permute-done.1.refs_1_ = bf16[48,256]{1,0:T(8,128)(2,1)S(1)} collective-permute-done((bf16[48,256]{1,0:T(8,128)(2,1)S(1)}, bf16[48,256]{1,0:T(8,128)(2,1)S(1)}, u32[]{:S(2)}, u32[]{:S(2)}) %collective-permute-start.1) | collective-permute-done | bytes 24608 | tf_op jit(solution)/shard_map/ppermute | solution.py:229
  10.3 0.0 collective-permute-done.2.refs_2_
  10.3 0.0 copy-done
  10.3 0.0 copy-start.1
  10.3 0.0 copy-start.2
  10.3 4.6 %pool.1 = (bf16[48,256]{1,0:T(8,128)(2,1)S(1)}, bf16[48,256]{1,0:T(8,128)(2,1)S(1)}, bf16[48,256]{1,0:T(8,128)(2,1)S(1)}, bf16[48,256]{1,0:T(8,128)(2,1)S(1)}) custom-call(bf16[48,256]{1,0:T(8,128)(2,1)S(1)} %collective-permute-done.refs_0_, bf16[48,256]{1,0:T(8,128)(2,1)S(1)} %collective-permute-done.1.refs_1_, ...), custom_call_target="tpu_custom_call" | custom-call | flops 26843545600 | bytes 8388608 | tf_op jit(solution)/shard_map/pool/pallas_call | solution.py:287
  14.9 1.5 %collective-permute-start.3 = (bf16[48,256]{1,0:T(8,128)(2,1)S(1)}, bf16[48,256]{1,0:T(8,128)(2,1)S(1)}, u32[]{:S(2)}, u32[]{:S(2)}) collective-permute-start(bf16[48,256]{1,0:T(8,128)(2,1)S(1)} %get-tuple-element.21), channel_id=1, source_target_pairs={{0,13},{1,12},{2,15},{3,14},{4,9},{5,8},{6,11},{7,10},{8,5},{9,4},... | collective-permute-start | bytes 73736 | tf_op jit(solution)/shard_map/ppermute | solution.py:229
  16.4 0.6 %collective-permute-start.4 = (bf16[48,256]{1,0:T(8,128)(2,1)S(1)}, bf16[48,256]{1,0:T(8,128)(2,1)S(1)}, u32[]{:S(2)}, u32[]{:S(2)}) collective-permute-start(bf16[48,256]{1,0:T(8,128)(2,1)S(1)} %get-tuple-element.22), channel_id=1, source_target_pairs={{0,9},{1,8},{2,11},{3,10},{4,13},{5,12},{6,15},{7,14},{8,1},{9,0},... | collective-permute-start | bytes 73736 | tf_op jit(solution)/shard_map/ppermute | solution.py:229
  17.0 2.1 %collective-permute-start.5 = (bf16[48,256]{1,0:T(8,128)(2,1)S(1)}, bf16[48,256]{1,0:T(8,128)(2,1)S(1)}, u32[]{:S(2)}, u32[]{:S(2)}) collective-permute-start(bf16[48,256]{1,0:T(8,128)(2,1)S(1)} %get-tuple-element.23), channel_id=1, source_target_pairs={{0,5},{1,4},{2,7},{3,6},{4,1},{5,0},{6,3},{7,2},{8,13},{9,12},{10,... | collective-permute-start | bytes 73736 | tf_op jit(solution)/shard_map/ppermute | solution.py:229
  19.0 0.1 place.1.refs_4_
  19.1 1.5 %collective-permute-done.7.refs_9_ = bf16[1024,256]{1,0:T(8,128)(2,1)S(1)} collective-permute-done((bf16[1024,256]{1,0:T(8,128)(2,1)S(1)}, bf16[1024,256]{1,0:T(8,128)(2,1)S(1)}, u32[]{:S(2)}, u32[]{:S(2)}) %collective-permute-start.7) | collective-permute-done | bytes 524320 | tf_op jit(solution)/shard_map/ppermute | solution.py:221
  20.7 0.0 collective-permute-start.8
  20.7 0.0 collective-permute-done.3.refs_0_
  20.7 0.2 collective-permute-done.4.refs_1_
  20.8 0.7 %collective-permute-done.5.refs_2_ = bf16[48,256]{1,0:T(8,128)(2,1)S(1)} collective-permute-done((bf16[48,256]{1,0:T(8,128)(2,1)S(1)}, bf16[48,256]{1,0:T(8,128)(2,1)S(1)}, u32[]{:S(2)}, u32[]{:S(2)}) %collective-permute-start.5) | collective-permute-done | bytes 24608 | tf_op jit(solution)/shard_map/ppermute | solution.py:229
  21.6 0.0 collective-permute-done.6.refs_8_
  21.6 0.0 copy-done.1
  21.6 0.0 copy-done.2
  21.6 0.9 %update.1 = (bf16[64,256]{1,0:T(8,128)(2,1)S(1)}, f32[64,256]{1,0:T(8,128)S(1)}) custom-call(bf16[48,256]{1,0:T(8,128)(2,1)S(1)} %collective-permute-done.3.refs_0_, bf16[48,256]{1,0:T(8,128)(2,1)S(1)} %collective-permute-done.4.refs_1_, bf16[48,256]{1,0:T(8,128)(2,1)S(1)} %collective-permute-done.5.refs_2_, bf16[48,256]{1,0:T(8,128)(2,1)S(1)} %get-tuple-element.24.refs_3_, ...), custom_call_target="tpu_custom_call" | custom-call | flops 26843545600 | bytes 8388608 | tf_op jit(solution)/shard_map/update/pallas_call | solution.py:316
  22.4 0.1 collective-permute-done.8.refs_0_
  22.6 0.9 %finish.1 = bf16[64,256]{1,0:T(8,128)(2,1)} custom-call(bf16[64,256]{1,0:T(8,128)(2,1)S(1)} %get-tuple-element.27.normed_ref, f32[64,256]{1,0:T(8,128)S(1)} %get-tuple-element.28.total_ref, bf16[1024,256]{1,0:T(8,128)(2,1)S(1)} %collective-permute-done.8.refs_0_), custom_call_target="tpu_custom_call" | custom-call | tf_op jit(solution)/shard_map/finish/pallas_call | solution.py:330
Async XLA Ops:
  0.0 10.3 %copy-start = (bf16[64,256,256]{2,1,0:T(8,128)(2,1)S(1)}, bf16[64,256,256]{2,1,0:T(8,128)(2,1)}, u32[]{:S(2)}) copy-start(bf16[64,256,256]{2,1,0:T(8,128)(2,1)} %refs_4_.3) | copy-start | bytes 25165828
  1.3 7.0 %collective-permute-start = (bf16[48,256]{1,0:T(8,128)(2,1)S(1)}, bf16[48,256]{1,0:T(8,128)(2,1)S(1)}, u32[]{:S(2)}, u32[]{:S(2)}) collective-permute-start(bf16[48,256]{1,0:T(8,128)(2,1)S(1)} %get-tuple-element.17), channel_id=1, source_target_pairs={{0,13},{1,12},{2,15},{3,14},{4,9},{5,8},{6,11},{7,10},{8,5},{9,4},... | collective-permute-start | bytes 73736 | tf_op jit(solution)/shard_map/ppermute | solution.py:229
  5.9 4.4 %collective-permute-start.1 = (bf16[48,256]{1,0:T(8,128)(2,1)S(1)}, bf16[48,256]{1,0:T(8,128)(2,1)S(1)}, u32[]{:S(2)}, u32[]{:S(2)}) collective-permute-start(bf16[48,256]{1,0:T(8,128)(2,1)S(1)} %get-tuple-element.18), channel_id=1, source_target_pairs={{0,9},{1,8},{2,11},{3,10},{4,13},{5,12},{6,15},{7,14},{8,1},{9,0},... | collective-permute-start | bytes 73736 | tf_op jit(solution)/shard_map/ppermute | solution.py:229
  5.9 4.4 %collective-permute-start.2 = (bf16[48,256]{1,0:T(8,128)(2,1)S(1)}, bf16[48,256]{1,0:T(8,128)(2,1)S(1)}, u32[]{:S(2)}, u32[]{:S(2)}) collective-permute-start(bf16[48,256]{1,0:T(8,128)(2,1)S(1)} %get-tuple-element.19), channel_id=1, source_target_pairs={{0,5},{1,4},{2,7},{3,6},{4,1},{5,0},{6,3},{7,2},{8,13},{9,12},{10,... | collective-permute-start | bytes 73736 | tf_op jit(solution)/shard_map/ppermute | solution.py:229
  6.8 13.8 %collective-permute-start.7 = (bf16[1024,256]{1,0:T(8,128)(2,1)S(1)}, bf16[1024,256]{1,0:T(8,128)(2,1)S(1)}, u32[]{:S(2)}, u32[]{:S(2)}) collective-permute-start(bf16[1024,256]{1,0:T(8,128)(2,1)S(1)} %get-tuple-element.26.refs_7_), channel_id=1, source_target_pairs={{0,2},{1,3},{2,0},{3,1},{4,6},{5,7},{6,4},{7,5},{8,10},{9,11},{10,... | collective-permute-start | bytes 1572872 | tf_op jit(solution)/shard_map/ppermute | solution.py:221
  8.3 13.2 %collective-permute-start.6 = (bf16[1024,256]{1,0:T(8,128)(2,1)S(1)}, bf16[1024,256]{1,0:T(8,128)(2,1)S(1)}, u32[]{:S(2)}, u32[]{:S(2)}) collective-permute-start(bf16[1024,256]{1,0:T(8,128)(2,1)S(1)} %get-tuple-element.26.refs_7_), channel_id=1, source_target_pairs={{0,1},{1,0},{2,3},{3,2},{4,5},{5,4},{6,7},{7,6},{8,9},{9,8},{10,11... | collective-permute-start | bytes 1572872 | tf_op jit(solution)/shard_map/ppermute | solution.py:221
  10.3 11.3 %copy-start.1 = (bf16[64,256]{1,0:T(8,128)(2,1)S(1)}, bf16[64,256]{1,0:T(8,128)(2,1)}, u32[]{:S(2)}) copy-start(bf16[64,256]{1,0:T(8,128)(2,1)} %refs_5_.1) | copy-start | bytes 98308
  10.3 11.3 %copy-start.2 = (f32[256]{0:T(256)S(1)}, f32[256]{0:T(256)}, u32[]{:S(2)}) copy-start(f32[256]{0:T(256)} %param.11) | copy-start | bytes 3076
  14.9 5.8 %collective-permute-start.3 = (bf16[48,256]{1,0:T(8,128)(2,1)S(1)}, bf16[48,256]{1,0:T(8,128)(2,1)S(1)}, u32[]{:S(2)}, u32[]{:S(2)}) collective-permute-start(bf16[48,256]{1,0:T(8,128)(2,1)S(1)} %get-tuple-element.21), channel_id=1, source_target_pairs={{0,13},{1,12},{2,15},{3,14},{4,9},{5,8},{6,11},{7,10},{8,5},{9,4},... | collective-permute-start | bytes 73736 | tf_op jit(solution)/shard_map/ppermute | solution.py:229
  16.4 4.5 %collective-permute-start.4 = (bf16[48,256]{1,0:T(8,128)(2,1)S(1)}, bf16[48,256]{1,0:T(8,128)(2,1)S(1)}, u32[]{:S(2)}, u32[]{:S(2)}) collective-permute-start(bf16[48,256]{1,0:T(8,128)(2,1)S(1)} %get-tuple-element.22), channel_id=1, source_target_pairs={{0,9},{1,8},{2,11},{3,10},{4,13},{5,12},{6,15},{7,14},{8,1},{9,0},... | collective-permute-start | bytes 73736 | tf_op jit(solution)/shard_map/ppermute | solution.py:229
  17.0 4.6 %collective-permute-start.5 = (bf16[48,256]{1,0:T(8,128)(2,1)S(1)}, bf16[48,256]{1,0:T(8,128)(2,1)S(1)}, u32[]{:S(2)}, u32[]{:S(2)}) collective-permute-start(bf16[48,256]{1,0:T(8,128)(2,1)S(1)} %get-tuple-element.23), channel_id=1, source_target_pairs={{0,5},{1,4},{2,7},{3,6},{4,1},{5,0},{6,3},{7,2},{8,13},{9,12},{10,... | collective-permute-start | bytes 73736 | tf_op jit(solution)/shard_map/ppermute | solution.py:229
  20.7 1.9 %collective-permute-start.8 = (bf16[1024,256]{1,0:T(8,128)(2,1)S(1)}, bf16[1024,256]{1,0:T(8,128)(2,1)S(1)}, u32[]{:S(2)}, u32[]{:S(2)}) collective-permute-start(bf16[1024,256]{1,0:T(8,128)(2,1)S(1)} %collective-permute-done.7.refs_9_), channel_id=1, source_target_pairs={{0,1},{1,0},{2,3},{3,2},{4,5},{5,4},{6,7},{7,6},{8,9},{9,8},{10,11... | collective-permute-start | bytes 1572872 | tf_op jit(solution)/shard_map/ppermute | solution.py:221
